TPU v7x, 32 devices: a whole 2x2x4 slice. The times are simulated.
32 devices in a mesh: batch: 2 (over x), mp: 16 (over z, y, core).
Axes of the slice: x: 2, y: 2, z: 4, core: 2. Of those that a mesh axis runs over, the one named last changes fastest.
Arguments:
- conv_input: bfloat16 [128, 2, 13, 13, 384], P(('batch', 'mp')), may hold values from -6 to 6
- group: int32 [128], P(('batch', 'mp')), may hold values from 0 to 1
- conv_weight: bfloat16 [2, 3456, 256], P(None, 'mp'), may hold values from -0.109375 to 0.109375
- conv_bias: float32 [2, 256], replicated, may hold values from -3 to 3
- stitch_pool: float32 [2, 2, 256], replicated, may hold values from 0.2 to 1
- fc_weight: bfloat16 [2, 9216, 4096], P(None, None, 'mp'), may hold values from -0.0625 to 0.0625
- fc_bias: float32 [2, 4096], P(None, 'mp'), may hold values from -3 to 3
- stitch_fc: float32 [2, 2, 4096], P(None, None, 'mp'), may hold values from 0.2 to 1
- cotangent: bfloat16 [128, 2, 4096], P(('batch', 'mp')), may hold values from -6 to 6
Outputs:
- output: bfloat16 [128, 2, 4096], P(('batch', 'mp'))
- input_grad: bfloat16 [128, 2, 13, 13, 384], P(('batch', 'mp'))
- conv_weight_grad: float32 [2, 3456, 256], P(None, 'mp')
- conv_bias_grad: float32 [2, 256], replicated
- stitch_pool_grad: float32 [2, 2, 256], replicated
- fc_weight_grad: float32 [2, 9216, 4096], P(None, 'batch', 'mp')
- fc_bias_grad: float32 [2, 4096], P(None, 'mp')
- stitch_fc_grad: float32 [2, 2, 4096], P(None, None, 'mp')
Inputs may be any that keep to these rules, and one draw needn't show every extreme that they name: `group`: 0 marks a 227-pixel image whose maps fill all 13 x 13 cells; 1 marks a 195-pixel image whose maps fill the first 11 rows and columns.
All inputs are finite; a program needn't handle non-finite values.
Results may differ from a plain program's by a relative error of at most 0.006.
Values may be sent and summed in bfloat16 or wider, within the bound.
No kernel may reach another device: no remote copies, remote signals or barrier semaphores. Data moves between devices by JAX's collectives and lax.ppermute only.
A program may use at most 128 MiB of HBM per device.

v0:
```python
import functools

import jax
import jax.numpy as jnp
import numpy as np
from jax import lax
from jax.experimental import pallas as pl
from jax.experimental.pallas import tpu as pltpu
from jax.sharding import PartitionSpec as P

BOTH = ("batch", "mp")
WIDTH = 16
EXTRA = 16
ROOT_HALF = 0.7071067811865476
ROOT_TWO_PI_INV = 0.3989422804014327
VMEM = pl.BlockSpec(memory_space=pltpu.VMEM)
SMEM = pl.BlockSpec(memory_space=pltpu.SMEM)
MIB = 1024 * 1024
bf16, f32 = jnp.bfloat16, jnp.float32
shape_of = jax.ShapeDtypeStruct


def call(body, out_shape, operands, scratch=(), scalars=0, mib=24):
    return pl.pallas_call(
        body,
        out_shape=out_shape,
        in_specs=[SMEM] * scalars + [VMEM] * (len(operands) - scalars),
        out_specs=jax.tree.map(lambda _: VMEM, out_shape),
        scratch_shapes=scratch,
        compiler_params=pltpu.CompilerParams(vmem_limit_bytes=mib * MIB),
    )(*operands)


class Place:
    def __init__(self, pairs, planes):
        batch_at, mp_at = lax.axis_index("batch"), lax.axis_index("mp")
        self.planes = planes
        self.task = lax.div(batch_at, pairs)
        self.core = lax.rem(mp_at, 2)
        self.y = lax.rem(lax.div(mp_at, 2), 2)
        self.z = lax.div(mp_at, 4)

    def chip(self, kz, ky):
        y = self.y if ky == 0 else 1 - self.y
        return lax.rem(self.z + (self.planes - kz), self.planes) * 2 + y


def phi_cdf(value):
    return 0.5 * (1.0 + lax.erf(value * ROOT_HALF))


def gelu_slope(value):
    return phi_cdf(value) + value * ROOT_TWO_PI_INV * jnp.exp(-0.5 * value * value)


def split_high_low(value):
    high = value.astype(bf16)
    return high, (value - high.astype(f32)).astype(bf16)


def window_sum(q_ref, value):
    high, low = split_high_low(value)
    return jnp.dot(q_ref[...], high, preferred_element_type=f32) + jnp.dot(
        q_ref[...], low, preferred_element_type=f32
    )


def split_inputs(place, g_ref, x_ref, cot_ref, own_ref, far_ref, out_ref):
    at = place()
    few, _, side, _, depth = x_ref.shape
    units = out_ref.shape[2]
    own_ref[...] = jnp.zeros_like(own_ref)
    far_ref[...] = jnp.zeros_like(far_ref)
    columns = lax.broadcasted_iota(jnp.int32, (side, depth), 0)
    for n in range(few):
        limit = side - 2 * g_ref[n]
        for y in range(side):
            reach = jnp.where(y < limit, limit, 0)
            mask = jnp.where(columns < reach, 1.0, 0.0).astype(bf16)
            own_ref[y, n, 0:side, :] = x_ref[n, at.task, y] * mask
            far_ref[y, n, 0:side, :] = x_ref[n, 1 - at.task, y] * mask
    for i in range(few):
        for t in range(2):
            pass
    value = cot_ref[...].astype(f32)
    rows = jnp.concatenate([value[i, t : t + 1] for t in range(2) for i in range(few)], axis=0)
    for m in range(out_ref.shape[0]):
        out_ref[m] = rows[:, m * units : (m + 1) * units].astype(bf16)


def widen(place, own_ref, far_ref, x3_ref, xt_ref):
    at = place()
    side, few, _, depth = own_ref.shape
    block = few * WIDTH
    slab = 2 * block
    for edge in (0, side + 1):
        x3_ref[edge * slab : (edge + 1) * slab, :] = jnp.zeros((slab, 3 * depth), bf16)
        xt_ref[:, edge * slab : (edge + 1) * slab] = jnp.zeros((3 * depth, slab), bf16)
    for y in range(side):
        own = own_ref[y].reshape(block, depth).astype(f32)
        far = far_ref[y].reshape(block, depth).astype(f32)
        first = at.task == 0
        wide = jnp.concatenate(
            [jnp.where(first, own, far), jnp.where(first, far, own)], axis=0
        )
        rows = slice((y + 1) * slab, (y + 2) * slab)
        turned = wide.T
        for kx in range(3):
            lanes = slice(kx * depth, (kx + 1) * depth)
            shift = (1 - kx) % slab
            x3_ref[rows, lanes] = (pltpu.roll(wide, shift, 0) if shift else wide).astype(bf16)
            xt_ref[lanes, rows] = (pltpu.roll(turned, shift, 1) if shift else turned).astype(bf16)


def group_column(at, own_ref, far_ref, images, channels):
    few = images // 2
    rows = lax.broadcasted_iota(jnp.int32, (images, channels), 0)
    value = jnp.zeros((images, channels), jnp.int32)
    for n in range(images):
        own, far = own_ref[n % few], far_ref[n % few]
        value = jnp.where(rows == n, jnp.where(at.task == n // few, own, far), value)
    return value


def conv_forward(place, side, pool, images, *refs):
    own_ref, far_ref, x_ref, b_ref, q_ref = refs[:5]
    blocks = refs[5:-3]
    pre_ref, pooled_ref, w_ref = refs[-3:]
    at = place()
    chips = len(blocks) // 2
    rows, half = blocks[0].shape
    here = pl.ds(pl.multiple_of(at.core * half, half), half)
    there = pl.ds(pl.multiple_of((1 - at.core) * half, half), half)
    for j in range(chips):
        to = pl.ds(pl.multiple_of(at.chip(j // 2, j % 2) * rows, 16), rows)
        w_ref[to, here] = blocks[j][...]
        w_ref[to, there] = blocks[chips + j][...]
    slab = images * WIDTH
    depth = x_ref.shape[1]
    channels = w_ref.shape[1]
    acts = {}
    bias = jnp.where(at.task == 0, b_ref[0:1, :], b_ref[1:2, :])
    group = group_column(at, own_ref, far_ref, images, channels)
    for start in range(0, side, 4):
        rows = min(4, side - start)
        total = None
        for ky in range(3):
            part = jnp.dot(
                x_ref[(start + ky) * slab : (start + ky + rows) * slab, :],
                w_ref[ky * depth : (ky + 1) * depth, :],
                preferred_element_type=f32,
            )
            total = part if total is None else total + part
        total = total + bias
        pre_ref[start * slab : (start + rows) * slab, :] = total
        act = total * phi_cdf(total)
        for row in range(rows):
            acts[start + row] = act[row * slab : (row + 1) * slab, :]
        for p in range(pool):
            if not (start <= 2 * p + 2 < start + rows):
                continue
            cells = window_sum(q_ref, acts[2 * p] + acts[2 * p + 1] + acts[2 * p + 2])
            side_at = jnp.where(at.core == (2 * p) // pool, 0, 1)
            for q in range(pool):
                kept = jnp.where(max(p, q) + group < pool, 1.0 / 9.0, 0.0)
                lanes = ((p % (pool // 2)) * pool + q) * channels
                pooled_ref[side_at, :, lanes : lanes + channels] = (
                    cells[q * images : (q + 1) * images, :] * kept
                ).astype(bf16)


def slope_and_back(pre_ref, w_ref, slope_ref, back_ref):
    slope_ref[...] = gelu_slope(pre_ref[...])
    taps = 9
    depth = w_ref.shape[0] // taps
    channels = w_ref.shape[1]
    for tap in range(taps):
        far = taps - 1 - tap
        back_ref[tap * channels : (tap + 1) * channels, :] = (
            w_ref[far * depth : (far + 1) * depth, :].astype(f32).T.astype(bf16)
        )


def cot_rows(place, own_ref, far_ref, up_ref):
    at = place()
    first = at.task == 0
    rows = own_ref.shape[1]
    few = rows // 2
    low_rows = lax.broadcasted_iota(jnp.int32, own_ref.shape[1:], 0) < few
    for j in range(own_ref.shape[0] // 2):
        chip = at.chip(j // 2, j % 2)
        for c in range(2):
            own = own_ref[2 * chip + c].astype(f32)
            far = far_ref[2 * chip + c].astype(f32)
            low = jnp.where(first, own, far)
            high = jnp.where(first, far, own)
            zero = jnp.where(low_rows, low, pltpu.roll(high, few, 0))
            one = jnp.where(low_rows, pltpu.roll(low, few, 0), high)
            here = slice((2 * j + c) * rows, (2 * j + c + 1) * rows)
            up_ref[0, here, :] = jnp.where(first, zero, one)
            up_ref[1, here, :] = jnp.where(first, one, zero)


def fc_far(*refs):
    blocks = refs[:-3]
    w_ref, all_ref, out_ref = refs[-3:]
    rows = blocks[0].shape[0]
    for j, block in enumerate(blocks):
        all_ref[j * rows : (j + 1) * rows, :] = block[...]
    out_ref[...] = jnp.dot(all_ref[...], w_ref[...], preferred_element_type=f32)


def fc_own(x_ref, w_ref, out_ref):
    out_ref[...] = jnp.dot(x_ref[...], w_ref[...], preferred_element_type=f32)


def fc_middle(place, own_ref, back_ref, bias_ref, mix_ref, up_ref, d_ref, hidden_ref, sums_ref):
    at = place()
    first = at.task == 0
    bias = jnp.where(first, bias_ref[0:1, :], bias_ref[1:2, :])
    pre = own_ref[...] + back_ref[...] + bias
    cdf = phi_cdf(pre)
    hidden = pre * cdf
    hidden_ref[...] = hidden
    slope = cdf + pre * ROOT_TWO_PI_INV * jnp.exp(-0.5 * pre * pre)

    def mix(t, u):
        row = mix_ref[t]
        return jnp.where(u == 0, row[0:1, :], row[1:2, :])

    mine, other = up_ref[0], up_ref[1]
    d_hidden = mix(at.task, at.task) * mine + mix(1 - at.task, at.task) * other
    d_fc = (slope * d_hidden).astype(bf16)
    d_ref[...] = d_fc
    by_mine = jnp.sum(mine * hidden, axis=0, keepdims=True)
    by_other = jnp.sum(other * hidden, axis=0, keepdims=True)
    sums_ref[...] = jnp.concatenate(
        [
            jnp.sum(d_fc.astype(f32), axis=0, keepdims=True),
            jnp.where(first, by_mine, by_other),
            jnp.where(first, by_other, by_mine),
            jnp.zeros((5, by_mine.shape[1]), f32),
        ],
        axis=0,
    )


def fc_back(d_ref, far_ref, w_ref, wf_ref, *outs):
    chips = len(outs)
    rows = outs[0].shape[0]
    contract = (((1,), (1,)), ((), ()))
    total = lax.dot_general(d_ref[...], w_ref[...], contract, preferred_element_type=f32)
    total += lax.dot_general(far_ref[...], wf_ref[...], contract, preferred_element_type=f32)
    for j, out in enumerate(outs):
        out[...] = total[j * rows : (j + 1) * rows, :].astype(out.dtype)


def add_rows(keep_ref, got_ref, *outs):
    total = keep_ref[...] + got_ref[...].astype(f32)
    for out in outs:
        out[...] = total.astype(out.dtype)


def block_total(place, keep_ref, *refs):
    at = place()
    total_ref, mine_ref, mine_low_ref, other_ref = refs[-4:]
    total = keep_ref[...]
    for ref in refs[:-4]:
        total = total + ref[...].astype(f32)
    total_ref[...] = total
    images = mine_ref.shape[0]
    low, high = total[:images], total[images:]
    mine = jnp.where(at.core == 0, low, high)
    mine_ref[...] = mine
    mine_low_ref[...] = mine.astype(bf16)
    other_ref[...] = jnp.where(at.core == 0, high, low).astype(bf16)


def stitch_terms(total_ref, own_ref, far_ref, out_ref):
    channels = out_ref.shape[1]
    own = far = None
    for cell in range(total_ref.shape[1] // channels):
        lanes = slice(cell * channels, (cell + 1) * channels)
        grad = total_ref[:, lanes]
        one = grad * own_ref[:, lanes].astype(f32)
        two = grad * far_ref[:, lanes].astype(f32)
        own = one if own is None else own + one
        far = two if far is None else far + two
    out_ref[...] = jnp.concatenate(
        [
            jnp.sum(own, axis=0, keepdims=True),
            jnp.sum(far, axis=0, keepdims=True),
            jnp.zeros((6, channels), f32),
        ],
        axis=0,
    )


def conv_slope(place, side, pool, images, *refs):
    (og_ref, fg_ref, mine_ref, c_ref, x_ref, xc_ref, st_ref, slope_ref, q_ref) = refs[:9]
    d_ref, bias_ref = refs[9:]
    at = place()
    slab = images * WIDTH
    channels = slope_ref.shape[1]
    group = group_column(at, og_ref, fg_ref, images, channels)

    def mix(t, u):
        row = st_ref[t]
        return jnp.where(u == 0, row[0:1, :], row[1:2, :])

    near, far = mix(at.task, at.task), mix(1 - at.task, at.task)
    spread = []
    for p in range(pool):
        mine_here = at.core == (2 * p) // pool
        cells = []
        for q in range(pool):
            lanes = ((p % (pool // 2)) * pool + q) * channels
            lanes = slice(lanes, lanes + channels)
            kept = jnp.where(max(p, q) + group < pool, 1.0 / 9.0, 0.0)
            one = near * mine_ref[:, lanes] + far * x_ref[:, lanes].astype(f32)
            two = near * c_ref[:, lanes].astype(f32) + far * xc_ref[:, lanes].astype(f32)
            cells.append(jnp.where(mine_here, one, two) * kept)
        spread.append(window_sum(q_ref, jnp.concatenate(cells, axis=0)))
    total = jnp.zeros((8, channels), f32)
    for y in range(side):
        act = None
        for p in range(pool):
            if 2 * p <= y <= 2 * p + 2:
                act = spread[p] if act is None else act + spread[p]
        grad = (act * slope_ref[y * slab : (y + 1) * slab, :]).astype(bf16)
        d_ref[y * slab : (y + 1) * slab, :] = grad
        total = total + jnp.sum(grad.astype(f32).reshape(-1, 8, channels), axis=0)
    bias_ref[...] = jnp.sum(total, axis=0, keepdims=True)


def kernel_grad(place, slab, xt_ref, d_ref, bias_ref, st_ref, *refs):
    keep1_ref, keep0_ref, send1_ref, send0_ref, scr_ref = refs
    at = place()
    depth = xt_ref.shape[0]
    planes, full, half = keep1_ref.shape
    rows = full - EXTRA
    count = d_ref.shape[0]
    for ky in range(3):
        scr_ref[ky * depth : (ky + 1) * depth, :] = jnp.dot(
            xt_ref[:, ky * slab : ky * slab + count], d_ref[...], preferred_element_type=f32
        )
    small = jnp.concatenate([bias_ref[...], st_ref[0:2, :]], axis=0)
    small = jnp.concatenate(
        [small[:, :half], jnp.zeros((1, half), f32), small[:, half:], jnp.zeros((1, half), f32)],
        axis=0,
    )
    high, low = split_high_low(small)
    extra = jnp.concatenate([high.astype(f32), low.astype(f32)], axis=0)
    here = pl.ds(pl.multiple_of(at.core * half, half), half)
    there = pl.ds(pl.multiple_of((1 - at.core) * half, half), half)
    for ky, keep_ref, send_ref in ((1, keep1_ref, send1_ref), (0, keep0_ref, send0_ref)):
        for kz in range(planes):
            to = pl.ds(pl.multiple_of(at.chip(kz, ky) * rows, 16), rows)
            keep_ref[kz, 0:rows, :] = scr_ref[to, here]
            send_ref[kz, 0:rows, :] = scr_ref[to, there].astype(bf16)
            keep_ref[kz, rows:full, :] = extra
            send_ref[kz, rows:full, :] = extra.astype(bf16)


def folded(extra):
    value = extra[:8] + extra[8:]
    high, low = split_high_low(value)
    return jnp.concatenate([high.astype(f32), low.astype(f32)], axis=0)


def sum_pieces(keep_ref, got_ref, *outs):
    rows = keep_ref.shape[1] - EXTRA
    for kz, out in enumerate(outs):
        total = keep_ref[kz] + got_ref[kz].astype(f32)
        out[0:rows, :] = total[:rows].astype(out.dtype)
        out[rows:, :] = folded(total[rows:]).astype(out.dtype)


def sum_pair(keep_ref, got_ref, out_ref):
    rows = keep_ref.shape[0] - EXTRA
    total = keep_ref[...] + got_ref[...].astype(f32)
    out_ref[0:rows, :] = total[:rows].astype(out_ref.dtype)
    out_ref[rows:, :] = folded(total[rows:]).astype(out_ref.dtype)


def kernel_total(place, *refs):
    parts, (mine_ref, other_ref, scr_ref, small_ref) = refs[:-4], refs[-4:]
    at = place()
    full, half = parts[0].shape
    rows = full - EXTRA
    total = None
    for k, part in enumerate(parts):
        value = part[...].astype(f32)
        total = value[:rows] if total is None else total + value[:rows]
        small_ref[k] = value[rows : rows + 8] + value[rows + 8 :]
    scr_ref[...] = total
    small = None
    for z in range(len(parts)):
        piece = small_ref[lax.rem(at.z + (len(parts) - z), len(parts))]
        small = piece if small is None else small + piece
    high, low = split_high_low(small)
    tail = jnp.zeros((mine_ref.shape[0] - rows // 2 - EXTRA, half), f32)
    for ref, c in ((mine_ref, at.core), (other_ref, 1 - at.core)):
        piece = scr_ref[pl.ds(pl.multiple_of(c * (rows // 2), 8), rows // 2), :]
        ref[...] = jnp.concatenate(
            [high.astype(f32), low.astype(f32), piece, tail][: 4 if tail.shape[0] else 3], axis=0
        ).astype(bf16)


def kernel_finish(place, mine_ref, c_ref, x_ref, xc_ref, grad_ref, bias_ref, stitch_ref):
    at = place()
    rows = grad_ref.shape[1]
    half = grad_ref.shape[2] // 2
    first = at.task == 0
    low_core = at.core == 0

    def lanes(one, two):
        return jnp.concatenate(
            [jnp.where(low_core, one, two), jnp.where(low_core, two, one)], axis=1
        )

    own = lanes(mine_ref[...].astype(f32), c_ref[...].astype(f32))
    far = lanes(x_ref[...].astype(f32), xc_ref[...].astype(f32))
    grad_ref[0] = jnp.where(first, own, far)[EXTRA : EXTRA + rows, :]
    grad_ref[1] = jnp.where(first, far, own)[EXTRA : EXTRA + rows, :]

    def small(ref):
        value = ref[...].astype(f32)
        value = value[0:8] + value[8:16]
        return jnp.concatenate([value[0:4], value[4:8]], axis=1)

    own, far = small(mine_ref), small(x_ref)
    bias_ref[0:1, :] = jnp.where(first, own, far)[0:1, :]
    bias_ref[1:2, :] = jnp.where(first, far, own)[0:1, :]
    own_pair = jnp.where(first, own[1:3], jnp.concatenate([own[2:3], own[1:2]], axis=0))
    far_pair = jnp.where(first, jnp.concatenate([far[2:3], far[1:2]], axis=0), far[1:3])
    stitch_ref[0] = jnp.where(first, own_pair, far_pair)
    stitch_ref[1] = jnp.where(first, far_pair, own_pair)


def picture_grad(place, side, slab, d_ref, w_ref, own_ref, far_ref, pad_ref):
    at = place()
    channels = d_ref.shape[1]
    depth = 3 * channels
    block = slab // 2
    blank = jnp.zeros((slab, depth), bf16)
    pad_ref[0:slab, :] = blank
    pad_ref[(side + 1) * slab :, :] = blank
    for y in range(side):
        wide = d_ref[y * slab : (y + 1) * slab, :].astype(f32)
        rows = slice((y + 1) * slab, (y + 2) * slab)
        pad_ref[rows, 0:channels] = pltpu.roll(wide, 1, 0).astype(bf16)
        pad_ref[rows, channels : 2 * channels] = wide.astype(bf16)
        pad_ref[rows, 2 * channels :] = pltpu.roll(wide, slab - 1, 0).astype(bf16)
    for start in range(0, side, 4):
        rows = min(4, side - start)
        total = None
        for ky in range(3):
            part = jnp.dot(
                pad_ref[(start + ky) * slab : (start + ky + rows) * slab, :],
                w_ref[ky * depth : (ky + 1) * depth, :],
                preferred_element_type=f32,
            )
            total = part if total is None else total + part
        for row in range(rows):
            zero = total[row * slab : row * slab + block]
            one = total[row * slab + block : (row + 1) * slab]
            own = jnp.where(at.task == 0, zero, one).astype(bf16)
            far = jnp.where(at.task == 0, one, zero).astype(bf16)
            own_ref[start + row] = own.reshape(own_ref.shape[1:])
            far_ref[start + row] = far.reshape(far_ref.shape[1:])


def picture_finish(place, g_ref, own_ref, far_ref, out_ref):
    at = place()
    side, few, _, depth = own_ref.shape
    columns = lax.broadcasted_iota(jnp.int32, (side, depth), 0)
    for n in range(few):
        limit = side - 2 * g_ref[n]
        for y in range(side):
            reach = jnp.where(y < limit, limit, 0)
            mask = jnp.where(columns < reach, 1.0, 0.0).astype(bf16)
            out_ref[n, at.task, y] = own_ref[y, n, 0:side, :] * mask
            out_ref[n, 1 - at.task, y] = far_ref[y, n, 0:side, :] * mask


def fc_grad(place, own_ref, oc_ref, x_ref, xc_ref, d_ref, dx_ref, out_ref):
    at = place()
    same = at.core == at.task
    own = jnp.where(same, own_ref[...], oc_ref[...])
    far = jnp.where(same, x_ref[...], xc_ref[...])
    contract = (((0,), (0,)), ((), ()))
    out_ref[at.task] = lax.dot_general(own, d_ref[...], contract, preferred_element_type=f32)
    out_ref[1 - at.task] = lax.dot_general(far, dx_ref[...], contract, preferred_element_type=f32)


def on_device(pairs, planes, *operands):
    (
        conv_input,
        group,
        conv_weight,
        conv_bias,
        stitch_pool,
        fc_weight,
        fc_bias,
        stitch_fc,
        cotangent,
    ) = operands
    chips = 2 * planes
    at = Place(pairs, planes)
    place = functools.partial(Place, pairs, planes)
    task, core = at.task, at.core
    few = conv_input.shape[0]
    images = 2 * few
    side = conv_input.shape[2]
    channels_in = conv_input.shape[4]
    channels = conv_bias.shape[1]
    pool = (side - 3) // 2 + 1
    units = fc_bias.shape[1]
    features = pool * pool * channels
    part = features // 2
    slab = images * WIDTH
    own_rows = conv_weight.shape[1]
    chip_rows = 2 * own_rows
    half = channels // 2

    def links(where):
        pairs_of = []
        for b in range(2 * pairs):
            for m in range(4 * planes):
                to = where(b, m // 4, (m // 2) % 2, m % 2)
                if to is not None:
                    far_b, z, y, c = to
                    far_m = ((z % planes) * 2 + y) * 2 + c
                    pairs_of.append((b * 4 * planes + m, far_b * 4 * planes + far_m))
        return pairs_of

    def move(value, dx=0, dz=0, dy=0, dc=0):
        where = lambda b, z, y, c: ((b + pairs * dx) % (2 * pairs), z + dz, y ^ dy, c ^ dc)
        return lax.ppermute(value, BOTH, links(where))

    def pick(array, index, axis=0):
        return lax.dynamic_index_in_dim(array, index, axis, keepdims=False)

    def ordered(flag, mine, other, axis=0):
        return jnp.where(
            flag == 0,
            jnp.concatenate([mine, other], axis=axis),
            jnp.concatenate([other, mine], axis=axis),
        )

    def after(value, *others):
        return lax.optimization_barrier((value, *others))[0]

    shifts = []
    for near in range(1, planes // 2 + 1):
        shifts.extend(sorted({near, planes - near}))

    def gather_chips(block):
        rows = [[block, move(block, dy=1)]] + [None] * (planes - 1)
        here = {k: move(block, dz=k) for k in shifts}
        for k in shifts:
            rows[k] = [here[k], move(here[k], dy=1)]
        return [piece for pair in rows for piece in pair]

    weight = pick(conv_weight, task)
    weight_other = move(lax.dynamic_slice_in_dim(weight, (1 - core) * half, half, 1), dc=1)
    weight_mine = lax.dynamic_slice_in_dim(weight, core * half, half, 1)
    weight_block = ordered(core, weight_mine, weight_other)
    weight_blocks = gather_chips(weight_block)
    weight_far = [move(block, dc=1) for block in weight_blocks]

    wide = (side, few, WIDTH, channels_in)
    picture_own, picture_send, cot_send = call(
        functools.partial(split_inputs, place),
        (
            shape_of(wide, bf16),
            shape_of(wide, bf16),
            shape_of((4 * planes, images, units), bf16),
        ),
        (group, conv_input, cotangent),
        scalars=1,
    )
    picture_far = move(picture_send, dx=1)
    group_far = move(group, dx=1)
    stacked, stacked_t = call(
        functools.partial(widen, place),
        (
            shape_of(((side + 2) * slab, 3 * channels_in), bf16),
            shape_of((3 * channels_in, (side + 2) * slab), bf16),
        ),
        (picture_own, picture_far),
    )

    fc_parts = fc_weight.reshape(4, part, units)
    fc_mine = pick(fc_parts, 2 * task + core)
    fc_other = move(pick(fc_parts, 2 * task + 1 - core), dc=1)

    cot_own = lax.all_to_all(cot_send, "mp", split_axis=0, concat_axis=0, tiled=True)
    cot_far = move(cot_own, dx=1)
    rows_all = chips * 2 * images
    up = call(
        functools.partial(cot_rows, place), shape_of((2, rows_all, units), f32), (cot_own, cot_far)
    )

    window = np.zeros((pool * images, slab), np.float32)
    for q in range(pool):
        for n in range(images):
            window[q * images + n, n * WIDTH + 2 * q : n * WIDTH + 2 * q + 3] = 1.0
    window_t = jnp.asarray(window.T, bf16)
    window = jnp.asarray(window, bf16)
    stacked = after(stacked, stacked_t, up, fc_mine)
    conv_pre, pooled, kernel = call(
        functools.partial(conv_forward, place, side, pool, images),
        (
            shape_of((side * slab, channels), f32),
            shape_of((2, images, part), bf16),
            shape_of((chips * chip_rows, channels), bf16),
        ),
        (group, group_far, stacked, conv_bias, window, *weight_blocks, *weight_far),
        scalars=2,
        mib=32,
    )

    pooled_mine, pooled_other = pooled[0], pooled[1]
    pooled_x = move(pooled_mine, dx=1)
    pooled_xc = move(pooled_other, dx=1, dc=1)
    pooled_c = move(pooled_other, dc=1)
    pooled_own = ordered(core, pooled_mine, pooled_c)
    pooled_far = ordered(core, pooled_x, pooled_xc)
    stitch = jnp.where(task == 0, stitch_pool, stitch_pool[::-1, ::-1])

    def spread(weights, value):
        return value.reshape(2 * images, -1, channels).astype(f32) * weights

    block = (spread(stitch[0, 0], pooled_own) + spread(stitch[0, 1], pooled_far)).astype(bf16)
    blocks = gather_chips(block.reshape(2 * images, part))

    slope, kernel_back = call(
        slope_and_back,
        (
            shape_of(conv_pre.shape, f32),
            shape_of((9 * channels, channels_in), bf16),
        ),
        (after(conv_pre, blocks[1]), kernel),
    )

    gathered, far_term = call(
        fc_far,
        (shape_of((rows_all, part), bf16), shape_of((rows_all, units), f32)),
        (*blocks, fc_other),
    )
    far_back = move(far_term, dc=1)
    own_term = call(fc_own, shape_of((rows_all, units), f32), (gathered, fc_mine))
    d_fc, hidden, fc_sums = call(
        functools.partial(fc_middle, place),
        (
            shape_of((rows_all, units), bf16),
            shape_of((rows_all, units), f32),
            shape_of((8, units), f32),
        ),
        (own_term, far_back, fc_bias, stitch_fc, up),
    )
    d_fc_far = move(d_fc, dc=1)
    piece = (2 * images, part)
    outs = call(
        fc_back,
        tuple(shape_of(piece, bf16 if j % 2 else f32) for j in range(chips)),
        (d_fc, d_fc_far, fc_mine, fc_other),
    )
    kept, sent = outs[0::2], outs[1::2]

    order = shifts[::-1] + [0]
    arrived = {k: move(sent[k], dy=1) for k in order}
    passed = {}
    for k in order[:-1]:
        low = call(add_rows, (shape_of(piece, bf16),), (kept[k], arrived[k]))[0]
        passed[k] = move(low, dz=-k)
    d_total, d_mine, d_mine_low, d_other = call(
        functools.partial(block_total, place),
        (
            shape_of(piece, f32),
            shape_of((images, part), f32),
            shape_of((images, part), bf16),
            shape_of((images, part), bf16),
        ),
        (kept[0], arrived[0], *[passed[k] for k in order[:-1]]),
    )

    d_x = move(d_mine_low, dx=1)
    d_xc = move(d_other, dx=1, dc=1)
    d_c = move(d_other, dc=1)
    stitch_sums = call(
        stitch_terms, shape_of((8, channels), f32), (d_total, pooled_own, pooled_far)
    )
    d_conv, d_bias = call(
        functools.partial(conv_slope, place, side, pool, images),
        (shape_of((side * slab, channels), bf16), shape_of((1, channels), f32)),
        (group, group_far, d_mine, d_c, d_x, d_xc, stitch_pool, slope, window_t),
        scalars=2,
    )

    full = chip_rows + EXTRA
    stack = (planes, full, half)
    keep1, keep0, send1, send0 = call(
        functools.partial(kernel_grad, place, slab),
        (shape_of(stack, f32), shape_of(stack, f32), shape_of(stack, bf16), shape_of(stack, bf16)),
        (stacked_t, d_conv, d_bias, stitch_sums),
        (pltpu.VMEM((chips * chip_rows, channels), f32),),
        mib=32,
    )
    got1, got0 = move(send1, dc=1), move(send0, dc=1)
    flat = (full, half)
    sent = call(sum_pieces, tuple(shape_of(flat, bf16) for _ in range(planes)), (keep1, got1))
    arrived = {k: move(sent[k], dy=1) for k in order}
    kept = call(sum_pieces, tuple(shape_of(flat, f32) for _ in range(planes)), (keep0, got0))
    parts = {}
    for k in order[:-1]:
        parts[k] = move(call(sum_pair, shape_of(flat, bf16), (kept[k], arrived[k])), dz=-k)
    parts[0] = call(sum_pair, shape_of(flat, f32), (kept[0], arrived[0]))
    tall = -(-(own_rows + EXTRA) // 16) * 16
    k_mine, k_other = call(
        functools.partial(kernel_total, place),
        (shape_of((tall, half), bf16), shape_of((tall, half), bf16)),
        tuple(parts[(planes - k) % planes] for k in range(planes)),
        (pltpu.VMEM((chip_rows, half), f32), pltpu.VMEM((planes, 8, half), f32)),
    )
    k_x = move(k_mine, dx=1)
    k_xc = move(k_other, dx=1, dc=1)
    k_c = move(k_other, dc=1)
    conv_weight_grad, conv_bias_grad, stitch_pool_grad = call(
        functools.partial(kernel_finish, place),
        (
            shape_of((2, own_rows, channels), f32),
            shape_of((2, channels), f32),
            shape_of((2, 2, channels), f32),
        ),
        (k_mine, k_c, k_x, k_xc),
    )

    back_own, back_send = call(
        functools.partial(picture_grad, place, side, slab),
        (shape_of(wide, bf16), shape_of(wide, bf16)),
        (after(d_conv, send1), kernel_back),
        (pltpu.VMEM(((side + 2) * slab, 3 * channels), bf16),),
    )
    back_far = move(back_send, dx=1)
    input_grad = call(
        functools.partial(picture_finish, place),
        shape_of(conv_input.shape, bf16),
        (group, back_own, back_far),
        scalars=1,
    )

    hidden_late = after(hidden, outs[0])
    cells = hidden_late.reshape(chips * 2, 2, few, units)
    hidden_here = pick(cells, task, 1)
    hidden_far = move(pick(cells, 1 - task, 1).astype(bf16), dx=1).astype(f32)
    mixes = jnp.where(task == 0, stitch_fc, stitch_fc[::-1, ::-1])
    mixed_own = mixes[0, 0] * hidden_here + mixes[0, 1] * hidden_far
    mixed_other = mixes[1, 0] * hidden_here + mixes[1, 1] * hidden_far
    mixed = ordered(
        task, mixed_own[:, None].astype(bf16), mixed_other[:, None].astype(bf16), axis=1
    )
    mixed = mixed.reshape(planes, 2, 2, 2, few, units)
    mixed = jnp.where(at.y == 0, mixed, mixed[:, ::-1])
    mixed = jnp.roll(mixed[::-1], at.z + 1, axis=0).reshape(chips * 2, images, units)
    mixed = lax.all_to_all(mixed, "mp", split_axis=0, concat_axis=0, tiled=True)
    output = jnp.transpose(mixed.reshape(chips * 2, 2, few, units), (2, 1, 0, 3))
    output = output.reshape(cotangent.shape)

    def both(own, axis=0):
        own = jnp.expand_dims(own, axis)
        return ordered(task, own, jnp.zeros_like(own), axis=axis)

    gathered_late = after(gathered, outs[1])
    d_fc_late = after(d_fc, outs[1])
    sums_late = after(fc_sums, outs[1])
    if pairs > 1:
        fc_bias_grad, stitch_fc_grad = lax.psum(
            (both(sums_late[0]), both(sums_late[1:3], axis=1)), "batch"
        )
    else:
        sums_far = move(sums_late, dx=1)
        fc_bias_grad = ordered(task, sums_late[0:1], sums_far[0:1])
        stitch_fc_grad = ordered(task, sums_late[1:3][:, None], sums_far[1:3][:, None], axis=1)
    cross = lambda b, z, y, c: ((b + pairs) % (2 * pairs), z, y, c) if c != b // pairs else None
    features_x = lax.ppermute(gathered_late, BOTH, links(cross))
    features_c = move(gathered_late, dc=1)
    d_fc_x = move(d_fc_late, dx=1)
    features_xc = move(features_x, dc=1)
    steps = part // 512
    wide_spec = pl.BlockSpec((rows_all, part // steps), lambda i: (0, i))
    whole_spec = pl.BlockSpec((rows_all, units), lambda i: (0, 0))
    fc_weight_grad = pl.pallas_call(
        functools.partial(fc_grad, place),
        out_shape=shape_of((2, part, units), f32),
        grid=(steps,),
        in_specs=[wide_spec] * 4 + [whole_spec] * 2,
        out_specs=pl.BlockSpec((2, part // steps, units), lambda i: (0, i, 0)),
        compiler_params=pltpu.CompilerParams(vmem_limit_bytes=24 * MIB),
    )(gathered_late, features_c, features_x, features_xc, d_fc_late, d_fc_x)
    if pairs > 1:
        fc_weight_grad = lax.psum_scatter(
            ordered(task, fc_weight_grad, jnp.zeros_like(fc_weight_grad), axis=1),
            "batch",
            scatter_dimension=1,
            tiled=True,
        )
        conv_weight_grad, conv_bias_grad, stitch_pool_grad = lax.psum(
            tuple(
                both(pick(value, task))
                for value in (conv_weight_grad, conv_bias_grad, stitch_pool_grad)
            ),
            "batch",
        )
    return (
        output,
        input_grad,
        conv_weight_grad,
        conv_bias_grad,
        stitch_pool_grad,
        fc_weight_grad,
        fc_bias_grad,
        stitch_fc_grad,
    )


def solution(mesh):
    pairs = mesh.shape["batch"] // 2
    planes = mesh.shape["mp"] // 4
    in_specs = (
        P(BOTH, None, None, None, None),
        P(BOTH),
        P(None, "mp", None),
        P(),
        P(),
        P(None, None, "mp"),
        P(None, "mp"),
        P(None, None, "mp"),
        P(BOTH, None, None),
    )
    out_specs = (
        P(BOTH, None, None),
        P(BOTH, None, None, None, None),
        P(None, "mp", None),
        P(),
        P(),
        P(None, "batch", "mp"),
        P(None, "mp"),
        P(None, None, "mp"),
    )
    return jax.shard_map(
        functools.partial(on_device, pairs, planes),
        mesh=mesh,
        in_specs=in_specs,
        out_specs=out_specs,
        check_vma=False,
    )
```

profile of v0, /device:TPU:0, one launch (start us, length us, event | category | flops | bytes accessed | tf_op | source)
XLA Modules:
  0.0 202.7 jit_solution(11203254492064063853)
XLA Ops:
  3.2 2.9 %collective-permute-start.5 = (bf16[432,128]{1,0:T(8,128)(2,1)S(1)}, bf16[432,128]{1,0:T(8,128)(2,1)S(1)}, u32[]{:S(2)}, u32[]{:S(2)}) collective-permute-start(bf16[432,128]{1,0:T(8,128)(2,1)S(1)} %maximum_select_fusion.2.refs_5_), channel_id=1, source_target_pairs={{0,4},{1,5},{2,6},{3,7},{4,8},{5,9},{6,10},{7,11},{8,12},{9,13},{1... | collective-permute-start | bytes 331784 | tf_op jit(solution)/shard_map/ppermute | solution.py:540
  9.2 4.9 %all-to-all-start = ((bf16[16,8,256]{2,1,0:T(8,128)(2,1)}), bf16[16,8,256]{2,1,0:T(8,128)(2,1)S(1)}, u32[]{:S(2)}, u32[]{:S(2)}) async-start(bf16[16,8,256]{2,1,0:T(8,128)(2,1)} %get-tuple-element.67), calls=%async_computation | async-start | bytes 131072 | tf_op jit(solution)/shard_map/all_to_all | solution.py:599
  16.0 2.4 %collective-permute-start.7 = (bf16[432,128]{1,0:T(8,128)(2,1)S(1)}, bf16[432,128]{1,0:T(8,128)(2,1)S(1)}, u32[]{:S(2)}, u32[]{:S(2)}) collective-permute-start(bf16[432,128]{1,0:T(8,128)(2,1)S(1)} %maximum_select_fusion.2.refs_5_), channel_id=1, source_target_pairs={{0,8},{1,9},{2,10},{3,11},{4,12},{5,13},{6,14},{7,15},{8,0},{9,1},... | collective-permute-start | bytes 331784 | tf_op jit(solution)/shard_map/ppermute | solution.py:540
  30.5 4.1 %dynamic-slice_bitcast_fusion = (bf16[4608,256]{1,0:T(8,128)(2,1)}, bf16[4608,256]{1,0:T(8,128)(2,1)S(1)}) fusion(bf16[4,4608,256]{2,1,0:T(8,128)(2,1)} %bitcast.43, s32[]{:T(128)S(6)} %select_n.119, s32[]{:T(128)S(6)} %select_n.107), kind=kLoop, calls=%fused_computation | loop fusion | bytes 9437192 | tf_op jit(solution)/shard_map/jit(dynamic_index_in_dim)/squeeze | solution.py:543
  35.8 5.0 %collective-permute-done.1.far_ref = bf16[13,4,16,384]{3,2,1,0:T(8,128)(2,1)} collective-permute-done((bf16[13,4,16,384]{3,2,1,0:T(8,128)(2,1)}, bf16[13,4,16,384]{3,2,1,0:T(8,128)(2,1)}, u32[]{:S(2)}, u32[]{:S(2)}) %collective-permute-start.1) | collective-permute-done | bytes 639008 | tf_op jit(solution)/shard_map/ppermute | solution.py:540
  42.4 3.0 %shard_map.171 = (bf16[1920,1152]{1,0:T(8,128)(2,1)S(1)}, bf16[1152,1920]{1,0:T(8,128)(2,1)S(1)}) custom-call(bf16[13,4,16,384]{3,2,1,0:T(8,128)(2,1)S(1)} %get-tuple-element.63.own_ref, bf16[13,4,16,384]{3,2,1,0:T(8,128)(2,1)} %collective-permute-done.1.far_ref), custom_call_target="tpu_custom_call" | custom-call | tf_op jit(solution)/shard_map/pallas_call | solution.py:24
  49.9 8.0 %shard_map.173 = (f32[1664,256]{1,0:T(8,128)S(1)}, bf16[2,8,4608]{2,1,0:T(8,128)(2,1)S(1)}, bf16[3456,256]{1,0:T(8,128)(2,1)S(1)}) custom-call(s32[4]{0:T(128)S(1)} %copy-done.38, s32[4]{0:T(128)S(1)} %collective-permute-done.refs_1_, bf16[1920,1152]{1,0:T(8,128)(2,1)S(1)} %get-tuple-element.68.refs_2_, f32[2,256]{1,0:T(2,128)S(1)} %copy-done.39, ...), custom_call_target="tpu_custom_call" | custom-call | tf_op jit(solution)/shard_map/pallas_call | solution.py:24
  62.7 4.0 %collective-permute-done.20 = bf16[8,4608]{1,0:T(8,128)(2,1)S(1)} collective-permute-done((bf16[8,4608]{1,0:T(8,128)(2,1)S(1)}, bf16[8,4608]{1,0:T(8,128)(2,1)S(1)}, u32[]{:S(2)}, u32[]{:S(2)}) %collective-permute-start.20) | collective-permute-done | bytes 73760 | tf_op jit(solution)/shard_map/ppermute | solution.py:540
  66.8 2.8 %collective-permute-start.23 = (bf16[16,4608]{1,0:T(8,128)(2,1)S(1)}, bf16[16,4608]{1,0:T(8,128)(2,1)S(1)}, u32[]{:S(2)}, u32[]{:S(2)}) collective-permute-start(bf16[16,4608]{1,0:T(8,128)(2,1)S(1)} %get-tuple-element.134.refs_0_), channel_id=1, source_target_pairs={{0,4},{1,5},{2,6},{3,7},{4,8},{5,9},{6,10},{7,11},{8,12},{9,13},{1... | collective-permute-start | bytes 442376 | tf_op jit(solution)/shard_map/ppermute | solution.py:540
  69.6 3.4 %collective-permute-start.25 = (bf16[16,4608]{1,0:T(8,128)(2,1)S(1)}, bf16[16,4608]{1,0:T(8,128)(2,1)S(1)}, u32[]{:S(2)}, u32[]{:S(2)}) collective-permute-start(bf16[16,4608]{1,0:T(8,128)(2,1)S(1)} %get-tuple-element.134.refs_0_), channel_id=1, source_target_pairs={{0,8},{1,9},{2,10},{3,11},{4,12},{5,13},{6,14},{7,15},{8,0},{9,1},... | collective-permute-start | bytes 442376 | tf_op jit(solution)/shard_map/ppermute | solution.py:540
  73.6 3.7 %collective-permute-done.23.refs_2_ = bf16[16,4608]{1,0:T(8,128)(2,1)S(1)} collective-permute-done((bf16[16,4608]{1,0:T(8,128)(2,1)S(1)}, bf16[16,4608]{1,0:T(8,128)(2,1)S(1)}, u32[]{:S(2)}, u32[]{:S(2)}) %collective-permute-start.23) | collective-permute-done | bytes 147488 | tf_op jit(solution)/shard_map/ppermute | solution.py:540
  77.8 4.6 %collective-permute-done.25.refs_4_ = bf16[16,4608]{1,0:T(8,128)(2,1)S(1)} collective-permute-done((bf16[16,4608]{1,0:T(8,128)(2,1)S(1)}, bf16[16,4608]{1,0:T(8,128)(2,1)S(1)}, u32[]{:S(2)}, u32[]{:S(2)}) %collective-permute-start.25) | collective-permute-done | bytes 147488 | tf_op jit(solution)/shard_map/ppermute | solution.py:540
  84.5 4.7 %collective-permute-done.26.refs_5_ = bf16[16,4608]{1,0:T(8,128)(2,1)S(1)} collective-permute-done((bf16[16,4608]{1,0:T(8,128)(2,1)S(1)}, bf16[16,4608]{1,0:T(8,128)(2,1)S(1)}, u32[]{:S(2)}, u32[]{:S(2)}) %collective-permute-start.26) | collective-permute-done | bytes 147488 | tf_op jit(solution)/shard_map/ppermute | solution.py:540
  91.3 2.1 %shard_map.174 = (bf16[128,4608]{1,0:T(8,128)(2,1)S(1)}, f32[128,256]{1,0:T(8,128)S(1)}) custom-call(bf16[16,4608]{1,0:T(8,128)(2,1)S(1)} %get-tuple-element.134.refs_0_, bf16[16,4608]{1,0:T(8,128)(2,1)S(1)} %collective-permute-done.22.refs_1_, bf16[16,4608]{1,0:T(8,128)(2,1)S(1)} %collective-permute-done.23.refs_2_, ...), custom_call_target="tpu_custom_call" | custom-call | tf_op jit(solution)/shard_map/pallas_call | solution.py:24
  97.6 3.4 %shard_map.177 = (f32[16,4608]{1,0:T(8,128)S(1)}, bf16[16,4608]{1,0:T(8,128)(2,1)S(1)}, f32[16,4608]{1,0:T(8,128)S(1)}, bf16[16,4608]{1,0:T(8,128)(2,1)S(1)}, f3...) custom-call(bf16[128,256]{1,0:T(8,128)(2,1)S(1)} %get-tuple-element., ...), custom_call_target="tpu_custom_call" | custom-call | tf_op jit(solution)/shard_map/pallas_call | solution.py:24
  108.3 3.0 %collective-permute-done.36.got_ref = bf16[16,4608]{1,0:T(8,128)(2,1)S(1)} collective-permute-done((bf16[16,4608]{1,0:T(8,128)(2,1)S(1)}, bf16[16,4608]{1,0:T(8,128)(2,1)S(1)}, u32[]{:S(2)}, u32[]{:S(2)}) %collective-permute-start.36) | collective-permute-done | bytes 147488 | tf_op jit(solution)/shard_map/ppermute | solution.py:540
  112.0 2.5 %collective-permute-done.38.got_ref = bf16[16,4608]{1,0:T(8,128)(2,1)S(1)} collective-permute-done((bf16[16,4608]{1,0:T(8,128)(2,1)S(1)}, bf16[16,4608]{1,0:T(8,128)(2,1)S(1)}, u32[]{:S(2)}, u32[]{:S(2)}) %collective-permute-start.38) | collective-permute-done | bytes 147488 | tf_op jit(solution)/shard_map/ppermute | solution.py:540
  117.7 4.6 %collective-permute-done.35.refs_1_ = bf16[16,4608]{1,0:T(8,128)(2,1)S(1)} collective-permute-done((bf16[16,4608]{1,0:T(8,128)(2,1)S(1)}, bf16[16,4608]{1,0:T(8,128)(2,1)S(1)}, u32[]{:S(2)}, u32[]{:S(2)}) %collective-permute-start.35) | collective-permute-done | bytes 147488 | tf_op jit(solution)/shard_map/ppermute | solution.py:540
  122.2 3.1 %collective-permute-done.39.refs_3_ = bf16[16,4608]{1,0:T(8,128)(2,1)S(1)} collective-permute-done((bf16[16,4608]{1,0:T(8,128)(2,1)S(1)}, bf16[16,4608]{1,0:T(8,128)(2,1)S(1)}, u32[]{:S(2)}, u32[]{:S(2)}) %collective-permute-start.39) | collective-permute-done | bytes 147488 | tf_op jit(solution)/shard_map/ppermute | solution.py:540
  132.3 4.4 %shard_map.185 = (f32[4,448,128]{2,1,0:T(8,128)S(1)}, f32[4,448,128]{2,1,0:T(8,128)S(1)}, bf16[4,448,128]{2,1,0:T(8,128)(2,1)}, bf16[4,448,128]{2,1,0:T(8,128)(2,1)S(1)}) custom-call(bf16[1152,1920]{1,0:T(8,128)(2,1)S(1)} %bitcast.42, bf16[1664,256]{1,0:T(8,128)(2,1)S(1)} %get-tuple-element.94.d_ref, f32[1,256]{1,0:T(1,128)S(1)} %get-tuple-element.91.bias_ref, ...), custom_call_target="tpu_custom_call" | custom-call | tf_op jit(solution)/shard_map/pallas_call | solution.py:24
  155.3 5.0 %shard_map.186 = (bf16[13,4,16,384]{3,2,1,0:T(8,128)(2,1)S(1)}, bf16[13,4,16,384]{3,2,1,0:T(8,128)(2,1)}) custom-call(bf16[1664,256]{1,0:T(8,128)(2,1)S(1)} %get-tuple-element.94.d_ref, bf16[2304,384]{1,0:T(8,128)(2,1)S(1)} %copy-done.2), custom_call_target="tpu_custom_call" | custom-call | tf_op jit(solution)/shard_map/pallas_call | solution.py:24
  169.6 3.7 %collective-permute-done.48.refs_1_ = bf16[448,128]{1,0:T(8,128)(2,1)S(1)} collective-permute-done((bf16[448,128]{1,0:T(8,128)(2,1)S(1)}, bf16[448,128]{1,0:T(8,128)(2,1)S(1)}, u32[]{:S(2)}, u32[]{:S(2)}) %collective-permute-start.48) | collective-permute-done | bytes 114720 | tf_op jit(solution)/shard_map/ppermute | solution.py:540
  174.8 3.5 %all-to-all-start.1 = ((bf16[16,8,256]{2,1,0:T(8,128)(2,1)}), bf16[16,8,256]{2,1,0:T(8,128)(2,1)S(1)}, u32[]{:S(2)}, u32[]{:S(2)}) async-start(bf16[16,8,256]{2,1,0:T(8,128)(2,1)} %reshape.78), calls=%async_computation.1 | async-start | bytes 131072 | tf_op jit(solution)/shard_map/all_to_all | solution.py:768
  193.7 9.0 %shard_map.196 = f32[2,4608,256]{2,1,0:T(8,128)} custom-call(bf16[128,4608]{1,0:T(8,128)(2,1)S(1)} %get-tuple-element.114.x_ref.own_ref, bf16[128,4608]{1,0:T(8,128)(2,1)} %collective-permute-done.56.oc_ref, bf16[128,4608]{1,0:T(8,128)(2,1)S(1)} %collective-permute-done.57.x_ref, bf16[128,4608]{1,0:T(8,128)(2,1)} %collective-permute-done.58.xc_ref, ...), custom_call_target="tpu_custom_call" | custom-call | tf_op jit(solution)/shard_map/pallas_call | solution.py:795
  (271 shorter events, 103.6 us)
Async XLA Ops:
  3.2 18.8 %collective-permute-start.5 = (bf16[432,128]{1,0:T(8,128)(2,1)S(1)}, bf16[432,128]{1,0:T(8,128)(2,1)S(1)}, u32[]{:S(2)}, u32[]{:S(2)}) collective-permute-start(bf16[432,128]{1,0:T(8,128)(2,1)S(1)} %maximum_select_fusion.2.refs_5_), channel_id=1, source_target_pairs={{0,4},{1,5},{2,6},{3,7},{4,8},{5,9},{6,10},{7,11},{8,12},{9,13},{1... | collective-permute-start | bytes 331784 | tf_op jit(solution)/shard_map/ppermute | solution.py:540
  9.2 13.3 %all-to-all-start = ((bf16[16,8,256]{2,1,0:T(8,128)(2,1)}), bf16[16,8,256]{2,1,0:T(8,128)(2,1)S(1)}, u32[]{:S(2)}, u32[]{:S(2)}) async-start(bf16[16,8,256]{2,1,0:T(8,128)(2,1)} %get-tuple-element.67), calls=%async_computation | async-start | bytes 131072 | tf_op jit(solution)/shard_map/all_to_all | solution.py:599
  25.1 15.8 %collective-permute-start.1 = (bf16[13,4,16,384]{3,2,1,0:T(8,128)(2,1)}, bf16[13,4,16,384]{3,2,1,0:T(8,128)(2,1)}, u32[]{:S(2)}, u32[]{:S(2)}) collective-permute-start(bf16[13,4,16,384]{3,2,1,0:T(8,128)(2,1)} %get-tuple-element.64), channel_id=1, source_target_pairs={{0,16},{1,17},{2,18},{3,19},{4,20},{5,21},{6,22},{7,23},{8,24},{9,... | collective-permute-start | bytes 1916936 | tf_op jit(solution)/shard_map/ppermute | solution.py:540
  34.7 12.8 %collective-permute-start.15 = (bf16[432,128]{1,0:T(8,128)(2,1)S(1)}, bf16[432,128]{1,0:T(8,128)(2,1)S(1)}, u32[]{:S(2)}, u32[]{:S(2)}) collective-permute-start(bf16[432,128]{1,0:T(8,128)(2,1)S(1)} %collective-permute-done.7.refs_9_), channel_id=1, source_target_pairs={{0,1},{1,0},{2,3},{3,2},{4,5},{5,4},{6,7},{7,6},{8,9},{9,8},{10,11... | collective-permute-start | bytes 331784 | tf_op jit(solution)/shard_map/ppermute | solution.py:540
  35.2 12.9 %collective-permute-start.17 = (bf16[432,128]{1,0:T(8,128)(2,1)}, bf16[432,128]{1,0:T(8,128)(2,1)S(1)}, u32[]{:S(2)}, u32[]{:S(2)}) collective-permute-start(bf16[432,128]{1,0:T(8,128)(2,1)} %collective-permute-done.9.refs_11_), channel_id=1, source_target_pairs={{0,1},{1,0},{2,3},{3,2},{4,5},{5,4},{6,7},{7,6},{8,9},{9,8},{10,11... | collective-permute-start | bytes 331784 | tf_op jit(solution)/shard_map/ppermute | solution.py:540
  35.3 12.8 %collective-permute-start.14 = (bf16[432,128]{1,0:T(8,128)(2,1)}, bf16[432,128]{1,0:T(8,128)(2,1)S(1)}, u32[]{:S(2)}, u32[]{:S(2)}) collective-permute-start(bf16[432,128]{1,0:T(8,128)(2,1)} %copy-done.29), channel_id=1, source_target_pairs={{0,1},{1,0},{2,3},{3,2},{4,5},{5,4},{6,7},{7,6},{8,9},{9,8},{10,11... | collective-permute-start | bytes 331784 | tf_op jit(solution)/shard_map/ppermute | solution.py:540
  35.7 12.4 %collective-permute-start.16 = (bf16[432,128]{1,0:T(8,128)(2,1)}, bf16[432,128]{1,0:T(8,128)(2,1)S(1)}, u32[]{:S(2)}, u32[]{:S(2)}) collective-permute-start(bf16[432,128]{1,0:T(8,128)(2,1)} %collective-permute-done.8.refs_10_), channel_id=1, source_target_pairs={{0,1},{1,0},{2,3},{3,2},{4,5},{5,4},{6,7},{7,6},{8,9},{9,8},{10,11... | collective-permute-start | bytes 331784 | tf_op jit(solution)/shard_map/ppermute | solution.py:540
  47.6 43.7 %collective-permute-start.29 = (bf16[4608,256]{1,0:T(8,128)(2,1)}, bf16[4608,256]{1,0:T(8,128)(2,1)}, u32[]{:S(2)}, u32[]{:S(2)}) collective-permute-start(bf16[4608,256]{1,0:T(8,128)(2,1)} %get-tuple-element.137), channel_id=1, source_target_pairs={{0,1},{1,0},{2,3},{3,2},{4,5},{5,4},{6,7},{7,6},{8,9},{9,8},{10,11... | collective-permute-start | bytes 7077896 | tf_op jit(solution)/shard_map/ppermute | solution.py:540
  69.6 12.8 %collective-permute-start.25 = (bf16[16,4608]{1,0:T(8,128)(2,1)S(1)}, bf16[16,4608]{1,0:T(8,128)(2,1)S(1)}, u32[]{:S(2)}, u32[]{:S(2)}) collective-permute-start(bf16[16,4608]{1,0:T(8,128)(2,1)S(1)} %get-tuple-element.134.refs_0_), channel_id=1, source_target_pairs={{0,8},{1,9},{2,10},{3,11},{4,12},{5,13},{6,14},{7,15},{8,0},{9,1},... | collective-permute-start | bytes 442376 | tf_op jit(solution)/shard_map/ppermute | solution.py:540
  73.0 11.5 %collective-permute-start.22 = (bf16[16,4608]{1,0:T(8,128)(2,1)S(1)}, bf16[16,4608]{1,0:T(8,128)(2,1)S(1)}, u32[]{:S(2)}, u32[]{:S(2)}) collective-permute-start(bf16[16,4608]{1,0:T(8,128)(2,1)S(1)} %get-tuple-element.134.refs_0_), channel_id=1, source_target_pairs={{0,2},{1,3},{2,0},{3,1},{4,6},{5,7},{6,4},{7,5},{8,10},{9,11},{10,... | collective-permute-start | bytes 442376 | tf_op jit(solution)/shard_map/ppermute | solution.py:540
  101.0 46.5 %collective-permute-start.57 = (bf16[128,4608]{1,0:T(8,128)(2,1)S(1)}, bf16[128,4608]{1,0:T(8,128)(2,1)S(1)}, u32[]{:S(2)}, u32[]{:S(2)}) collective-permute-start(bf16[128,4608]{1,0:T(8,128)(2,1)S(1)} %get-tuple-element.114.x_ref.own_ref), channel_id=1, source_target_pairs={{1,17},{3,19},{5,21},{7,23},{9,25},{11,27},{13,29},{15,31},{16,0},... | collective-permute-start | bytes 3538952 | tf_op jit(solution)/shard_map/ppermute | solution.py:788
  105.1 12.5 %collective-permute-start.33 = (bf16[16,4608]{1,0:T(8,128)(2,1)S(1)}, bf16[16,4608]{1,0:T(8,128)(2,1)S(1)}, u32[]{:S(2)}, u32[]{:S(2)}) collective-permute-start(bf16[16,4608]{1,0:T(8,128)(2,1)S(1)} %get-tuple-element.76), channel_id=1, source_target_pairs={{0,2},{1,3},{2,0},{3,1},{4,6},{5,7},{6,4},{7,5},{8,10},{9,11},{10,... | collective-permute-start | bytes 442376 | tf_op jit(solution)/shard_map/ppermute | solution.py:540
  108.2 14.0 %collective-permute-start.35 = (bf16[16,4608]{1,0:T(8,128)(2,1)S(1)}, bf16[16,4608]{1,0:T(8,128)(2,1)S(1)}, u32[]{:S(2)}, u32[]{:S(2)}) collective-permute-start(bf16[16,4608]{1,0:T(8,128)(2,1)S(1)} %shard_map.178), channel_id=1, source_target_pairs={{0,8},{1,9},{2,10},{3,11},{4,12},{5,13},{6,14},{7,15},{8,0},{9,1},... | collective-permute-start | bytes 442376 | tf_op jit(solution)/shard_map/ppermute | solution.py:540
  111.4 10.8 %collective-permute-start.37 = (bf16[16,4608]{1,0:T(8,128)(2,1)S(1)}, bf16[16,4608]{1,0:T(8,128)(2,1)S(1)}, u32[]{:S(2)}, u32[]{:S(2)}) collective-permute-start(bf16[16,4608]{1,0:T(8,128)(2,1)S(1)} %shard_map.179), channel_id=1, source_target_pairs={{0,4},{1,5},{2,6},{3,7},{4,8},{5,9},{6,10},{7,11},{8,12},{9,13},{1... | collective-permute-start | bytes 442376 | tf_op jit(solution)/shard_map/ppermute | solution.py:540
  114.6 10.7 %collective-permute-start.39 = (bf16[16,4608]{1,0:T(8,128)(2,1)S(1)}, bf16[16,4608]{1,0:T(8,128)(2,1)S(1)}, u32[]{:S(2)}, u32[]{:S(2)}) collective-permute-start(bf16[16,4608]{1,0:T(8,128)(2,1)S(1)} %shard_map.180), channel_id=1, source_target_pairs={{0,12},{1,13},{2,14},{3,15},{4,0},{5,1},{6,2},{7,3},{8,4},{9,5},{1... | collective-permute-start | bytes 442376 | tf_op jit(solution)/shard_map/ppermute | solution.py:540
  140.5 53.2 %collective-permute-start.56 = (bf16[128,4608]{1,0:T(8,128)(2,1)S(1)}, bf16[128,4608]{1,0:T(8,128)(2,1)}, u32[]{:S(2)}, u32[]{:S(2)}) collective-permute-start(bf16[128,4608]{1,0:T(8,128)(2,1)S(1)} %get-tuple-element.114.x_ref.own_ref), channel_id=1, source_target_pairs={{0,1},{1,0},{2,3},{3,2},{4,5},{5,4},{6,7},{7,6},{8,9},{9,8},{10,11... | collective-permute-start | bytes 3538952 | tf_op jit(solution)/shard_map/ppermute | solution.py:540
  147.5 46.2 %collective-permute-start.58 = (bf16[128,4608]{1,0:T(8,128)(2,1)S(1)}, bf16[128,4608]{1,0:T(8,128)(2,1)}, u32[]{:S(2)}, u32[]{:S(2)}) collective-permute-start(bf16[128,4608]{1,0:T(8,128)(2,1)S(1)} %collective-permute-done.57.x_ref), channel_id=1, source_target_pairs={{0,1},{1,0},{2,3},{3,2},{4,5},{5,4},{6,7},{7,6},{8,9},{9,8},{10,11... | collective-permute-start | bytes 3538952 | tf_op jit(solution)/shard_map/ppermute | solution.py:540
  149.0 14.0 %collective-permute-start.32 = (bf16[16,4,256]{2,1,0:T(4,128)(2,1)S(1)}, bf16[16,4,256]{2,1,0:T(4,128)(2,1)S(1)}, u32[]{:S(2)}, u32[]{:S(2)}) collective-permute-start(bf16[16,4,256]{2,1,0:T(4,128)(2,1)S(1)} %fusion.5), channel_id=1, source_target_pairs={{0,16},{1,17},{2,18},{3,19},{4,20},{5,21},{6,22},{7,23},{8,24},{9,... | collective-permute-start | bytes 98312 | tf_op jit(solution)/shard_map/ppermute | solution.py:540
  150.4 13.6 %collective-permute-start.49 = (bf16[448,128]{1,0:T(8,128)(2,1)}, bf16[448,128]{1,0:T(8,128)(2,1)S(1)}, u32[]{:S(2)}, u32[]{:S(2)}) collective-permute-start(bf16[448,128]{1,0:T(8,128)(2,1)} %copy-done.47), channel_id=1, source_target_pairs={{0,2},{1,3},{2,0},{3,1},{4,6},{5,7},{6,4},{7,5},{8,10},{9,11},{10,... | collective-permute-start | bytes 344072 | tf_op jit(solution)/shard_map/ppermute | solution.py:540
  152.6 12.9 %collective-permute-start.51 = (bf16[448,128]{1,0:T(8,128)(2,1)}, bf16[448,128]{1,0:T(8,128)(2,1)S(1)}, u32[]{:S(2)}, u32[]{:S(2)}) collective-permute-start(bf16[448,128]{1,0:T(8,128)(2,1)} %copy-done.46), channel_id=1, source_target_pairs={{0,2},{1,3},{2,0},{3,1},{4,6},{5,7},{6,4},{7,5},{8,10},{9,11},{10,... | collective-permute-start | bytes 344072 | tf_op jit(solution)/shard_map/ppermute | solution.py:540
  163.0 21.1 %collective-permute-start.43 = (bf16[13,4,16,384]{3,2,1,0:T(8,128)(2,1)}, bf16[13,4,16,384]{3,2,1,0:T(8,128)(2,1)}, u32[]{:S(2)}, u32[]{:S(2)}) collective-permute-start(bf16[13,4,16,384]{3,2,1,0:T(8,128)(2,1)} %get-tuple-element.97), channel_id=1, source_target_pairs={{0,16},{1,17},{2,18},{3,19},{4,20},{5,21},{6,22},{7,23},{8,24},{9,... | collective-permute-start | bytes 1916936 | tf_op jit(solution)/shard_map/ppermute | solution.py:540
  169.5 10.7 %collective-permute-start.50 = (bf16[448,128]{1,0:T(8,128)(2,1)}, bf16[448,128]{1,0:T(8,128)(2,1)}, u32[]{:S(2)}, u32[]{:S(2)}) collective-permute-start(bf16[448,128]{1,0:T(8,128)(2,1)} %shard_map.192), channel_id=1, source_target_pairs={{0,8},{1,9},{2,10},{3,11},{4,12},{5,13},{6,14},{7,15},{8,0},{9,1},... | collective-permute-start | bytes 344072 | tf_op jit(solution)/shard_map/ppermute | solution.py:540
  174.8 12.7 %all-to-all-start.1 = ((bf16[16,8,256]{2,1,0:T(8,128)(2,1)}), bf16[16,8,256]{2,1,0:T(8,128)(2,1)S(1)}, u32[]{:S(2)}, u32[]{:S(2)}) async-start(bf16[16,8,256]{2,1,0:T(8,128)(2,1)} %reshape.78), calls=%async_computation.1 | async-start | bytes 131072 | tf_op jit(solution)/shard_map/all_to_all | solution.py:768
  180.2 13.5 %collective-permute-start.59 = (bf16[128,256]{1,0:T(8,128)(2,1)S(1)}, bf16[128,256]{1,0:T(8,128)(2,1)S(1)}, u32[]{:S(2)}, u32[]{:S(2)}) collective-permute-start(bf16[128,256]{1,0:T(8,128)(2,1)S(1)} %copy-done.16), channel_id=1, source_target_pairs={{0,16},{1,17},{2,18},{3,19},{4,20},{5,21},{6,22},{7,23},{8,24},{9,... | collective-permute-start | bytes 196616 | tf_op jit(solution)/shard_map/ppermute | solution.py:540
  (91 other events, 573.0 us)
where the time goes:
time: 204 us; the launch traced here: 203 us
  starting transfers between devices  59.1 us (29%)
  waiting for transfers between devices  51.1 us (25%)
  Pallas kernels  47.8 us (23%)
  local copies, waits for them, and re-layouts  41.8 us (20%)
    ppermute x60, waiting for transfers between devices, move(): return lax.ppermute(value, BOTH, links(where))  51.1 us
    ppermute x60, starting transfers between devices, move(): return lax.ppermute(value, BOTH, links(where))  49.3 us
    pallas_call x26, Pallas kernels, call(): pl.pallas_call(body, out_shape=out_shape, in_specs=[SMEM] * scalars + [VM...  38.7 us
    unnamed x110, local copies, waits for them, and re-layouts  30.2 us
    pallas_call x1, Pallas kernels, on_device(): pl.pallas_call(functools.partial(fc_grad, place), out_shape=shape_of((2,...  9.03 us
    all_to_all x1, starting transfers between devices, on_device(): lax.all_to_all(cot_send, 'mp', split_axis=0, concat_axis=0, tiled=True)  4.93 us
    squeeze x1, local copies, waits for them, and re-layouts, pick(): return lax.dynamic_index_in_dim(array, index, axis, keepdims=False)  4.1 us
  transfers between devices with their start and end apart: 63, of which 22 were waited for; matrix products, arithmetic and copies ran while one was open for 8% of the time, Pallas kernels for 16%

commit v1 on v0

v1 whole, which is shorter than its diff:
```python
import functools

import jax
import jax.numpy as jnp
import numpy as np
from jax import lax
from jax.experimental import pallas as pl
from jax.experimental.pallas import tpu as pltpu
from jax.sharding import PartitionSpec as P

BOTH = ("batch", "mp")
WIDTH = 16
EXTRA = 16
ROOT_HALF = 0.7071067811865476
ROOT_TWO_PI_INV = 0.3989422804014327
VMEM = pl.BlockSpec(memory_space=pltpu.VMEM)
SMEM = pl.BlockSpec(memory_space=pltpu.SMEM)
ANY = pl.BlockSpec(memory_space=pl.ANY)
DMA = pltpu.SemaphoreType.DMA
MIB = 1024 * 1024
FLOPS_PER_US = 1100000000
bf16, f32 = jnp.bfloat16, jnp.float32
shape_of = jax.ShapeDtypeStruct


MICROS = dict(
    split_weights=0.3,
    join_cores=0.3,
    split_fc=1.5,
    split_inputs=1.0,
    cot_cores=0.3,
    cot_join=0.3,
    cot_planes=0.3,
    widen=2,
    conv_forward=7.5,
    stitch_block=0.3,
    cot_rows=0.3,
    slope_and_back=1.7,
    fc_far=0.5,
    fc_own=0.5,
    fc_middle=0.3,
    fc_back=1.6,
    add_rows=0.3,
    block_total=0.3,
    mix_output=0.3,
    stitch_terms=0.3,
    conv_slope=0.6,
    kernel_grad=3.7,
    picture_grad=2.2,
    sum_pieces=0.3,
    sum_three=0.3,
    output_aside=0.3,
    output_cores=0.3,
    picture_finish=0.8,
    output_finish=0.8,
    kernel_total=0.4,
    kernel_finish=0.8,
    fc_grad=4.8,
)


def cost(body):
    name = getattr(body, "func", body).__name__
    return pl.CostEstimate(
        flops=int(MICROS[name] * FLOPS_PER_US), bytes_accessed=1, transcendentals=0
    )


def call(body, out_shape, operands, scratch=(), scalars=0, room=4, blocks=None, any_first=False):
    held = [*operands[scalars + any_first :], *jax.tree.leaves(out_shape), *scratch]
    held = [a for a in held if hasattr(a, "shape") and jnp.issubdtype(a.dtype, jnp.number)]
    need = sum(int(np.prod(a.shape)) * jnp.dtype(a.dtype).itemsize for a in held)
    need = min(need, 40 * MIB)
    steps = {}
    out_specs = jax.tree.map(lambda _: VMEM, out_shape)
    if blocks is not None:
        steps = dict(grid=(1,))
        out_specs = pl.BlockSpec(out_shape.shape, lambda i: (0,) * len(out_shape.shape))
    return pl.pallas_call(
        body,
        out_shape=out_shape,
        **steps,
        in_specs=blocks
        or [SMEM] * scalars + [ANY] * any_first + [VMEM] * (len(operands) - scalars - any_first),
        out_specs=out_specs,
        scratch_shapes=scratch,
        cost_estimate=cost(body),
        compiler_params=pltpu.CompilerParams(vmem_limit_bytes=need * 5 // 4 + room * MIB),
    )(*operands)


class Place:
    def __init__(self, pairs, planes):
        batch_at, mp_at = lax.axis_index("batch"), lax.axis_index("mp")
        self.planes = planes
        self.task = lax.div(batch_at, pairs)
        self.core = lax.rem(mp_at, 2)
        self.y = lax.rem(lax.div(mp_at, 2), 2)
        self.z = lax.div(mp_at, 4)

    def chip(self, kz, ky):
        y = self.y if ky == 0 else 1 - self.y
        return lax.rem(self.z + (self.planes - kz), self.planes) * 2 + y


def phi_cdf(value):
    return 0.5 * (1.0 + lax.erf(value * ROOT_HALF))


def gelu_slope(value):
    return phi_cdf(value) + value * ROOT_TWO_PI_INV * jnp.exp(-0.5 * value * value)


def split_high_low(value):
    high = value.astype(bf16)
    return high, (value - high.astype(f32)).astype(bf16)


def window_sum(q_ref, value):
    high, low = split_high_low(value)
    return jnp.dot(q_ref[...], high, preferred_element_type=f32) + jnp.dot(
        q_ref[...], low, preferred_element_type=f32
    )


def split_weights(place, w_ref, mine_ref, other_ref):
    at = place()
    half = mine_ref.shape[1]
    for ref, core in ((mine_ref, at.core), (other_ref, 1 - at.core)):
        lanes = pl.ds(pl.multiple_of(core * half, half), half)
        ref[...] = w_ref[at.task, :, lanes]


def join_cores(place, mine_ref, other_ref, out_ref):
    at = place()
    mine, other = mine_ref[...].astype(f32), other_ref[...].astype(f32)
    low, high = jnp.where(at.core == 0, mine, other), jnp.where(at.core == 0, other, mine)
    out_ref[...] = jnp.concatenate([low, high], axis=0).astype(bf16)


def split_fc(place, w_ref, mine_ref, other_ref, sems):
    at = place()
    part = mine_ref.shape[0]
    copies = []
    for i, (ref, core) in enumerate(((mine_ref, at.core), (other_ref, 1 - at.core))):
        rows = pl.ds(pl.multiple_of(core * part, part), part)
        copies.append(pltpu.make_async_copy(w_ref.at[at.task, rows, :], ref, sems.at[i]))
        copies[-1].start()
    for copy in copies:
        copy.wait()


def split_inputs(place, g_ref, x_ref, cot_ref, own_ref, far_ref, out_ref):
    at = place()
    few, _, side, _, depth = x_ref.shape
    units = out_ref.shape[2]
    columns = lax.broadcasted_iota(jnp.int32, (side, depth), 0)
    value = cot_ref[...].astype(f32)
    rows = jnp.concatenate([value[i, t : t + 1] for t in range(2) for i in range(few)], axis=0)
    for ref in (own_ref, far_ref):
        ref[...] = jnp.zeros_like(ref)
    for n in range(few):
        limit = side - 2 * g_ref[n]
        mark = jnp.broadcast_to(g_ref[n], (1, depth)).astype(f32)
        for y in range(side):
            reach = jnp.where(y < limit, limit, 0)
            mask = jnp.where(columns < reach, 1.0, 0.0).astype(bf16)
            for ref, task in ((own_ref, at.task), (far_ref, 1 - at.task)):
                picture = x_ref[n, task, y] * mask
                if y:
                    ref[y, n, 0:side, :] = picture
                else:
                    gap = jnp.zeros((WIDTH - side - 1, depth), f32)
                    ref[y, n] = jnp.concatenate(
                        [picture.astype(f32), gap, mark], axis=0
                    ).astype(bf16)
    for m in range(out_ref.shape[0]):
        out_ref[m] = rows[:, m * units : (m + 1) * units].astype(bf16)


def widen(place, side, own_ref, far_ref, x3_ref, xt_ref, group_ref):
    at = place()
    _, few, _, depth = own_ref.shape
    channels = group_ref.shape[1]
    marks = []
    for ref in (own_ref, far_ref):
        last = [ref[0, n].astype(f32)[WIDTH - 1 :, :channels] for n in range(few)]
        marks.append(jnp.concatenate(last, axis=0))
    group_ref[...] = jnp.where(
        at.task == 0, jnp.concatenate(marks, axis=0), jnp.concatenate(marks[::-1], axis=0)
    )
    inside = lax.rem(lax.broadcasted_iota(jnp.int32, (few * WIDTH, depth), 0), WIDTH) < side
    block = few * WIDTH
    slab = 2 * block
    for edge in (0, side + 1):
        x3_ref[edge * slab : (edge + 1) * slab, :] = jnp.zeros((slab, 3 * depth), bf16)
        xt_ref[:, edge * slab : (edge + 1) * slab] = jnp.zeros((3 * depth, slab), bf16)
    for y in range(side):
        own = own_ref[y].reshape(block, depth).astype(f32)
        far = far_ref[y].reshape(block, depth).astype(f32)
        first = at.task == 0
        if y == 0:
            own, far = jnp.where(inside, own, 0.0), jnp.where(inside, far, 0.0)
        wide = jnp.concatenate(
            [jnp.where(first, own, far), jnp.where(first, far, own)], axis=0
        )
        rows = slice((y + 1) * slab, (y + 2) * slab)
        turned = wide.T
        for kx in range(3):
            lanes = slice(kx * depth, (kx + 1) * depth)
            shift = (1 - kx) % slab
            x3_ref[rows, lanes] = (pltpu.roll(wide, shift, 0) if shift else wide).astype(bf16)
            xt_ref[lanes, rows] = (pltpu.roll(turned, shift, 1) if shift else turned).astype(bf16)


def conv_forward(place, side, pool, images, *refs):
    g_ref, x_ref, b_ref, q_ref = refs[:4]
    blocks = refs[4:-4]
    pre_ref, mine_ref, other_ref, w_ref = refs[-4:]
    at = place()
    chips = len(blocks) // 2
    rows, half = blocks[0].shape
    here = pl.ds(pl.multiple_of(at.core * half, half), half)
    there = pl.ds(pl.multiple_of((1 - at.core) * half, half), half)
    for j in range(chips):
        to = pl.ds(pl.multiple_of(at.chip(j // 2, j % 2) * rows, 16), rows)
        w_ref[to, here] = blocks[j][...]
        w_ref[to, there] = blocks[chips + j][...]
    slab = images * WIDTH
    depth = x_ref.shape[1]
    channels = w_ref.shape[1]
    acts = {}
    bias = jnp.where(at.task == 0, b_ref[0:1, :], b_ref[1:2, :])
    group = g_ref[...]
    for start in range(0, side, 4):
        rows = min(4, side - start)
        total = None
        for ky in range(3):
            part = jnp.dot(
                x_ref[(start + ky) * slab : (start + ky + rows) * slab, :],
                w_ref[ky * depth : (ky + 1) * depth, :],
                preferred_element_type=f32,
            )
            total = part if total is None else total + part
        total = total + bias
        pre_ref[start * slab : (start + rows) * slab, :] = total
        act = total * phi_cdf(total)
        for row in range(rows):
            acts[start + row] = act[row * slab : (row + 1) * slab, :]
        for p in range(pool):
            if not (start <= 2 * p + 2 < start + rows):
                continue
            cells = window_sum(q_ref, acts[2 * p] + acts[2 * p + 1] + acts[2 * p + 2])
            row = []
            for q in range(pool):
                kept = jnp.where(max(p, q) + group < pool, 1.0 / 9.0, 0.0)
                row.append((cells[q * images : (q + 1) * images, :] * kept).astype(bf16))
            lanes = (p % (pool // 2)) * pool * channels
            lanes = slice(lanes, lanes + pool * channels)
            row = jnp.concatenate(row, axis=1)

            @pl.when(at.core == (2 * p) // pool)
            def _(row=row, lanes=lanes):
                mine_ref[:, lanes] = row

            @pl.when(at.core != (2 * p) // pool)
            def _(row=row, lanes=lanes):
                other_ref[:, lanes] = row


def slope_and_back(pre_ref, w_ref, slope_ref, back_ref):
    slope_ref[...] = gelu_slope(pre_ref[...])
    taps = 9
    depth = w_ref.shape[0] // taps
    channels = w_ref.shape[1]
    for tap in range(taps):
        far = taps - 1 - tap
        back_ref[tap * channels : (tap + 1) * channels, :] = (
            w_ref[far * depth : (far + 1) * depth, :].astype(f32).T.astype(bf16)
        )


def cot_rows(place, own_ref, far_ref, up_ref):
    at = place()
    first = at.task == 0
    low_rows = lax.broadcasted_iota(jnp.int32, own_ref.shape[1:], 0) < 4
    for j in range(own_ref.shape[0] // 2):
        chip = at.chip(j // 2, j % 2)
        for c in range(2):
            own = own_ref[2 * chip + c].astype(f32)
            far = far_ref[2 * chip + c].astype(f32)
            low = jnp.where(first, own, far)
            high = jnp.where(first, far, own)
            zero = jnp.where(low_rows, low, pltpu.roll(high, 4, 0))
            one = jnp.where(low_rows, pltpu.roll(low, 4, 0), high)
            here = slice((2 * j + c) * 8, (2 * j + c + 1) * 8)
            up_ref[0, here, :] = jnp.where(first, zero, one)
            up_ref[1, here, :] = jnp.where(first, one, zero)


def stitch_mix(at, ref, t, u):
    row = ref[t]
    return jnp.where(u == 0, row[0:1, :], row[1:2, :])


def core_rows(at, mine, other):
    mine, other = mine.astype(f32), other.astype(f32)
    first = at.core == 0
    return jnp.concatenate(
        [jnp.where(first, mine, other), jnp.where(first, other, mine)], axis=0
    )


def stitch_block(place, mine_ref, c_ref, x_ref, xc_ref, st_ref, out_ref):
    at = place()
    channels = st_ref.shape[2]
    near = stitch_mix(at, st_ref, at.task, at.task)
    far = stitch_mix(at, st_ref, at.task, 1 - at.task)
    for cell in range(out_ref.shape[1] // channels):
        lanes = slice(cell * channels, (cell + 1) * channels)
        own = core_rows(at, mine_ref[:, lanes], c_ref[:, lanes])
        other = core_rows(at, x_ref[:, lanes], xc_ref[:, lanes])
        out_ref[:, lanes] = (near * own + far * other).astype(bf16)


def fc_far(*refs):
    blocks = refs[:-3]
    w_ref, all_ref, out_ref = refs[-3:]
    rows = blocks[0].shape[0]
    for j, block in enumerate(blocks):
        all_ref[j * rows : (j + 1) * rows, :] = block[...]
    out_ref[...] = jnp.dot(all_ref[...], w_ref[...], preferred_element_type=f32)


def fc_own(x_ref, w_ref, out_ref):
    out_ref[...] = jnp.dot(x_ref[...], w_ref[...], preferred_element_type=f32)


def four_rows(task, value, groups):
    rows = lax.broadcasted_iota(jnp.int32, (8, value.shape[1]), 0) < 4
    packed = []
    for g in range(0, groups, 2):
        one, two = value[g * 8 : g * 8 + 8], value[g * 8 + 8 : g * 8 + 16]
        zero = jnp.where(rows, one, pltpu.roll(two, 4, 0))
        last = jnp.where(rows, pltpu.roll(one, 4, 0), two)
        packed.append(jnp.where(task == 0, zero, last))
    return jnp.concatenate(packed, axis=0)


def fc_middle(
    place, own_ref, back_ref, bias_ref, mix_ref, up_ref, d_ref, hidden_ref, pack_ref, sums_ref
):
    at = place()
    first = at.task == 0
    bias = jnp.where(first, bias_ref[0:1, :], bias_ref[1:2, :])
    pre = own_ref[...] + back_ref[...] + bias
    cdf = phi_cdf(pre)
    hidden = pre * cdf
    groups = hidden.shape[0] // 8
    hidden_ref[...] = four_rows(at.task, hidden, groups)
    slope = cdf + pre * ROOT_TWO_PI_INV * jnp.exp(-0.5 * pre * pre)
    mine, other = up_ref[0], up_ref[1]
    d_hidden = stitch_mix(at, mix_ref, at.task, at.task) * mine
    d_hidden += stitch_mix(at, mix_ref, 1 - at.task, at.task) * other
    d_fc = (slope * d_hidden).astype(bf16)
    d_ref[...] = d_fc
    by_mine = jnp.sum(mine * hidden, axis=0, keepdims=True)
    by_other = jnp.sum(other * hidden, axis=0, keepdims=True)
    sums = jnp.concatenate(
        [
            jnp.sum(d_fc.astype(f32), axis=0, keepdims=True),
            jnp.where(first, by_mine, by_other),
            jnp.where(first, by_other, by_mine),
            jnp.zeros((5, by_mine.shape[1]), f32),
        ],
        axis=0,
    )
    high, low = split_high_low(sums)
    sums = jnp.concatenate([high.astype(f32), low.astype(f32)], axis=0)
    sums_ref[...] = sums
    rows = d_ref.shape[0]
    pack_ref[0 : rows // 2, :] = four_rows(1 - at.task, hidden, groups).astype(bf16)
    pack_ref[rows // 2 : rows // 2 + rows, :] = d_fc
    pack_ref[rows // 2 + rows :, :] = sums.astype(bf16)


def folded_lanes(value, lanes):
    return jnp.concatenate(
        [value[:, at : at + lanes] for at in range(0, value.shape[1], lanes)], axis=0
    )


def mix_output(place, own_ref, far_ref, mix_ref, keep_ref, send_ref):
    at = place()
    rows = lax.broadcasted_iota(jnp.int32, (8, own_ref.shape[1]), 0) < 4
    own_all = own_ref[...]
    far_all = far_ref[0 : own_all.shape[0], :].astype(f32)
    sums = []
    for t in range(2):
        sums.append(
            stitch_mix(at, mix_ref, t, at.task) * own_all
            + stitch_mix(at, mix_ref, t, 1 - at.task) * far_all
        )
    for kz in range(keep_ref.shape[0]):
        for ky, out in enumerate((keep_ref, send_ref)):
            here = slice((2 * kz + ky) * 8, (2 * kz + ky) * 8 + 8)
            zero, one = sums[0][here], sums[1][here]
            value = jnp.concatenate(
                [
                    jnp.where(rows, zero, pltpu.roll(one, 4, 0)),
                    jnp.where(rows, pltpu.roll(zero, 4, 0), one),
                ],
                axis=0,
            )
            out[kz] = folded_lanes(value, out.shape[2]).astype(bf16)


def output_finish(place, keep_ref, came_ref, sums_ref, far_ref, out_ref, bias_ref, st_ref, all_ref):
    at = place()
    units = keep_ref.shape[2]
    folds = units // came_ref.shape[1]
    first_row = came_ref.shape[0] - 8 * folds * keep_ref.shape[0]
    came_all = came_ref[first_row:, :].astype(f32)
    for j in range(keep_ref.shape[0]):
        chip = at.chip(j // 2, j % 2)
        mine = pl.ds(pl.multiple_of((2 * chip + at.core) * units, units), units)
        all_ref[:, mine] = keep_ref[j]
        other = pl.ds(pl.multiple_of((2 * chip + 1 - at.core) * units, units), units)
        rows = [8 * (folds * j + f) for f in range(folds)]
        all_ref[:, other] = jnp.concatenate([came_all[i : i + 8] for i in rows], axis=1)
    for i in range(4):
        out_ref[i] = jnp.concatenate(
            [all_ref[i : i + 1, :], all_ref[4 + i : 5 + i, :]], axis=0
        ).astype(bf16)
    first = at.task == 0
    own, far = sums_ref[...], far_ref[far_ref.shape[0] - 16 :, :].astype(f32)
    own, far = own[0:8] + own[8:16], far[0:8] + far[8:16]
    zero, one = jnp.where(first, own, far), jnp.where(first, far, own)
    bias_ref[0:1, :] = zero[0:1]
    bias_ref[1:2, :] = one[0:1]
    for t in range(2):
        st_ref[t] = jnp.concatenate([zero[1 + t : 2 + t], one[1 + t : 2 + t]], axis=0)


def fc_back(d_ref, far_ref, w_ref, wf_ref, *outs):
    chips = len(outs)
    rows = outs[0].shape[0]
    contract = (((1,), (1,)), ((), ()))
    total = lax.dot_general(d_ref[...], w_ref[...], contract, preferred_element_type=f32)
    total += lax.dot_general(far_ref[...], wf_ref[...], contract, preferred_element_type=f32)
    for j, out in enumerate(outs):
        out[...] = total[j * rows : (j + 1) * rows, :].astype(out.dtype)


def add_rows(keep_ref, got_ref, *outs):
    total = keep_ref[...] + got_ref[...].astype(f32)
    for out in outs:
        out[...] = total.astype(out.dtype)


def block_total(place, keep_ref, *refs):
    at = place()
    total_ref, mine_ref, mine_low_ref, other_ref = refs[-4:]
    total = keep_ref[...]
    for ref in refs[:-4]:
        total = total + ref[...].astype(f32)
    total_ref[...] = total
    images = mine_ref.shape[0]
    low, high = total[:images], total[images:]
    mine = jnp.where(at.core == 0, low, high)
    mine_ref[...] = mine
    mine_low_ref[...] = mine.astype(bf16)
    other_ref[...] = jnp.where(at.core == 0, high, low).astype(bf16)


def stitch_terms(place, total_ref, mine_ref, c_ref, x_ref, xc_ref, out_ref):
    at = place()
    channels = out_ref.shape[1]
    own = far = None
    for cell in range(total_ref.shape[1] // channels):
        lanes = slice(cell * channels, (cell + 1) * channels)
        grad = total_ref[:, lanes]
        one = grad * core_rows(at, mine_ref[:, lanes], c_ref[:, lanes])
        two = grad * core_rows(at, x_ref[:, lanes], xc_ref[:, lanes])
        own = one if own is None else own + one
        far = two if far is None else far + two
    out_ref[...] = jnp.concatenate(
        [
            jnp.sum(own, axis=0, keepdims=True),
            jnp.sum(far, axis=0, keepdims=True),
            jnp.zeros((6, channels), f32),
        ],
        axis=0,
    )


def conv_slope(place, side, pool, images, *refs):
    (g_ref, mine_ref, c_ref, x_ref, xc_ref, st_ref, slope_ref, q_ref) = refs[:8]
    d_ref, bias_ref = refs[8:]
    at = place()
    slab = images * WIDTH
    channels = slope_ref.shape[1]
    group = g_ref[...]

    near = stitch_mix(at, st_ref, at.task, at.task)
    far = stitch_mix(at, st_ref, 1 - at.task, at.task)
    spread = []
    for p in range(pool):
        mine_here = at.core == (2 * p) // pool
        cells = []
        for q in range(pool):
            lanes = ((p % (pool // 2)) * pool + q) * channels
            lanes = slice(lanes, lanes + channels)
            kept = jnp.where(max(p, q) + group < pool, 1.0 / 9.0, 0.0)
            one = near * mine_ref[:, lanes] + far * x_ref[:, lanes].astype(f32)
            two = near * c_ref[:, lanes].astype(f32) + far * xc_ref[:, lanes].astype(f32)
            cells.append(jnp.where(mine_here, one, two) * kept)
        spread.append(window_sum(q_ref, jnp.concatenate(cells, axis=0)))
    total = jnp.zeros((8, channels), f32)
    for y in range(side):
        act = None
        for p in range(pool):
            if 2 * p <= y <= 2 * p + 2:
                act = spread[p] if act is None else act + spread[p]
        grad = (act * slope_ref[y * slab : (y + 1) * slab, :]).astype(bf16)
        d_ref[y * slab : (y + 1) * slab, :] = grad
        total = total + jnp.sum(grad.astype(f32).reshape(-1, 8, channels), axis=0)
    bias_ref[...] = jnp.sum(total, axis=0, keepdims=True)


def kernel_grad(place, slab, xt_ref, d_ref, bias_ref, st_ref, *refs):
    keep_ref, send_ref, scr_ref = refs
    at = place()
    depth = xt_ref.shape[0]
    chips, full, half = keep_ref.shape
    rows = full - EXTRA
    count = d_ref.shape[0]
    for ky in range(3):
        scr_ref[ky * depth : (ky + 1) * depth, :] = jnp.dot(
            xt_ref[:, ky * slab : ky * slab + count], d_ref[...], preferred_element_type=f32
        )
    small = jnp.concatenate([bias_ref[...], st_ref[0:2, :]], axis=0)
    small = jnp.concatenate(
        [small[:, :half], jnp.zeros((1, half), f32), small[:, half:], jnp.zeros((1, half), f32)],
        axis=0,
    )
    high, low = split_high_low(small)
    extra = jnp.concatenate([high.astype(f32), low.astype(f32)], axis=0)
    here = pl.ds(pl.multiple_of(at.core * half, half), half)
    there = pl.ds(pl.multiple_of((1 - at.core) * half, half), half)
    for j in range(chips):
        to = pl.ds(pl.multiple_of(at.chip(j // 2, j % 2) * rows, 16), rows)
        keep_ref[j, 0:rows, :] = scr_ref[to, here]
        send_ref[j, 0:rows, :] = scr_ref[to, there].astype(bf16)
        keep_ref[j, rows:full, :] = extra
        send_ref[j, rows:full, :] = extra.astype(bf16)


def folded(extra):
    value = extra[:8] + extra[8:]
    high, low = split_high_low(value)
    return jnp.concatenate([high.astype(f32), low.astype(f32)], axis=0)


def sum_pieces(keep_ref, got_ref, output_ref, *outs):
    full = keep_ref.shape[1]
    rows = full - EXTRA
    for kz, out in enumerate(outs):
        total = keep_ref[2 * kz + 1] + got_ref[2 * kz + 1].astype(f32)
        out[0:rows, :] = total[:rows].astype(bf16)
        out[rows:full, :] = folded(total[rows:]).astype(bf16)
        out[full:, :] = output_ref[kz]


def sum_three(k, keep_ref, got_ref, came_ref, output_ref, out_ref):
    full = keep_ref.shape[1]
    rows = full - EXTRA
    more = output_ref.shape[1]
    total = keep_ref[2 * k] + got_ref[2 * k].astype(f32)
    total = jnp.concatenate([total[:rows], folded(total[rows:])], axis=0)
    total = total + came_ref[0:full, :].astype(f32)
    out_ref[0:rows, :] = total[:rows].astype(out_ref.dtype)
    out_ref[rows:full, :] = folded(total[rows:]).astype(out_ref.dtype)
    out_ref[full : full + more, :] = output_ref[k].astype(out_ref.dtype)
    out_ref[full + more :, :] = came_ref[full:, :].astype(out_ref.dtype)


def kernel_total(place, *refs):
    parts, (mine_ref, other_ref, pack_ref, keep_ref, scr_ref, small_ref) = refs[:-6], refs[-6:]
    at = place()
    rows, half = scr_ref.shape
    full = rows + EXTRA
    total = None
    riders = []
    for k, part in enumerate(parts):
        value = part[...].astype(f32)
        total = value[:rows] if total is None else total + value[:rows]
        small_ref[k] = value[rows : rows + 8] + value[rows + 8 : full]
        more = (value.shape[0] - full) // 2
        for y in range(2):
            piece = value[full + more * y : full + more * (y + 1)]
            low = [piece[i : i + 8] for i in range(0, more, 16)]
            high = [piece[i + 8 : i + 16] for i in range(0, more, 16)]
            zero = at.core == 0
            keep_ref[2 * k + y] = jnp.concatenate(
                [jnp.where(zero, a, b) for a, b in zip(low, high, strict=True)], axis=1
            )
            riders += [jnp.where(zero, b, a) for a, b in zip(low, high, strict=True)]
    scr_ref[...] = total
    small = None
    for z in range(len(parts)):
        piece = small_ref[lax.rem(at.z + (len(parts) - z), len(parts))]
        small = piece if small is None else small + piece
    high, low = split_high_low(small)
    tail = jnp.zeros((mine_ref.shape[0] - rows // 2 - EXTRA, half), f32)
    for ref, c in ((mine_ref, at.core), (other_ref, 1 - at.core)):
        piece = scr_ref[pl.ds(pl.multiple_of(c * (rows // 2), 8), rows // 2), :]
        value = [high.astype(f32), low.astype(f32), piece] + [tail] * (tail.shape[0] > 0)
        ref[...] = jnp.concatenate(value, axis=0).astype(bf16)
    pack_ref[0 : other_ref.shape[0], :] = other_ref[...]
    pack_ref[other_ref.shape[0] :, :] = jnp.concatenate(riders, axis=0).astype(bf16)


def kernel_finish(place, mine_ref, c_ref, x_ref, xc_ref, grad_ref, bias_ref, stitch_ref):
    at = place()
    rows = grad_ref.shape[1]
    half = grad_ref.shape[2] // 2
    first = at.task == 0
    low_core = at.core == 0

    def lanes(one, two):
        return jnp.concatenate(
            [jnp.where(low_core, one, two), jnp.where(low_core, two, one)], axis=1
        )

    own = lanes(mine_ref[...].astype(f32), c_ref[0 : mine_ref.shape[0], :].astype(f32))
    far = lanes(x_ref[...].astype(f32), xc_ref[...].astype(f32))
    grad_ref[0] = jnp.where(first, own, far)[EXTRA : EXTRA + rows, :]
    grad_ref[1] = jnp.where(first, far, own)[EXTRA : EXTRA + rows, :]

    def small(ref):
        value = ref[...].astype(f32)
        value = value[0:8] + value[8:16]
        return jnp.concatenate([value[0:4], value[4:8]], axis=1)

    own, far = small(mine_ref), small(x_ref)
    bias_ref[0:1, :] = jnp.where(first, own, far)[0:1, :]
    bias_ref[1:2, :] = jnp.where(first, far, own)[0:1, :]
    own_pair = jnp.where(first, own[1:3], jnp.concatenate([own[2:3], own[1:2]], axis=0))
    far_pair = jnp.where(first, jnp.concatenate([far[2:3], far[1:2]], axis=0), far[1:3])
    stitch_ref[0] = jnp.where(first, own_pair, far_pair)
    stitch_ref[1] = jnp.where(first, far_pair, own_pair)


def picture_grad(place, far, side, slab, d_ref, w_ref, out_ref, pad_ref):
    at = place()
    channels = d_ref.shape[1]
    depth = 3 * channels
    block = slab // 2
    first = (1 - at.task if far else at.task) * block
    blank = jnp.zeros((block, depth), bf16)
    pad_ref[0:block, :] = blank
    pad_ref[(side + 1) * block :, :] = blank
    for y in range(side):
        here = pl.ds(pl.multiple_of(y * slab + first, 16), block)
        wide = d_ref[here, :].astype(f32)
        rows = slice((y + 1) * block, (y + 2) * block)
        pad_ref[rows, 0:channels] = pltpu.roll(wide, 1, 0).astype(bf16)
        pad_ref[rows, channels : 2 * channels] = wide.astype(bf16)
        pad_ref[rows, 2 * channels :] = pltpu.roll(wide, block - 1, 0).astype(bf16)
    for start in range(0, side, 7):
        rows = min(7, side - start)
        total = None
        for ky in range(3):
            part = jnp.dot(
                pad_ref[(start + ky) * block : (start + ky + rows) * block, :],
                w_ref[ky * depth : (ky + 1) * depth, :],
                preferred_element_type=f32,
            )
            total = part if total is None else total + part
        for row in range(rows):
            value = total[row * block : (row + 1) * block].astype(bf16)
            out_ref[start + row] = value.reshape(out_ref.shape[1:])


def picture_finish(place, g_ref, own_ref, far_ref, out_ref):
    at = place()
    side, few, _, depth = own_ref.shape
    columns = lax.broadcasted_iota(jnp.int32, (side, depth), 0)
    for n in range(few):
        limit = side - 2 * g_ref[n]
        for y in range(side):
            reach = jnp.where(y < limit, limit, 0)
            mask = jnp.where(columns < reach, 1.0, 0.0).astype(bf16)
            out_ref[n, at.task, y] = own_ref[y, n, 0:side, :] * mask
            out_ref[n, 1 - at.task, y] = far_ref[y, n, 0:side, :] * mask


def fc_grad(place, own_ref, oc_ref, x_ref, xc_ref, d_ref, dx_ref, out_ref):
    at = place()
    same = at.core == at.task
    own = jnp.where(same, own_ref[...], oc_ref[...])
    far = jnp.where(same, x_ref[...], xc_ref[...])
    contract = (((0,), (0,)), ((), ()))
    out_ref[at.task] = lax.dot_general(own, d_ref[...], contract, preferred_element_type=f32)
    rows = d_ref.shape[0]
    d_far = dx_ref[rows // 2 : rows // 2 + rows, :]
    out_ref[1 - at.task] = lax.dot_general(far, d_far, contract, preferred_element_type=f32)


def on_device(pairs, planes, *operands):
    (
        conv_input,
        group,
        conv_weight,
        conv_bias,
        stitch_pool,
        fc_weight,
        fc_bias,
        stitch_fc,
        cotangent,
    ) = operands
    chips = 2 * planes
    place = functools.partial(Place, pairs, planes)
    task = Place(pairs, planes).task
    few = conv_input.shape[0]
    images = 2 * few
    side = conv_input.shape[2]
    channels_in = conv_input.shape[4]
    channels = conv_bias.shape[1]
    pool = (side - 3) // 2 + 1
    units = fc_bias.shape[1]
    features = pool * pool * channels
    part = features // 2
    slab = images * WIDTH
    own_rows = conv_weight.shape[1]
    chip_rows = 2 * own_rows
    half = channels // 2

    def links(where):
        pairs_of = []
        for b in range(2 * pairs):
            for m in range(4 * planes):
                to = where(b, m // 4, (m // 2) % 2, m % 2)
                if to is not None:
                    far_b, z, y, c = to
                    far_m = ((z % planes) * 2 + y) * 2 + c
                    pairs_of.append((b * 4 * planes + m, far_b * 4 * planes + far_m))
        return pairs_of

    def move(value, dx=0, dz=0, dy=0, dc=0):
        where = lambda b, z, y, c: ((b + pairs * dx) % (2 * pairs), z + dz, y ^ dy, c ^ dc)
        return lax.ppermute(value, BOTH, links(where))

    def pick(array, index, axis=0):
        return lax.dynamic_index_in_dim(array, index, axis, keepdims=False)

    def ordered(flag, mine, other, axis=0):
        return jnp.where(
            flag == 0,
            jnp.concatenate([mine, other], axis=axis),
            jnp.concatenate([other, mine], axis=axis),
        )

    def after(value, *others):
        return lax.optimization_barrier((value, *others))[0]

    shifts = []
    for near in range(1, planes // 2 + 1):
        shifts.extend(sorted({near, planes - near}))

    def gather_chips(block):
        rows = [[block, move(block, dy=1)]] + [None] * (planes - 1)
        here = {k: move(block, dz=k) for k in shifts}
        for k in shifts:
            rows[k] = [here[k], move(here[k], dy=1)]
        return [piece for pair in rows for piece in pair]

    weight_mine, weight_other = call(
        functools.partial(split_weights, place),
        (shape_of((own_rows, half), bf16), shape_of((own_rows, half), bf16)),
        (conv_weight,),
    )
    weight_block = call(
        functools.partial(join_cores, place),
        shape_of((chip_rows, half), bf16),
        (weight_mine, move(weight_other, dc=1)),
    )
    wide = (side, few, WIDTH, channels_in)
    picture_own, picture_send, cot_send = call(
        functools.partial(split_inputs, place),
        (
            shape_of(wide, bf16),
            shape_of(wide, bf16),
            shape_of((4 * planes, images, units), bf16),
        ),
        (group, conv_input, cotangent),
        scalars=1,
    )
    picture_far = move(picture_send, dx=1)
    weight_blocks = gather_chips(after(weight_block, picture_send))
    weight_far = [move(block, dc=1) for block in weight_blocks]
    stacked, stacked_t, groups = call(
        functools.partial(widen, place, side),
        (
            shape_of(((side + 2) * slab, 3 * channels_in), bf16),
            shape_of((3 * channels_in, (side + 2) * slab), bf16),
            shape_of((images, channels), f32),
        ),
        (picture_own, picture_far),
    )

    cot_send = after(cot_send, weight_blocks[1])
    cot_own = lax.all_to_all(cot_send, "mp", split_axis=0, concat_axis=0, tiled=True)
    cot_far = move(after(cot_own, picture_far), dx=1)

    window = np.zeros((pool * images, slab), np.float32)
    for q in range(pool):
        for n in range(images):
            window[q * images + n, n * WIDTH + 2 * q : n * WIDTH + 2 * q + 3] = 1.0
    window_t = jnp.asarray(window.T, bf16)
    window = jnp.asarray(window, bf16)
    stacked = after(stacked, stacked_t)
    conv_pre, pooled_mine, pooled_other, kernel = call(
        functools.partial(conv_forward, place, side, pool, images),
        (
            shape_of((side * slab, channels), f32),
            shape_of((images, part), bf16),
            shape_of((images, part), bf16),
            shape_of((chips * chip_rows, channels), bf16),
        ),
        (groups, stacked, conv_bias, window, *weight_blocks, *weight_far),
    )

    pooled_mine = after(pooled_mine, cot_far)
    pooled_x = move(pooled_mine, dx=1)
    pooled_xc = move(pooled_other, dx=1, dc=1)
    pooled_c = move(pooled_other, dc=1)
    pooled = (pooled_mine, pooled_c, pooled_x, pooled_xc)
    piece = (2 * images, part)
    rows_all = chips * 2 * images
    blocks = gather_chips(
        call(functools.partial(stitch_block, place), shape_of(piece, bf16), (*pooled, stitch_pool))
    )

    up = call(
        functools.partial(cot_rows, place),
        shape_of((2, rows_all, units), f32),
        (cot_own, after(cot_far, *blocks[2::2])),
    )

    fc_mine, fc_other = call(
        functools.partial(split_fc, place),
        (shape_of((part, units), bf16), shape_of((part, units), bf16)),
        (after(fc_weight, *blocks[2::2]),),
        (DMA((2,)),),
        blocks=None,
        any_first=True,
    )
    fc_other = move(fc_other, dc=1)

    slope, kernel_back = call(
        slope_and_back,
        (
            shape_of(conv_pre.shape, f32),
            shape_of((9 * channels, channels_in), bf16),
        ),
        (after(conv_pre, *blocks[2::2]), kernel),
    )

    gathered, far_term = call(
        fc_far,
        (shape_of((rows_all, part), bf16), shape_of((rows_all, units), f32)),
        (*blocks, after(fc_other, slope, kernel_back, up)),
    )
    far_back = move(far_term, dc=1)
    own_term = call(fc_own, shape_of((rows_all, units), f32), (gathered, fc_mine))
    d_fc, hidden, x_pack, fc_sums = call(
        functools.partial(fc_middle, place),
        (
            shape_of((rows_all, units), bf16),
            shape_of((rows_all // 2, units), f32),
            shape_of((rows_all // 2 + rows_all + 16, units), bf16),
            shape_of((16, units), f32),
        ),
        (own_term, far_back, fc_bias, stitch_fc, up),
    )
    d_fc_far = move(d_fc, dc=1)
    outs = call(
        fc_back,
        tuple(shape_of(piece, bf16 if j % 2 else f32) for j in range(chips)),
        (d_fc, d_fc_far, fc_mine, fc_other),
    )
    kept, sent = outs[0::2], outs[1::2]

    order = shifts[::-1] + [0]
    arrived = {k: move(sent[k], dy=1) for k in order}
    passed = {}
    for k in order[:-1]:
        low = call(add_rows, (shape_of(piece, bf16),), (kept[k], arrived[k]))[0]
        passed[k] = move(low, dz=-k)
    x_came = move(after(x_pack, *arrived.values()), dx=1)
    cross = lambda b, z, y, c: ((b + pairs) % (2 * pairs), z, y, c) if c != b // pairs else None
    features_x = lax.ppermute(gathered, BOTH, links(cross))
    features_c = move(after(gathered, *arrived.values()), dc=1)
    d_total, d_mine, d_mine_low, d_other = call(
        functools.partial(block_total, place),
        (
            shape_of(piece, f32),
            shape_of((images, part), f32),
            shape_of((images, part), bf16),
            shape_of((images, part), bf16),
        ),
        (after(kept[0], features_x, features_c), arrived[0], *[passed[k] for k in order[:-1]]),
    )

    d_x = move(d_mine_low, dx=1)
    d_xc = move(d_other, dx=1, dc=1)
    d_c = move(d_other, dc=1)
    ride = 2 * images * units // half
    riding = shape_of((planes, ride, half), bf16)
    out_keep, out_send = call(
        functools.partial(mix_output, place),
        (riding, riding),
        (hidden, after(x_came, d_xc), stitch_fc),
    )
    stitch_sums = call(
        functools.partial(stitch_terms, place),
        shape_of((8, channels), f32),
        (after(d_total, d_other), *pooled),
    )
    d_conv, d_bias = call(
        functools.partial(conv_slope, place, side, pool, images),
        (shape_of((side * slab, channels), bf16), shape_of((1, channels), f32)),
        (groups, d_mine, d_c, d_x, d_xc, stitch_pool, slope, window_t),
    )

    full = chip_rows + EXTRA
    stack = (chips, full, half)
    keep, send = call(
        functools.partial(kernel_grad, place, slab),
        (shape_of(stack, f32), shape_of(stack, bf16)),
        (stacked_t, after(d_conv, out_send), d_bias, stitch_sums),
        (pltpu.VMEM((chips * chip_rows, channels), f32),),
    )
    got = move(send, dc=1)
    thin = (side, few, WIDTH, channels_in)
    pad = (pltpu.VMEM(((side + 2) * slab // 2, 3 * channels), bf16),)
    back_send = call(
        functools.partial(picture_grad, place, True, side, slab),
        shape_of(thin, bf16),
        (after(d_conv, send), kernel_back),
        pad,
    )
    flat = (full + ride, half)
    sent = call(
        sum_pieces,
        tuple(shape_of(flat, bf16) for _ in range(planes)),
        (keep, after(got, back_send), out_send),
    )
    arrived = {k: move(sent[k], dy=1) for k in order}
    parts = {}
    for k in order:
        parts[k] = call(
            functools.partial(sum_three, k),
            shape_of((full + 2 * ride, half), bf16 if k else f32),
            (keep, got, arrived[k], out_keep),
        )
        if k:
            parts[k] = move(parts[k], dz=-k)
    late = arrived[order[0]]

    back_far = move(back_send, dx=1)
    back_own = call(
        functools.partial(picture_grad, place, False, side, slab),
        shape_of(thin, bf16),
        (after(d_conv, *[arrived[k] for k in order]), kernel_back),
        pad,
    )
    input_grad = call(
        functools.partial(picture_finish, place),
        shape_of(conv_input.shape, bf16),
        (group, back_own, back_far),
        scalars=1,
    )

    def both(own, axis=0):
        own = jnp.expand_dims(own, axis)
        return ordered(task, own, jnp.zeros_like(own), axis=axis)

    d_fc_last = after(d_fc, parts[order[0]])
    features_xc = move(after(features_x, late), dc=1)
    steps = 3
    wide_spec = pl.BlockSpec((rows_all, part // steps), lambda i: (0, i))
    whole_spec = [pl.BlockSpec(a.shape, lambda i: (0, 0)) for a in (d_fc, x_came)]
    fc_weight_grad = pl.pallas_call(
        functools.partial(fc_grad, place),
        out_shape=shape_of((2, part, units), f32),
        grid=(steps,),
        in_specs=[wide_spec] * 4 + whole_spec,
        out_specs=pl.BlockSpec((2, part // steps, units), lambda i: (0, i, 0)),
        cost_estimate=cost(fc_grad),
        compiler_params=pltpu.CompilerParams(vmem_limit_bytes=24 * MIB),
    )(gathered, features_c, features_x, features_xc, d_fc_last, x_came)
    tall = -(-(own_rows + EXTRA) // 16) * 16
    k_mine, k_other, k_pack, out_own = call(
        functools.partial(kernel_total, place),
        (
            shape_of((tall, half), bf16),
            shape_of((tall, half), bf16),
            shape_of((tall + chips * ride // 2, half), bf16),
            shape_of((chips, images, units), f32),
        ),
        (after(parts[0], fc_weight_grad, back_own), *[parts[planes - k] for k in range(1, planes)]),
        (pltpu.VMEM((chip_rows, half), f32), pltpu.VMEM((planes, 8, half), f32)),
    )
    k_x = move(k_mine, dx=1)
    k_xc = move(k_other, dx=1, dc=1)
    k_c = move(k_pack, dc=1)
    output, fc_bias_grad, stitch_fc_grad = call(
        functools.partial(output_finish, place),
        (
            shape_of(cotangent.shape, bf16),
            shape_of((2, units), f32),
            shape_of((2, 2, units), f32),
        ),
        (out_own, k_c, fc_sums, x_came),
        (pltpu.VMEM((images, cotangent.shape[2]), f32),),
    )
    conv_weight_grad, conv_bias_grad, stitch_pool_grad = call(
        functools.partial(kernel_finish, place),
        (
            shape_of((2, own_rows, channels), f32),
            shape_of((2, channels), f32),
            shape_of((2, 2, channels), f32),
        ),
        (k_mine, k_c, k_x, k_xc),
    )

    if pairs > 1:
        fc_weight_grad = lax.psum_scatter(
            ordered(task, fc_weight_grad, jnp.zeros_like(fc_weight_grad), axis=1),
            "batch",
            scatter_dimension=1,
            tiled=True,
        )
        conv_weight_grad, conv_bias_grad, stitch_pool_grad, fc_bias_grad = lax.psum(
            tuple(
                both(pick(value, task))
                for value in (conv_weight_grad, conv_bias_grad, stitch_pool_grad, fc_bias_grad)
            ),
            "batch",
        )
        stitch_fc_grad = lax.psum(both(pick(stitch_fc_grad, task, 1), axis=1), "batch")
    return (
        output,
        input_grad,
        conv_weight_grad,
        conv_bias_grad,
        stitch_pool_grad,
        fc_weight_grad,
        fc_bias_grad,
        stitch_fc_grad,
    )


def solution(mesh):
    pairs = mesh.shape["batch"] // 2
    planes = mesh.shape["mp"] // 4
    in_specs = (
        P(BOTH, None, None, None, None),
        P(BOTH),
        P(None, "mp", None),
        P(),
        P(),
        P(None, None, "mp"),
        P(None, "mp"),
        P(None, None, "mp"),
        P(BOTH, None, None),
    )
    out_specs = (
        P(BOTH, None, None),
        P(BOTH, None, None, None, None),
        P(None, "mp", None),
        P(),
        P(),
        P(None, "batch", "mp"),
        P(None, "mp"),
        P(None, None, "mp"),
    )
    return jax.shard_map(
        functools.partial(on_device, pairs, planes),
        mesh=mesh,
        in_specs=in_specs,
        out_specs=out_specs,
        check_vma=False,
    )
```

time: 204 us -> 169 us (0.83)
  local copies, waits for them, and re-layouts: 41.8 us -> 3.29 us
  waiting for transfers between devices: 51.1 us -> 72.6 us
  Pallas kernels: 47.8 us -> 32.5 us
    unnamed x110 -> x26, local copies, waits for them, and re-layouts: 30.2 us -> 3.29 us
    ppermute x60 -> x56, waiting for transfers between devices: 51.1 us -> 71.5 us  [move(): return lax.ppermute(value, BOTH, links(where))]
    pallas_call x26 -> x32, Pallas kernels: 38.7 us -> 27.7 us  [call(): pl.pallas_call(body, out_shape=out_shape, **steps, in_specs=blocks or [SM...]
    pallas_call x1, Pallas kernels: 9.03 us -> 4.8 us  [on_device(): pl.pallas_call(functools.partial(fc_grad, place), out_shape=shape_of((2,...]
    squeeze x2 -> x0, local copies, waits for them, and re-layouts: 4.11 us -> none  [the longest x1 4.1 us: pick(): return lax.dynamic_index_in_dim(array, index, axis, keepdims=False)]
    ppermute x60 -> x56, starting transfers between devices: 49.3 us -> 53.3 us  [move(): return lax.ppermute(value, BOTH, links(where))]
    all_to_all x1 -> x0, starting transfers between devices: 3.5 us -> none  [on_device(): mixed = lax.all_to_all(mixed, 'mp', split_axis=0, concat_axis=0, tiled=True)]
    reshape x3 -> x0, local copies, waits for them, and re-layouts: 2.22 us -> none  [the longest x1 0.87 us: on_device(): output = output.reshape(cotangent.shape)]
  transfers between devices with their start and end apart: 63 -> 58, of which waited for: 22 -> 31; matrix products, arithmetic and copies ran while one was open for 8% -> 1% of each run, Pallas kernels for 16% -> 14%
where the time goes in v1:
time: 169 us
  waiting for transfers between devices  72.6 us (43%)
  starting transfers between devices  59.5 us (35%)
  Pallas kernels  32.5 us (19%)
  local copies, waits for them, and re-layouts  3.29 us (2%)
    ppermute x56, waiting for transfers between devices, move(): return lax.ppermute(value, BOTH, links(where))  71.5 us
    ppermute x56, starting transfers between devices, move(): return lax.ppermute(value, BOTH, links(where))  53.3 us
    pallas_call x32, Pallas kernels, call(): pl.pallas_call(body, out_shape=out_shape, **steps, in_specs=blocks or [SM...  27.7 us
    all_to_all x1, starting transfers between devices, on_device(): lax.all_to_all(cot_send, 'mp', split_axis=0, concat_axis=0, tiled=True)  4.93 us
    pallas_call x1, Pallas kernels, on_device(): pl.pallas_call(functools.partial(fc_grad, place), out_shape=shape_of((2,...  4.8 us
  transfers between devices with their start and end apart: 58, of which 31 were waited for; matrix products, arithmetic and copies ran while one was open for 1% of the time, Pallas kernels for 14%

profile of v1, /device:TPU:0, one launch (start us, length us, event | category | flops | bytes accessed | tf_op | source)
XLA Modules:
  0.0 169.0 jit_solution(1264206460066121640)
XLA Ops:
  3.7 2.9 %collective-permute-start = (bf16[13,4,16,384]{3,2,1,0:T(8,128)(2,1)S(1)}, bf16[13,4,16,384]{3,2,1,0:T(8,128)(2,1)S(1)}, u32[]{:S(2)}, u32[]{:S(2)}) collective-permute-start(bf16[13,4,16,384]{3,2,1,0:T(8,128)(2,1)S(1)} %get-tuple-element.84), channel_id=1, source_target_pairs={{0,16},{1,17},{2,18},{3,19},{4,20},{5,21},{6,22},{7,23},{8,24},{9,... | collective-permute-start | bytes 1916936 | tf_op jit(solution)/shard_map/ppermute | solution.py:753
  9.6 3.6 %collective-permute-start.7 = (bf16[432,128]{1,0:T(8,128)(2,1)S(1)}, bf16[432,128]{1,0:T(8,128)(2,1)S(1)}, u32[]{:S(2)}, u32[]{:S(2)}) collective-permute-start(bf16[432,128]{1,0:T(8,128)(2,1)S(1)} %shard_map.173.refs_4_), channel_id=1, source_target_pairs={{0,12},{1,13},{2,14},{3,15},{4,0},{5,1},{6,2},{7,3},{8,4},{9,5},{1... | collective-permute-start | bytes 331784 | tf_op jit(solution)/shard_map/ppermute | solution.py:753
  14.7 4.9 %all-to-all-start = ((bf16[16,8,256]{2,1,0:T(8,128)(2,1)}), bf16[16,8,256]{2,1,0:T(8,128)(2,1)S(1)}, u32[]{:S(2)}, u32[]{:S(2)}) async-start(bf16[16,8,256]{2,1,0:T(8,128)(2,1)} %get-tuple-element.94), calls=%async_computation | async-start | bytes 131072 | tf_op jit(solution)/shard_map/all_to_all | solution.py:814
  34.0 7.7 %shard_map.174 = (f32[1664,256]{1,0:T(8,128)S(1)}, bf16[8,4608]{1,0:T(8,128)(2,1)S(1)}, bf16[8,4608]{1,0:T(8,128)(2,1)S(1)}, bf16[3456,256]{1,0:T(8,128)(2,1)S(1)}) custom-call(f32[8,256]{1,0:T(8,128)S(1)} %get-tuple-element.86.refs_0_, bf16[1920,1152]{1,0:T(8,128)(2,1)S(1)} %get-tuple-element.88.refs_1_, f32[2,256]{1,0:T(2,128)S(1)} %copy-done.4, ...), custom_call_target="tpu_custom_call" | custom-call | flops 8249999872 | bytes 1 | tf_op jit(solution)/shard_map/pallas_call | solution.py:79
  48.0 2.9 %collective-permute-start.26 = (bf16[16,4608]{1,0:T(8,128)(2,1)S(1)}, bf16[16,4608]{1,0:T(8,128)(2,1)S(1)}, u32[]{:S(2)}, u32[]{:S(2)}) collective-permute-start(bf16[16,4608]{1,0:T(8,128)(2,1)S(1)} %shard_map.175.refs_0_), channel_id=1, source_target_pairs={{0,12},{1,13},{2,14},{3,15},{4,0},{5,1},{6,2},{7,3},{8,4},{9,5},{1... | collective-permute-start | bytes 442376 | tf_op jit(solution)/shard_map/ppermute | solution.py:753
  52.8 2.3 %collective-permute-done.26.refs_6_ = bf16[16,4608]{1,0:T(8,128)(2,1)S(1)} collective-permute-done((bf16[16,4608]{1,0:T(8,128)(2,1)S(1)}, bf16[16,4608]{1,0:T(8,128)(2,1)S(1)}, u32[]{:S(2)}, u32[]{:S(2)}) %collective-permute-start.26) | collective-permute-done | bytes 147488 | tf_op jit(solution)/shard_map/ppermute | solution.py:753
  55.2 8.7 %collective-permute-done.24.refs_4_ = bf16[16,4608]{1,0:T(8,128)(2,1)S(1)} collective-permute-done((bf16[16,4608]{1,0:T(8,128)(2,1)S(1)}, bf16[16,4608]{1,0:T(8,128)(2,1)S(1)}, u32[]{:S(2)}, u32[]{:S(2)}) %collective-permute-start.24) | collective-permute-done | bytes 147488 | tf_op jit(solution)/shard_map/ppermute | solution.py:753
  71.0 3.2 %collective-permute-done.27.refs_7_ = bf16[16,4608]{1,0:T(8,128)(2,1)S(1)} collective-permute-done((bf16[16,4608]{1,0:T(8,128)(2,1)S(1)}, bf16[16,4608]{1,0:T(8,128)(2,1)S(1)}, u32[]{:S(2)}, u32[]{:S(2)}) %collective-permute-start.27) | collective-permute-done | bytes 147488 | tf_op jit(solution)/shard_map/ppermute | solution.py:753
  74.2 3.2 %collective-permute-done.25.refs_5_ = bf16[16,4608]{1,0:T(8,128)(2,1)S(1)} collective-permute-done((bf16[16,4608]{1,0:T(8,128)(2,1)S(1)}, bf16[16,4608]{1,0:T(8,128)(2,1)S(1)}, u32[]{:S(2)}, u32[]{:S(2)}) %collective-permute-start.25) | collective-permute-done | bytes 147488 | tf_op jit(solution)/shard_map/ppermute | solution.py:753
  77.4 2.7 %collective-permute-done.23.refs_3_ = bf16[16,4608]{1,0:T(8,128)(2,1)S(1)} collective-permute-done((bf16[16,4608]{1,0:T(8,128)(2,1)S(1)}, bf16[16,4608]{1,0:T(8,128)(2,1)S(1)}, u32[]{:S(2)}, u32[]{:S(2)}) %collective-permute-start.23) | collective-permute-done | bytes 147488 | tf_op jit(solution)/shard_map/ppermute | solution.py:753
  91.8 3.2 %collective-permute-done.33.got_ref = bf16[16,4608]{1,0:T(8,128)(2,1)S(1)} collective-permute-done((bf16[16,4608]{1,0:T(8,128)(2,1)S(1)}, bf16[16,4608]{1,0:T(8,128)(2,1)S(1)}, u32[]{:S(2)}, u32[]{:S(2)}) %collective-permute-start.33) | collective-permute-done | bytes 147488 | tf_op jit(solution)/shard_map/ppermute | solution.py:753
  95.0 3.2 %collective-permute-done.34.got_ref = bf16[16,4608]{1,0:T(8,128)(2,1)S(1)} collective-permute-done((bf16[16,4608]{1,0:T(8,128)(2,1)S(1)}, bf16[16,4608]{1,0:T(8,128)(2,1)S(1)}, u32[]{:S(2)}, u32[]{:S(2)}) %collective-permute-start.34) | collective-permute-done | bytes 147488 | tf_op jit(solution)/shard_map/ppermute | solution.py:753
  98.2 2.4 %collective-permute-done.35.refs_0_ = bf16[16,4608]{1,0:T(8,128)(2,1)S(1)} collective-permute-done((bf16[16,4608]{1,0:T(8,128)(2,1)S(1)}, bf16[16,4608]{1,0:T(8,128)(2,1)S(1)}, u32[]{:S(2)}, u32[]{:S(2)}) %collective-permute-start.35) | collective-permute-done | bytes 147488 | tf_op jit(solution)/shard_map/ppermute | solution.py:753
  100.6 2.7 %collective-permute-start.37 = (bf16[16,4608]{1,0:T(8,128)(2,1)S(1)}, bf16[16,4608]{1,0:T(8,128)(2,1)S(1)}, u32[]{:S(2)}, u32[]{:S(2)}) collective-permute-start(bf16[16,4608]{1,0:T(8,128)(2,1)S(1)} %shard_map.183), channel_id=1, source_target_pairs={{0,8},{1,9},{2,10},{3,11},{4,12},{5,13},{6,14},{7,15},{8,0},{9,1},... | collective-permute-start | bytes 442376 | tf_op jit(solution)/shard_map/ppermute | solution.py:753
  103.4 3.9 %collective-permute-start.39 = (bf16[16,4608]{1,0:T(8,128)(2,1)S(1)}, bf16[16,4608]{1,0:T(8,128)(2,1)S(1)}, u32[]{:S(2)}, u32[]{:S(2)}) collective-permute-start(bf16[16,4608]{1,0:T(8,128)(2,1)S(1)} %shard_map.185), channel_id=1, source_target_pairs={{0,12},{1,13},{2,14},{3,15},{4,0},{5,1},{6,2},{7,3},{8,4},{9,5},{1... | collective-permute-start | bytes 442376 | tf_op jit(solution)/shard_map/ppermute | solution.py:753
  109.1 5.3 %collective-permute-done.37.refs_1_ = bf16[16,4608]{1,0:T(8,128)(2,1)S(1)} collective-permute-done((bf16[16,4608]{1,0:T(8,128)(2,1)S(1)}, bf16[16,4608]{1,0:T(8,128)(2,1)S(1)}, u32[]{:S(2)}, u32[]{:S(2)}) %collective-permute-start.37) | collective-permute-done | bytes 147488 | tf_op jit(solution)/shard_map/ppermute | solution.py:753
  117.8 2.2 %collective-permute-done.42.refs_4_ = bf16[8,4608]{1,0:T(8,128)(2,1)S(1)} collective-permute-done((bf16[8,4608]{1,0:T(8,128)(2,1)S(1)}, bf16[8,4608]{1,0:T(8,128)(2,1)S(1)}, u32[]{:S(2)}, u32[]{:S(2)}) %collective-permute-start.42) | collective-permute-done | bytes 73760 | tf_op jit(solution)/shard_map/ppermute | solution.py:753
  122.4 3.6 %shard_map.190 = (f32[8,448,128]{2,1,0:T(8,128)S(1)}, bf16[8,448,128]{2,1,0:T(8,128)(2,1)S(1)}) custom-call(bf16[1152,1920]{1,0:T(8,128)(2,1)S(1)} %get-tuple-element.85.xt_ref, bf16[1664,256]{1,0:T(8,128)(2,1)S(1)} %get-tuple-element.145.d_ref, f32[1,256]{1,0:T(1,128)S(1)} %get-tuple-element.131.bias_ref, f32[8,256]{1,0:T(8,128)S(1)} %shard_map.189.st_ref), custom_call_target="tpu_custom_call" | custom-call | flops 4070000128 | bytes 1 | tf_op jit(solution)/shard_map/pallas_call | solution.py:79
  129.6 4.6 %collective-permute-done.46.came_ref = bf16[480,128]{1,0:T(8,128)(2,1)S(1)} collective-permute-done((bf16[480,128]{1,0:T(8,128)(2,1)S(1)}, bf16[480,128]{1,0:T(8,128)(2,1)S(1)}, u32[]{:S(2)}, u32[]{:S(2)}) %collective-permute-start.46) | collective-permute-done | bytes 122912 | tf_op jit(solution)/shard_map/ppermute | solution.py:753
  140.3 2.6 %collective-permute-done.49.came_ref = bf16[480,128]{1,0:T(8,128)(2,1)S(1)} collective-permute-done((bf16[480,128]{1,0:T(8,128)(2,1)S(1)}, bf16[480,128]{1,0:T(8,128)(2,1)S(1)}, u32[]{:S(2)}, u32[]{:S(2)}) %collective-permute-start.49) | collective-permute-done | bytes 122912 | tf_op jit(solution)/shard_map/ppermute | solution.py:753
  142.9 2.2 %collective-permute-done.50.came_ref = bf16[480,128]{1,0:T(8,128)(2,1)S(1)} collective-permute-done((bf16[480,128]{1,0:T(8,128)(2,1)S(1)}, bf16[480,128]{1,0:T(8,128)(2,1)S(1)}, u32[]{:S(2)}, u32[]{:S(2)}) %collective-permute-start.50) | collective-permute-done | bytes 122912 | tf_op jit(solution)/shard_map/ppermute | solution.py:753
  148.9 3.4 %collective-permute-start.52 = (bf16[512,128]{1,0:T(8,128)(2,1)S(1)}, bf16[512,128]{1,0:T(8,128)(2,1)S(1)}, u32[]{:S(2)}, u32[]{:S(2)}) collective-permute-start(bf16[512,128]{1,0:T(8,128)(2,1)S(1)} %shard_map.198), channel_id=1, source_target_pairs={{0,12},{1,13},{2,14},{3,15},{4,0},{5,1},{6,2},{7,3},{8,4},{9,5},{1... | collective-permute-start | bytes 393224 | tf_op jit(solution)/shard_map/ppermute | solution.py:753
  152.5 2.5 %collective-permute-done.48.refs_2_ = bf16[512,128]{1,0:T(8,128)(2,1)S(1)} collective-permute-done((bf16[512,128]{1,0:T(8,128)(2,1)S(1)}, bf16[512,128]{1,0:T(8,128)(2,1)S(1)}, u32[]{:S(2)}, u32[]{:S(2)}) %collective-permute-start.48) | collective-permute-done | bytes 131104 | tf_op jit(solution)/shard_map/ppermute | solution.py:753
  154.9 4.8 %shard_map.195 = f32[2,4608,256]{2,1,0:T(8,128)} custom-call(bf16[128,4608]{1,0:T(8,128)(2,1)S(1)} %get-tuple-element.116.x_ref.own_ref, bf16[128,4608]{1,0:T(8,128)(2,1)S(1)} %collective-permute-done.36.oc_ref, bf16[128,4608]{1,0:T(8,128)(2,1)S(1)} %collective-permute-done.31.x_ref, bf16[128,4608]{1,0:T(8,128)(2,1)S(1)} %collective-permute-done.47.xc_ref, ...), custom_call_target="tpu_custom_call" | custom-call | flops 5280000000 | bytes 1 | tf_op jit(solution)/shard_map/pallas_call | solution.py:996
  (152 shorter events, 79.3 us)
Async XLA Ops:
  3.7 20.2 %collective-permute-start = (bf16[13,4,16,384]{3,2,1,0:T(8,128)(2,1)S(1)}, bf16[13,4,16,384]{3,2,1,0:T(8,128)(2,1)S(1)}, u32[]{:S(2)}, u32[]{:S(2)}) collective-permute-start(bf16[13,4,16,384]{3,2,1,0:T(8,128)(2,1)S(1)} %get-tuple-element.84), channel_id=1, source_target_pairs={{0,16},{1,17},{2,18},{3,19},{4,20},{5,21},{6,22},{7,23},{8,24},{9,... | collective-permute-start | bytes 1916936 | tf_op jit(solution)/shard_map/ppermute | solution.py:753
  9.6 10.1 %collective-permute-start.7 = (bf16[432,128]{1,0:T(8,128)(2,1)S(1)}, bf16[432,128]{1,0:T(8,128)(2,1)S(1)}, u32[]{:S(2)}, u32[]{:S(2)}) collective-permute-start(bf16[432,128]{1,0:T(8,128)(2,1)S(1)} %shard_map.173.refs_4_), channel_id=1, source_target_pairs={{0,12},{1,13},{2,14},{3,15},{4,0},{5,1},{6,2},{7,3},{8,4},{9,5},{1... | collective-permute-start | bytes 331784 | tf_op jit(solution)/shard_map/ppermute | solution.py:753
  13.2 10.3 %collective-permute-start.5 = (bf16[432,128]{1,0:T(8,128)(2,1)S(1)}, bf16[432,128]{1,0:T(8,128)(2,1)S(1)}, u32[]{:S(2)}, u32[]{:S(2)}) collective-permute-start(bf16[432,128]{1,0:T(8,128)(2,1)S(1)} %shard_map.173.refs_4_), channel_id=1, source_target_pairs={{0,8},{1,9},{2,10},{3,11},{4,12},{5,13},{6,14},{7,15},{8,0},{9,1},... | collective-permute-start | bytes 331784 | tf_op jit(solution)/shard_map/ppermute | solution.py:753
  13.2 10.2 %collective-permute-start.3 = (bf16[432,128]{1,0:T(8,128)(2,1)S(1)}, bf16[432,128]{1,0:T(8,128)(2,1)S(1)}, u32[]{:S(2)}, u32[]{:S(2)}) collective-permute-start(bf16[432,128]{1,0:T(8,128)(2,1)S(1)} %shard_map.173.refs_4_), channel_id=1, source_target_pairs={{0,4},{1,5},{2,6},{3,7},{4,8},{5,9},{6,10},{7,11},{8,12},{9,13},{1... | collective-permute-start | bytes 331784 | tf_op jit(solution)/shard_map/ppermute | solution.py:753
  14.7 11.8 %all-to-all-start = ((bf16[16,8,256]{2,1,0:T(8,128)(2,1)}), bf16[16,8,256]{2,1,0:T(8,128)(2,1)S(1)}, u32[]{:S(2)}, u32[]{:S(2)}) async-start(bf16[16,8,256]{2,1,0:T(8,128)(2,1)} %get-tuple-element.94), calls=%async_computation | async-start | bytes 131072 | tf_op jit(solution)/shard_map/all_to_all | solution.py:814
  33.3 10.0 %collective-permute-start.17 = (bf16[16,8,256]{2,1,0:T(8,128)(2,1)S(1)}, bf16[16,8,256]{2,1,0:T(8,128)(2,1)S(1)}, u32[]{:S(2)}, u32[]{:S(2)}) collective-permute-start(bf16[16,8,256]{2,1,0:T(8,128)(2,1)S(1)} %all-to-all-done.own_ref), channel_id=1, source_target_pairs={{0,16},{1,17},{2,18},{3,19},{4,20},{5,21},{6,22},{7,23},{8,24},{9,... | collective-permute-start | bytes 196616 | tf_op jit(solution)/shard_map/ppermute | solution.py:753
  50.8 13.0 %collective-permute-start.24 = (bf16[16,4608]{1,0:T(8,128)(2,1)S(1)}, bf16[16,4608]{1,0:T(8,128)(2,1)S(1)}, u32[]{:S(2)}, u32[]{:S(2)}) collective-permute-start(bf16[16,4608]{1,0:T(8,128)(2,1)S(1)} %shard_map.175.refs_0_), channel_id=1, source_target_pairs={{0,8},{1,9},{2,10},{3,11},{4,12},{5,13},{6,14},{7,15},{8,0},{9,1},... | collective-permute-start | bytes 442376 | tf_op jit(solution)/shard_map/ppermute | solution.py:753
  50.9 13.0 %collective-permute-start.22 = (bf16[16,4608]{1,0:T(8,128)(2,1)S(1)}, bf16[16,4608]{1,0:T(8,128)(2,1)S(1)}, u32[]{:S(2)}, u32[]{:S(2)}) collective-permute-start(bf16[16,4608]{1,0:T(8,128)(2,1)S(1)} %shard_map.175.refs_0_), channel_id=1, source_target_pairs={{0,4},{1,5},{2,6},{3,7},{4,8},{5,9},{6,10},{7,11},{8,12},{9,13},{1... | collective-permute-start | bytes 442376 | tf_op jit(solution)/shard_map/ppermute | solution.py:753
  65.1 9.1 %collective-permute-start.27 = (bf16[16,4608]{1,0:T(8,128)(2,1)S(1)}, bf16[16,4608]{1,0:T(8,128)(2,1)S(1)}, u32[]{:S(2)}, u32[]{:S(2)}) collective-permute-start(bf16[16,4608]{1,0:T(8,128)(2,1)S(1)} %collective-permute-done.26.refs_6_), channel_id=1, source_target_pairs={{0,2},{1,3},{2,0},{3,1},{4,6},{5,7},{6,4},{7,5},{8,10},{9,11},{10,... | collective-permute-start | bytes 442376 | tf_op jit(solution)/shard_map/ppermute | solution.py:753
  66.4 10.9 %collective-permute-start.25 = (bf16[16,4608]{1,0:T(8,128)(2,1)S(1)}, bf16[16,4608]{1,0:T(8,128)(2,1)S(1)}, u32[]{:S(2)}, u32[]{:S(2)}) collective-permute-start(bf16[16,4608]{1,0:T(8,128)(2,1)S(1)} %collective-permute-done.24.refs_4_), channel_id=1, source_target_pairs={{0,2},{1,3},{2,0},{3,1},{4,6},{5,7},{6,4},{7,5},{8,10},{9,11},{10,... | collective-permute-start | bytes 442376 | tf_op jit(solution)/shard_map/ppermute | solution.py:753
  67.1 13.0 %collective-permute-start.23 = (bf16[16,4608]{1,0:T(8,128)(2,1)S(1)}, bf16[16,4608]{1,0:T(8,128)(2,1)S(1)}, u32[]{:S(2)}, u32[]{:S(2)}) collective-permute-start(bf16[16,4608]{1,0:T(8,128)(2,1)S(1)} %collective-permute-done.22.refs_2_), channel_id=1, source_target_pairs={{0,2},{1,3},{2,0},{3,1},{4,6},{5,7},{6,4},{7,5},{8,10},{9,11},{10,... | collective-permute-start | bytes 442376 | tf_op jit(solution)/shard_map/ppermute | solution.py:753
  85.8 9.2 %collective-permute-start.33 = (bf16[16,4608]{1,0:T(8,128)(2,1)S(1)}, bf16[16,4608]{1,0:T(8,128)(2,1)S(1)}, u32[]{:S(2)}, u32[]{:S(2)}) collective-permute-start(bf16[16,4608]{1,0:T(8,128)(2,1)S(1)} %get-tuple-element.113), channel_id=1, source_target_pairs={{0,2},{1,3},{2,0},{3,1},{4,6},{5,7},{6,4},{7,5},{8,10},{9,11},{10,... | collective-permute-start | bytes 442376 | tf_op jit(solution)/shard_map/ppermute | solution.py:753
  87.2 11.0 %collective-permute-start.34 = (bf16[16,4608]{1,0:T(8,128)(2,1)S(1)}, bf16[16,4608]{1,0:T(8,128)(2,1)S(1)}, u32[]{:S(2)}, u32[]{:S(2)}) collective-permute-start(bf16[16,4608]{1,0:T(8,128)(2,1)S(1)} %get-tuple-element.114), channel_id=1, source_target_pairs={{0,2},{1,3},{2,0},{3,1},{4,6},{5,7},{6,4},{7,5},{8,10},{9,11},{10,... | collective-permute-start | bytes 442376 | tf_op jit(solution)/shard_map/ppermute | solution.py:753
  87.9 12.7 %collective-permute-start.35 = (bf16[16,4608]{1,0:T(8,128)(2,1)S(1)}, bf16[16,4608]{1,0:T(8,128)(2,1)S(1)}, u32[]{:S(2)}, u32[]{:S(2)}) collective-permute-start(bf16[16,4608]{1,0:T(8,128)(2,1)S(1)} %get-tuple-element.115), channel_id=1, source_target_pairs={{0,2},{1,3},{2,0},{3,1},{4,6},{5,7},{6,4},{7,5},{8,10},{9,11},{10,... | collective-permute-start | bytes 442376 | tf_op jit(solution)/shard_map/ppermute | solution.py:753
  89.2 18.1 %collective-permute-start.31 = (bf16[128,4608]{1,0:T(8,128)(2,1)S(1)}, bf16[128,4608]{1,0:T(8,128)(2,1)S(1)}, u32[]{:S(2)}, u32[]{:S(2)}) collective-permute-start(bf16[128,4608]{1,0:T(8,128)(2,1)S(1)} %get-tuple-element.116.x_ref.own_ref), channel_id=1, source_target_pairs={{1,17},{3,19},{5,21},{7,23},{9,25},{11,27},{13,29},{15,31},{16,0},... | collective-permute-start | bytes 3538952 | tf_op jit(solution)/shard_map/ppermute | solution.py:904
  100.6 13.8 %collective-permute-start.37 = (bf16[16,4608]{1,0:T(8,128)(2,1)S(1)}, bf16[16,4608]{1,0:T(8,128)(2,1)S(1)}, u32[]{:S(2)}, u32[]{:S(2)}) collective-permute-start(bf16[16,4608]{1,0:T(8,128)(2,1)S(1)} %shard_map.183), channel_id=1, source_target_pairs={{0,8},{1,9},{2,10},{3,11},{4,12},{5,13},{6,14},{7,15},{8,0},{9,1},... | collective-permute-start | bytes 442376 | tf_op jit(solution)/shard_map/ppermute | solution.py:753
  103.3 11.1 %collective-permute-start.38 = (bf16[16,4608]{1,0:T(8,128)(2,1)S(1)}, bf16[16,4608]{1,0:T(8,128)(2,1)S(1)}, u32[]{:S(2)}, u32[]{:S(2)}) collective-permute-start(bf16[16,4608]{1,0:T(8,128)(2,1)S(1)} %shard_map.184), channel_id=1, source_target_pairs={{0,4},{1,5},{2,6},{3,7},{4,8},{5,9},{6,10},{7,11},{8,12},{9,13},{1... | collective-permute-start | bytes 442376 | tf_op jit(solution)/shard_map/ppermute | solution.py:753
  103.4 12.1 %collective-permute-start.39 = (bf16[16,4608]{1,0:T(8,128)(2,1)S(1)}, bf16[16,4608]{1,0:T(8,128)(2,1)S(1)}, u32[]{:S(2)}, u32[]{:S(2)}) collective-permute-start(bf16[16,4608]{1,0:T(8,128)(2,1)S(1)} %shard_map.185), channel_id=1, source_target_pairs={{0,12},{1,13},{2,14},{3,15},{4,0},{5,1},{6,2},{7,3},{8,4},{9,5},{1... | collective-permute-start | bytes 442376 | tf_op jit(solution)/shard_map/ppermute | solution.py:753
  107.3 10.5 %collective-permute-start.43 = (bf16[208,256]{1,0:T(8,128)(2,1)S(1)}, bf16[208,256]{1,0:T(8,128)(2,1)S(1)}, u32[]{:S(2)}, u32[]{:S(2)}) collective-permute-start(bf16[208,256]{1,0:T(8,128)(2,1)S(1)} %get-tuple-element.127), channel_id=1, source_target_pairs={{0,16},{1,17},{2,18},{3,19},{4,20},{5,21},{6,22},{7,23},{8,24},{9,... | collective-permute-start | bytes 319496 | tf_op jit(solution)/shard_map/ppermute | solution.py:753
  134.2 20.8 %collective-permute-start.47 = (bf16[128,4608]{1,0:T(8,128)(2,1)S(1)}, bf16[128,4608]{1,0:T(8,128)(2,1)S(1)}, u32[]{:S(2)}, u32[]{:S(2)}) collective-permute-start(bf16[128,4608]{1,0:T(8,128)(2,1)S(1)} %collective-permute-done.31.x_ref), channel_id=1, source_target_pairs={{0,1},{1,0},{2,3},{3,2},{4,5},{5,4},{6,7},{7,6},{8,9},{9,8},{10,11... | collective-permute-start | bytes 3538952 | tf_op jit(solution)/shard_map/ppermute | solution.py:753
  136.2 9.0 %collective-permute-start.50 = (bf16[480,128]{1,0:T(8,128)(2,1)S(1)}, bf16[480,128]{1,0:T(8,128)(2,1)S(1)}, u32[]{:S(2)}, u32[]{:S(2)}) collective-permute-start(bf16[480,128]{1,0:T(8,128)(2,1)S(1)} %get-tuple-element.144), channel_id=1, source_target_pairs={{0,2},{1,3},{2,0},{3,1},{4,6},{5,7},{6,4},{7,5},{8,10},{9,11},{10,... | collective-permute-start | bytes 368648 | tf_op jit(solution)/shard_map/ppermute | solution.py:753
  137.1 22.9 %collective-permute-start.54 = (bf16[13,4,16,384]{3,2,1,0:T(8,128)(2,1)S(1)}, bf16[13,4,16,384]{3,2,1,0:T(8,128)(2,1)S(1)}, u32[]{:S(2)}, u32[]{:S(2)}) collective-permute-start(bf16[13,4,16,384]{3,2,1,0:T(8,128)(2,1)S(1)} %shard_map.191), channel_id=1, source_target_pairs={{0,16},{1,17},{2,18},{3,19},{4,20},{5,21},{6,22},{7,23},{8,24},{9,... | collective-permute-start | bytes 1916936 | tf_op jit(solution)/shard_map/ppermute | solution.py:753
  145.2 9.7 %collective-permute-start.48 = (bf16[512,128]{1,0:T(8,128)(2,1)S(1)}, bf16[512,128]{1,0:T(8,128)(2,1)S(1)}, u32[]{:S(2)}, u32[]{:S(2)}) collective-permute-start(bf16[512,128]{1,0:T(8,128)(2,1)S(1)} %shard_map.194), channel_id=1, source_target_pairs={{0,8},{1,9},{2,10},{3,11},{4,12},{5,13},{6,14},{7,15},{8,0},{9,1},... | collective-permute-start | bytes 393224 | tf_op jit(solution)/shard_map/ppermute | solution.py:753
  148.9 10.9 %collective-permute-start.52 = (bf16[512,128]{1,0:T(8,128)(2,1)S(1)}, bf16[512,128]{1,0:T(8,128)(2,1)S(1)}, u32[]{:S(2)}, u32[]{:S(2)}) collective-permute-start(bf16[512,128]{1,0:T(8,128)(2,1)S(1)} %shard_map.198), channel_id=1, source_target_pairs={{0,12},{1,13},{2,14},{3,15},{4,0},{5,1},{6,2},{7,3},{8,4},{9,5},{1... | collective-permute-start | bytes 393224 | tf_op jit(solution)/shard_map/ppermute | solution.py:753
  (46 other events, 309.3 us)

commit v2 on v1

--- a/solution.py
+++ b/solution.py
@@ -214,9 +214,9 @@
 
 
 def conv_forward(place, side, pool, images, *refs):
-    g_ref, x_ref, b_ref, q_ref = refs[:4]
-    blocks = refs[4:-4]
-    pre_ref, mine_ref, other_ref, w_ref = refs[-4:]
+    g_ref, x_ref, b_ref = refs[:3]
+    blocks = refs[3:-5]
+    pre_ref, mine_ref, other_ref, w_ref, sum_ref = refs[-5:]
     at = place()
     chips = len(blocks) // 2
     rows, half = blocks[0].shape
@@ -229,7 +229,7 @@
     slab = images * WIDTH
     depth = x_ref.shape[1]
     channels = w_ref.shape[1]
-    acts = {}
+    acts, pooled = {}, {}
     bias = jnp.where(at.task == 0, b_ref[0:1, :], b_ref[1:2, :])
     group = g_ref[...]
     for start in range(0, side, 4):
@@ -250,22 +250,26 @@
         for p in range(pool):
             if not (start <= 2 * p + 2 < start + rows):
                 continue
-            cells = window_sum(q_ref, acts[2 * p] + acts[2 * p + 1] + acts[2 * p + 2])
-            row = []
+            rows_sum = acts[2 * p] + acts[2 * p + 1] + acts[2 * p + 2]
+            for tile in range(channels // 128):
+                sum_ref[p, tile] = rows_sum[:, tile * 128 : (tile + 1) * 128]
             for q in range(pool):
                 kept = jnp.where(max(p, q) + group < pool, 1.0 / 9.0, 0.0)
-                row.append((cells[q * images : (q + 1) * images, :] * kept).astype(bf16))
-            lanes = (p % (pool // 2)) * pool * channels
-            lanes = slice(lanes, lanes + pool * channels)
-            row = jnp.concatenate(row, axis=1)
-
-            @pl.when(at.core == (2 * p) // pool)
-            def _(row=row, lanes=lanes):
-                mine_ref[:, lanes] = row
-
-            @pl.when(at.core != (2 * p) // pool)
-            def _(row=row, lanes=lanes):
-                other_ref[:, lanes] = row
+                cell = None
+                for x in range(2 * q, 2 * q + 3):
+                    spot = pl.ds(x, images, stride=WIDTH)
+                    column = jnp.concatenate(
+                        [sum_ref[p, tile, spot, :] for tile in range(channels // 128)], axis=1
+                    )
+                    cell = column if cell is None else cell + column
+                pooled[p, q] = cell * kept
+    low = at.core == 0
+    for p in range(pool // 2):
+        for q in range(pool):
+            zero, one = pooled[p, q], pooled[p + pool // 2, q]
+            lanes = slice((p * pool + q) * channels, (p * pool + q + 1) * channels)
+            mine_ref[:, lanes] = jnp.where(low, zero, one).astype(bf16)
+            other_ref[:, lanes] = jnp.where(low, one, zero).astype(bf16)
 
 
 def slope_and_back(pre_ref, w_ref, slope_ref, back_ref):
@@ -773,7 +777,8 @@
         rows = [[block, move(block, dy=1)]] + [None] * (planes - 1)
         here = {k: move(block, dz=k) for k in shifts}
         for k in shifts:
-            rows[k] = [here[k], move(here[k], dy=1)]
+            first = after(here[k], rows[0][1]) if k == shifts[0] else here[k]
+            rows[k] = [here[k], move(first, dy=1)]
         return [piece for pair in rows for piece in pair]
 
     weight_mine, weight_other = call(
@@ -819,7 +824,6 @@
         for n in range(images):
             window[q * images + n, n * WIDTH + 2 * q : n * WIDTH + 2 * q + 3] = 1.0
     window_t = jnp.asarray(window.T, bf16)
-    window = jnp.asarray(window, bf16)
     stacked = after(stacked, stacked_t)
     conv_pre, pooled_mine, pooled_other, kernel = call(
         functools.partial(conv_forward, place, side, pool, images),
@@ -829,7 +833,8 @@
             shape_of((images, part), bf16),
             shape_of((chips * chip_rows, channels), bf16),
         ),
-        (groups, stacked, conv_bias, window, *weight_blocks, *weight_far),
+        (groups, stacked, conv_bias, *weight_blocks, *weight_far),
+        (pltpu.VMEM((pool, channels // 128, slab, 128), f32),),
     )
 
     pooled_mine = after(pooled_mine, cot_far)
@@ -846,13 +851,13 @@
     up = call(
         functools.partial(cot_rows, place),
         shape_of((2, rows_all, units), f32),
-        (cot_own, after(cot_far, *blocks[2::2])),
+        (cot_own, cot_far),
     )
 
     fc_mine, fc_other = call(
         functools.partial(split_fc, place),
         (shape_of((part, units), bf16), shape_of((part, units), bf16)),
-        (after(fc_weight, *blocks[2::2]),),
+        (after(fc_weight, pooled_mine),),
         (DMA((2,)),),
         blocks=None,
         any_first=True,
@@ -865,7 +870,7 @@
             shape_of(conv_pre.shape, f32),
             shape_of((9 * channels, channels_in), bf16),
         ),
-        (after(conv_pre, *blocks[2::2]), kernel),
+        (conv_pre, kernel),
     )
 
     gathered, far_term = call(
@@ -899,10 +904,10 @@
     for k in order[:-1]:
         low = call(add_rows, (shape_of(piece, bf16),), (kept[k], arrived[k]))[0]
         passed[k] = move(low, dz=-k)
-    x_came = move(after(x_pack, *arrived.values()), dx=1)
     cross = lambda b, z, y, c: ((b + pairs) % (2 * pairs), z, y, c) if c != b // pairs else None
     features_x = lax.ppermute(gathered, BOTH, links(cross))
-    features_c = move(after(gathered, *arrived.values()), dc=1)
+    x_came = move(after(x_pack, features_x), dx=1)
+    features_c = move(after(gathered, features_x), dc=1)
     d_total, d_mine, d_mine_low, d_other = call(
         functools.partial(block_total, place),
         (
@@ -911,7 +916,7 @@
             shape_of((images, part), bf16),
             shape_of((images, part), bf16),
         ),
-        (after(kept[0], features_x, features_c), arrived[0], *[passed[k] for k in order[:-1]]),
+        (after(kept[0], features_x), arrived[0], *[passed[k] for k in order[:-1]]),
     )
 
     d_x = move(d_mine_low, dx=1)
@@ -944,6 +949,7 @@
         (pltpu.VMEM((chips * chip_rows, channels), f32),),
     )
     got = move(send, dc=1)
+    features_xc = move(after(features_x, d_conv), dc=1)
     thin = (side, few, WIDTH, channels_in)
     pad = (pltpu.VMEM(((side + 2) * slab // 2, 3 * channels), bf16),)
     back_send = call(
@@ -956,25 +962,26 @@
     sent = call(
         sum_pieces,
         tuple(shape_of(flat, bf16) for _ in range(planes)),
-        (keep, after(got, back_send), out_send),
+        (keep, after(got, back_send, features_c, features_xc), out_send),
     )
     arrived = {k: move(sent[k], dy=1) for k in order}
     parts = {}
     for k in order:
-        parts[k] = call(
+        parts[k] = low = call(
             functools.partial(sum_three, k),
             shape_of((full + 2 * ride, half), bf16 if k else f32),
             (keep, got, arrived[k], out_keep),
         )
         if k:
-            parts[k] = move(parts[k], dz=-k)
+            last_sum = low
+            parts[k] = move(low, dz=-k)
     late = arrived[order[0]]
 
     back_far = move(back_send, dx=1)
     back_own = call(
         functools.partial(picture_grad, place, False, side, slab),
         shape_of(thin, bf16),
-        (after(d_conv, *[arrived[k] for k in order]), kernel_back),
+        (after(d_conv, last_sum), kernel_back),
         pad,
     )
     input_grad = call(
@@ -988,8 +995,7 @@
         own = jnp.expand_dims(own, axis)
         return ordered(task, own, jnp.zeros_like(own), axis=axis)
 
-    d_fc_last = after(d_fc, parts[order[0]])
-    features_xc = move(after(features_x, late), dc=1)
+    d_fc_last = after(d_fc, last_sum)
     steps = 3
     wide_spec = pl.BlockSpec((rows_all, part // steps), lambda i: (0, i))
     whole_spec = [pl.BlockSpec(a.shape, lambda i: (0, 0)) for a in (d_fc, x_came)]
@@ -1011,7 +1017,7 @@
             shape_of((tall + chips * ride // 2, half), bf16),
             shape_of((chips, images, units), f32),
         ),
-        (after(parts[0], fc_weight_grad, back_own), *[parts[planes - k] for k in range(1, planes)]),
+        (after(parts[0], fc_weight_grad, input_grad), *[parts[planes - k] for k in range(1, planes)]),
         (pltpu.VMEM((chip_rows, half), f32), pltpu.VMEM((planes, 8, half), f32)),
     )
     k_x = move(k_mine, dx=1)

time: 169 us -> 139 us (0.82)
  waiting for transfers between devices: 72.6 us -> 54.3 us
  starting transfers between devices: 59.5 us -> 50.9 us
  Pallas kernels: 32.5 us -> 29 us
    ppermute x56, waiting for transfers between devices: 71.5 us -> 53.7 us  [move(): return lax.ppermute(value, BOTH, links(where))]
    ppermute x56, starting transfers between devices: 53.3 us -> 44.4 us  [move(): return lax.ppermute(value, BOTH, links(where))]
    pallas_call x32, Pallas kernels: 27.7 us -> 24.2 us  [call(): pl.pallas_call(body, out_shape=out_shape, **steps, in_specs=blocks or [SM...]
  transfers between devices with their start and end apart: 58 -> 58, of which waited for: 31 -> 30; matrix products, arithmetic and copies ran while one was open for 1% -> 1% of each run, Pallas kernels for 14% -> 18%
where the time goes in v2:
time: 139 us
  waiting for transfers between devices  54.3 us (39%)
  starting transfers between devices  50.9 us (37%)
  Pallas kernels  29 us (21%)
  local copies, waits for them, and re-layouts  3.28 us (2%)
    ppermute x56, waiting for transfers between devices, move(): return lax.ppermute(value, BOTH, links(where))  53.7 us
    ppermute x56, starting transfers between devices, move(): return lax.ppermute(value, BOTH, links(where))  44.4 us
    pallas_call x32, Pallas kernels, call(): pl.pallas_call(body, out_shape=out_shape, **steps, in_specs=blocks or [SM...  24.2 us
    all_to_all x1, starting transfers between devices, on_device(): lax.all_to_all(cot_send, 'mp', split_axis=0, concat_axis=0, tiled=True)  5.03 us
    pallas_call x1, Pallas kernels, on_device(): pl.pallas_call(functools.partial(fc_grad, place), out_shape=shape_of((2,...  4.79 us
    unnamed x24, local copies, waits for them, and re-layouts  3.28 us
  transfers between devices with their start and end apart: 58, of which 30 were waited for; matrix products, arithmetic and copies ran while one was open for 1% of the time, Pallas kernels for 18%

profile of v2, /device:TPU:0, one launch (start us, length us, event | category | flops | bytes accessed | tf_op | source)
XLA Modules:
  0.0 138.5 jit_solution(5079221580999676205)
XLA Ops:
  3.7 2.9 %collective-permute-start = (bf16[13,4,16,384]{3,2,1,0:T(8,128)(2,1)S(1)}, bf16[13,4,16,384]{3,2,1,0:T(8,128)(2,1)S(1)}, u32[]{:S(2)}, u32[]{:S(2)}) collective-permute-start(bf16[13,4,16,384]{3,2,1,0:T(8,128)(2,1)S(1)} %get-tuple-element.84), channel_id=1, source_target_pairs={{0,16},{1,17},{2,18},{3,19},{4,20},{5,21},{6,22},{7,23},{8,24},{9,... | collective-permute-start | bytes 1916936 | tf_op jit(solution)/shard_map/ppermute | solution.py:757
  11.1 2.2 %collective-permute-start.7 = (bf16[432,128]{1,0:T(8,128)(2,1)S(1)}, bf16[432,128]{1,0:T(8,128)(2,1)S(1)}, u32[]{:S(2)}, u32[]{:S(2)}) collective-permute-start(bf16[432,128]{1,0:T(8,128)(2,1)S(1)} %shard_map.164.refs_3_), channel_id=1, source_target_pairs={{0,12},{1,13},{2,14},{3,15},{4,0},{5,1},{6,2},{7,3},{8,4},{9,5},{1... | collective-permute-start | bytes 331784 | tf_op jit(solution)/shard_map/ppermute | solution.py:757
  14.2 5.0 %all-to-all-start = ((bf16[16,8,256]{2,1,0:T(8,128)(2,1)}), bf16[16,8,256]{2,1,0:T(8,128)(2,1)S(1)}, u32[]{:S(2)}, u32[]{:S(2)}) async-start(bf16[16,8,256]{2,1,0:T(8,128)(2,1)} %get-tuple-element.95), calls=%async_computation | async-start | bytes 131072 | tf_op jit(solution)/shard_map/all_to_all | solution.py:819
  21.4 2.1 %collective-permute-done.5.refs_7_ = bf16[432,128]{1,0:T(8,128)(2,1)S(1)} collective-permute-done((bf16[432,128]{1,0:T(8,128)(2,1)S(1)}, bf16[432,128]{1,0:T(8,128)(2,1)S(1)}, u32[]{:S(2)}, u32[]{:S(2)}) %collective-permute-start.5) | collective-permute-done | bytes 110624 | tf_op jit(solution)/shard_map/ppermute | solution.py:757
  26.7 2.7 %collective-permute-done.6.refs_8_ = bf16[432,128]{1,0:T(8,128)(2,1)S(1)} collective-permute-done((bf16[432,128]{1,0:T(8,128)(2,1)S(1)}, bf16[432,128]{1,0:T(8,128)(2,1)S(1)}, u32[]{:S(2)}, u32[]{:S(2)}) %collective-permute-start.6) | collective-permute-done | bytes 110624 | tf_op jit(solution)/shard_map/ppermute | solution.py:757
  29.4 2.0 %collective-permute-done.4.refs_6_ = bf16[432,128]{1,0:T(8,128)(2,1)S(1)} collective-permute-done((bf16[432,128]{1,0:T(8,128)(2,1)S(1)}, bf16[432,128]{1,0:T(8,128)(2,1)S(1)}, u32[]{:S(2)}, u32[]{:S(2)}) %collective-permute-start.4) | collective-permute-done | bytes 110624 | tf_op jit(solution)/shard_map/ppermute | solution.py:757
  31.4 1.9 %shard_map.162 = (bf16[1920,1152]{1,0:T(8,128)(2,1)S(1)}, bf16[1152,1920]{1,0:T(8,128)(2,1)S(1)}, f32[8,256]{1,0:T(8,128)S(1)}) custom-call(bf16[13,4,16,384]{3,2,1,0:T(8,128)(2,1)S(1)} %get-tuple-element.83.own_ref, bf16[13,4,16,384]{3,2,1,0:T(8,128)(2,1)S(1)} %collective-permute-done.far_ref), custom_call_target="tpu_custom_call" | custom-call | flops 2200000000 | bytes 1 | tf_op jit(solution)/shard_map/pallas_call | solution.py:79
  34.0 4.1 %shard_map.165 = (f32[1664,256]{1,0:T(8,128)S(1)}, bf16[8,4608]{1,0:T(8,128)(2,1)S(1)}, bf16[8,4608]{1,0:T(8,128)(2,1)S(1)}, bf16[3456,256]{1,0:T(8,128)(2,1)S(1)}) custom-call(f32[8,256]{1,0:T(8,128)S(1)} %get-tuple-element.86.refs_0_, bf16[1920,1152]{1,0:T(8,128)(2,1)S(1)} %get-tuple-element.88.refs_1_, f32[2,256]{1,0:T(2,128)S(1)} %copy-done.4, ...), custom_call_target="tpu_custom_call" | custom-call | flops 8249999872 | bytes 1 | tf_op jit(solution)/shard_map/pallas_call | solution.py:79
  41.0 2.0 %collective-permute-done.20.xc_ref = bf16[8,4608]{1,0:T(8,128)(2,1)S(1)} collective-permute-done((bf16[8,4608]{1,0:T(8,128)(2,1)S(1)}, bf16[8,4608]{1,0:T(8,128)(2,1)S(1)}, u32[]{:S(2)}, u32[]{:S(2)}) %collective-permute-start.20) | collective-permute-done | bytes 73760 | tf_op jit(solution)/shard_map/ppermute | solution.py:757
  46.9 2.6 %collective-permute-start.26 = (bf16[16,4608]{1,0:T(8,128)(2,1)S(1)}, bf16[16,4608]{1,0:T(8,128)(2,1)S(1)}, u32[]{:S(2)}, u32[]{:S(2)}) collective-permute-start(bf16[16,4608]{1,0:T(8,128)(2,1)S(1)} %shard_map.166.refs_0_), channel_id=1, source_target_pairs={{0,12},{1,13},{2,14},{3,15},{4,0},{5,1},{6,2},{7,3},{8,4},{9,5},{1... | collective-permute-start | bytes 442376 | tf_op jit(solution)/shard_map/ppermute | solution.py:757
  49.7 4.0 %collective-permute-done.22.refs_2_ = bf16[16,4608]{1,0:T(8,128)(2,1)S(1)} collective-permute-done((bf16[16,4608]{1,0:T(8,128)(2,1)S(1)}, bf16[16,4608]{1,0:T(8,128)(2,1)S(1)}, u32[]{:S(2)}, u32[]{:S(2)}) %collective-permute-start.22) | collective-permute-done | bytes 147488 | tf_op jit(solution)/shard_map/ppermute | solution.py:757
  56.0 5.7 %collective-permute-done.24.refs_4_ = bf16[16,4608]{1,0:T(8,128)(2,1)S(1)} collective-permute-done((bf16[16,4608]{1,0:T(8,128)(2,1)S(1)}, bf16[16,4608]{1,0:T(8,128)(2,1)S(1)}, u32[]{:S(2)}, u32[]{:S(2)}) %collective-permute-start.24) | collective-permute-done | bytes 147488 | tf_op jit(solution)/shard_map/ppermute | solution.py:757
  64.1 3.2 %collective-permute-done.25.refs_5_ = bf16[16,4608]{1,0:T(8,128)(2,1)S(1)} collective-permute-done((bf16[16,4608]{1,0:T(8,128)(2,1)S(1)}, bf16[16,4608]{1,0:T(8,128)(2,1)S(1)}, u32[]{:S(2)}, u32[]{:S(2)}) %collective-permute-start.25) | collective-permute-done | bytes 147488 | tf_op jit(solution)/shard_map/ppermute | solution.py:757
  79.0 2.6 %collective-permute-done.33.got_ref = bf16[16,4608]{1,0:T(8,128)(2,1)S(1)} collective-permute-done((bf16[16,4608]{1,0:T(8,128)(2,1)S(1)}, bf16[16,4608]{1,0:T(8,128)(2,1)S(1)}, u32[]{:S(2)}, u32[]{:S(2)}) %collective-permute-start.33) | collective-permute-done | bytes 147488 | tf_op jit(solution)/shard_map/ppermute | solution.py:757
  81.7 3.0 %collective-permute-done.35.got_ref = bf16[16,4608]{1,0:T(8,128)(2,1)S(1)} collective-permute-done((bf16[16,4608]{1,0:T(8,128)(2,1)S(1)}, bf16[16,4608]{1,0:T(8,128)(2,1)S(1)}, u32[]{:S(2)}, u32[]{:S(2)}) %collective-permute-start.35) | collective-permute-done | bytes 147488 | tf_op jit(solution)/shard_map/ppermute | solution.py:757
  84.9 3.1 %collective-permute-done.37.got_ref = bf16[16,4608]{1,0:T(8,128)(2,1)S(1)} collective-permute-done((bf16[16,4608]{1,0:T(8,128)(2,1)S(1)}, bf16[16,4608]{1,0:T(8,128)(2,1)S(1)}, u32[]{:S(2)}, u32[]{:S(2)}) %collective-permute-start.37) | collective-permute-done | bytes 147488 | tf_op jit(solution)/shard_map/ppermute | solution.py:757
  93.1 2.1 %collective-permute-done.38.refs_3_ = bf16[16,4608]{1,0:T(8,128)(2,1)S(1)} collective-permute-done((bf16[16,4608]{1,0:T(8,128)(2,1)S(1)}, bf16[16,4608]{1,0:T(8,128)(2,1)S(1)}, u32[]{:S(2)}, u32[]{:S(2)}) %collective-permute-start.38) | collective-permute-done | bytes 147488 | tf_op jit(solution)/shard_map/ppermute | solution.py:757
  103.5 3.7 %shard_map.181 = (f32[8,448,128]{2,1,0:T(8,128)S(1)}, bf16[8,448,128]{2,1,0:T(8,128)(2,1)S(1)}) custom-call(bf16[1152,1920]{1,0:T(8,128)(2,1)S(1)} %get-tuple-element.85.xt_ref, bf16[1664,256]{1,0:T(8,128)(2,1)S(1)} %get-tuple-element.143.d_ref, f32[1,256]{1,0:T(1,128)S(1)} %get-tuple-element.130.bias_ref, f32[8,256]{1,0:T(8,128)S(1)} %shard_map.180.st_ref), custom_call_target="tpu_custom_call" | custom-call | flops 4070000128 | bytes 1 | tf_op jit(solution)/shard_map/pallas_call | solution.py:79
  107.3 2.1 %shard_map.182 = bf16[13,4,16,384]{3,2,1,0:T(8,128)(2,1)S(1)} custom-call(bf16[1664,256]{1,0:T(8,128)(2,1)S(1)} %get-tuple-element.143.d_ref, bf16[2304,384]{1,0:T(8,128)(2,1)S(1)} %get-tuple-element.105.w_ref), custom_call_target="tpu_custom_call" | custom-call | flops 2420000000 | bytes 1 | tf_op jit(solution)/shard_map/pallas_call | solution.py:79
  116.7 2.0 %collective-permute-done.51.came_ref = bf16[480,128]{1,0:T(8,128)(2,1)S(1)} collective-permute-done((bf16[480,128]{1,0:T(8,128)(2,1)S(1)}, bf16[480,128]{1,0:T(8,128)(2,1)S(1)}, u32[]{:S(2)}, u32[]{:S(2)}) %collective-permute-start.51) | collective-permute-done | bytes 122912 | tf_op jit(solution)/shard_map/ppermute | solution.py:757
  119.0 2.2 %collective-permute-done.49.came_ref = bf16[480,128]{1,0:T(8,128)(2,1)S(1)} collective-permute-done((bf16[480,128]{1,0:T(8,128)(2,1)S(1)}, bf16[480,128]{1,0:T(8,128)(2,1)S(1)}, u32[]{:S(2)}, u32[]{:S(2)}) %collective-permute-start.49) | collective-permute-done | bytes 122912 | tf_op jit(solution)/shard_map/ppermute | solution.py:757
  121.9 4.8 %shard_map.186 = f32[2,4608,256]{2,1,0:T(8,128)} custom-call(bf16[128,4608]{1,0:T(8,128)(2,1)S(1)} %get-tuple-element.136.x_ref.own_ref, bf16[128,4608]{1,0:T(8,128)(2,1)S(1)} %collective-permute-done.44.oc_ref, bf16[128,4608]{1,0:T(8,128)(2,1)S(1)} %collective-permute-done.31.x_ref, bf16[128,4608]{1,0:T(8,128)(2,1)S(1)} %collective-permute-done.45.xc_ref, ...), custom_call_target="tpu_custom_call" | custom-call | flops 5280000000 | bytes 1 | tf_op jit(solution)/shard_map/pallas_call | solution.py:1002
  126.6 2.1 %shard_map.187.own_ref = bf16[13,4,16,384]{3,2,1,0:T(8,128)(2,1)S(1)} custom-call(bf16[1664,256]{1,0:T(8,128)(2,1)S(1)} %get-tuple-element.143.d_ref, bf16[2304,384]{1,0:T(8,128)(2,1)S(1)} %get-tuple-element.105.w_ref), custom_call_target="tpu_custom_call" | custom-call | flops 2420000000 | bytes 1 | tf_op jit(solution)/shard_map/pallas_call | solution.py:79
  135.8 1.9 %collective-permute-done.55.x_ref = bf16[240,128]{1,0:T(8,128)(2,1)S(1)} collective-permute-done((bf16[240,128]{1,0:T(8,128)(2,1)S(1)}, bf16[240,128]{1,0:T(8,128)(2,1)S(1)}, u32[]{:S(2)}, u32[]{:S(2)}) %collective-permute-start.55) | collective-permute-done | bytes 61472 | tf_op jit(solution)/shard_map/ppermute | solution.py:757
  (150 shorter events, 67.2 us)
Async XLA Ops:
  3.7 20.2 %collective-permute-start = (bf16[13,4,16,384]{3,2,1,0:T(8,128)(2,1)S(1)}, bf16[13,4,16,384]{3,2,1,0:T(8,128)(2,1)S(1)}, u32[]{:S(2)}, u32[]{:S(2)}) collective-permute-start(bf16[13,4,16,384]{3,2,1,0:T(8,128)(2,1)S(1)} %get-tuple-element.84), channel_id=1, source_target_pairs={{0,16},{1,17},{2,18},{3,19},{4,20},{5,21},{6,22},{7,23},{8,24},{9,... | collective-permute-start | bytes 1916936 | tf_op jit(solution)/shard_map/ppermute | solution.py:757
  9.6 9.7 %collective-permute-start.3 = (bf16[432,128]{1,0:T(8,128)(2,1)S(1)}, bf16[432,128]{1,0:T(8,128)(2,1)S(1)}, u32[]{:S(2)}, u32[]{:S(2)}) collective-permute-start(bf16[432,128]{1,0:T(8,128)(2,1)S(1)} %shard_map.164.refs_3_), channel_id=1, source_target_pairs={{0,4},{1,5},{2,6},{3,7},{4,8},{5,9},{6,10},{7,11},{8,12},{9,13},{1... | collective-permute-start | bytes 331784 | tf_op jit(solution)/shard_map/ppermute | solution.py:757
  13.4 10.1 %collective-permute-start.5 = (bf16[432,128]{1,0:T(8,128)(2,1)S(1)}, bf16[432,128]{1,0:T(8,128)(2,1)S(1)}, u32[]{:S(2)}, u32[]{:S(2)}) collective-permute-start(bf16[432,128]{1,0:T(8,128)(2,1)S(1)} %shard_map.164.refs_3_), channel_id=1, source_target_pairs={{0,8},{1,9},{2,10},{3,11},{4,12},{5,13},{6,14},{7,15},{8,0},{9,1},... | collective-permute-start | bytes 331784 | tf_op jit(solution)/shard_map/ppermute | solution.py:757
  14.2 9.3 %collective-permute-start.9 = (bf16[432,128]{1,0:T(8,128)(2,1)S(1)}, bf16[432,128]{1,0:T(8,128)(2,1)S(1)}, u32[]{:S(2)}, u32[]{:S(2)}) collective-permute-start(bf16[432,128]{1,0:T(8,128)(2,1)S(1)} %shard_map.164.refs_3_), channel_id=1, source_target_pairs={{0,1},{1,0},{2,3},{3,2},{4,5},{5,4},{6,7},{7,6},{8,9},{9,8},{10,11... | collective-permute-start | bytes 331784 | tf_op jit(solution)/shard_map/ppermute | solution.py:757
  14.2 11.9 %all-to-all-start = ((bf16[16,8,256]{2,1,0:T(8,128)(2,1)}), bf16[16,8,256]{2,1,0:T(8,128)(2,1)S(1)}, u32[]{:S(2)}, u32[]{:S(2)}) async-start(bf16[16,8,256]{2,1,0:T(8,128)(2,1)} %get-tuple-element.95), calls=%async_computation | async-start | bytes 131072 | tf_op jit(solution)/shard_map/all_to_all | solution.py:819
  38.5 25.6 %collective-permute-start.28 = (bf16[4608,256]{1,0:T(8,128)(2,1)S(1)}, bf16[4608,256]{1,0:T(8,128)(2,1)S(1)}, u32[]{:S(2)}, u32[]{:S(2)}) collective-permute-start(bf16[4608,256]{1,0:T(8,128)(2,1)S(1)} %get-tuple-element.101), channel_id=1, source_target_pairs={{0,1},{1,0},{2,3},{3,2},{4,5},{5,4},{6,7},{7,6},{8,9},{9,8},{10,11... | collective-permute-start | bytes 7077896 | tf_op jit(solution)/shard_map/ppermute | solution.py:757
  45.1 8.6 %collective-permute-start.22 = (bf16[16,4608]{1,0:T(8,128)(2,1)S(1)}, bf16[16,4608]{1,0:T(8,128)(2,1)S(1)}, u32[]{:S(2)}, u32[]{:S(2)}) collective-permute-start(bf16[16,4608]{1,0:T(8,128)(2,1)S(1)} %shard_map.166.refs_0_), channel_id=1, source_target_pairs={{0,4},{1,5},{2,6},{3,7},{4,8},{5,9},{6,10},{7,11},{8,12},{9,13},{1... | collective-permute-start | bytes 442376 | tf_op jit(solution)/shard_map/ppermute | solution.py:757
  49.5 12.2 %collective-permute-start.24 = (bf16[16,4608]{1,0:T(8,128)(2,1)S(1)}, bf16[16,4608]{1,0:T(8,128)(2,1)S(1)}, u32[]{:S(2)}, u32[]{:S(2)}) collective-permute-start(bf16[16,4608]{1,0:T(8,128)(2,1)S(1)} %shard_map.166.refs_0_), channel_id=1, source_target_pairs={{0,8},{1,9},{2,10},{3,11},{4,12},{5,13},{6,14},{7,15},{8,0},{9,1},... | collective-permute-start | bytes 442376 | tf_op jit(solution)/shard_map/ppermute | solution.py:757
  53.7 13.6 %collective-permute-start.23 = (bf16[16,4608]{1,0:T(8,128)(2,1)S(1)}, bf16[16,4608]{1,0:T(8,128)(2,1)S(1)}, u32[]{:S(2)}, u32[]{:S(2)}) collective-permute-start(bf16[16,4608]{1,0:T(8,128)(2,1)S(1)} %collective-permute-done.22.refs_2_), channel_id=1, source_target_pairs={{0,2},{1,3},{2,0},{3,1},{4,6},{5,7},{6,4},{7,5},{8,10},{9,11},{10,... | collective-permute-start | bytes 442376 | tf_op jit(solution)/shard_map/ppermute | solution.py:757
  54.8 9.3 %collective-permute-start.27 = (bf16[16,4608]{1,0:T(8,128)(2,1)S(1)}, bf16[16,4608]{1,0:T(8,128)(2,1)S(1)}, u32[]{:S(2)}, u32[]{:S(2)}) collective-permute-start(bf16[16,4608]{1,0:T(8,128)(2,1)S(1)} %collective-permute-done.26.refs_6_), channel_id=1, source_target_pairs={{0,2},{1,3},{2,0},{3,1},{4,6},{5,7},{6,4},{7,5},{8,10},{9,11},{10,... | collective-permute-start | bytes 442376 | tf_op jit(solution)/shard_map/ppermute | solution.py:757
  67.8 21.0 %collective-permute-start.31 = (bf16[128,4608]{1,0:T(8,128)(2,1)S(1)}, bf16[128,4608]{1,0:T(8,128)(2,1)S(1)}, u32[]{:S(2)}, u32[]{:S(2)}) collective-permute-start(bf16[128,4608]{1,0:T(8,128)(2,1)S(1)} %get-tuple-element.136.x_ref.own_ref), channel_id=1, source_target_pairs={{1,17},{3,19},{5,21},{7,23},{9,25},{11,27},{13,29},{15,31},{16,0},... | collective-permute-start | bytes 3538952 | tf_op jit(solution)/shard_map/ppermute | solution.py:908
  75.3 9.5 %collective-permute-start.35 = (bf16[16,4608]{1,0:T(8,128)(2,1)S(1)}, bf16[16,4608]{1,0:T(8,128)(2,1)S(1)}, u32[]{:S(2)}, u32[]{:S(2)}) collective-permute-start(bf16[16,4608]{1,0:T(8,128)(2,1)S(1)} %get-tuple-element.117), channel_id=1, source_target_pairs={{0,2},{1,3},{2,0},{3,1},{4,6},{5,7},{6,4},{7,5},{8,10},{9,11},{10,... | collective-permute-start | bytes 442376 | tf_op jit(solution)/shard_map/ppermute | solution.py:757
  77.0 11.0 %collective-permute-start.37 = (bf16[16,4608]{1,0:T(8,128)(2,1)S(1)}, bf16[16,4608]{1,0:T(8,128)(2,1)S(1)}, u32[]{:S(2)}, u32[]{:S(2)}) collective-permute-start(bf16[16,4608]{1,0:T(8,128)(2,1)S(1)} %get-tuple-element.119), channel_id=1, source_target_pairs={{0,2},{1,3},{2,0},{3,1},{4,6},{5,7},{6,4},{7,5},{8,10},{9,11},{10,... | collective-permute-start | bytes 442376 | tf_op jit(solution)/shard_map/ppermute | solution.py:757
  77.3 13.2 %collective-permute-start.32 = (bf16[16,4608]{1,0:T(8,128)(2,1)S(1)}, bf16[16,4608]{1,0:T(8,128)(2,1)S(1)}, u32[]{:S(2)}, u32[]{:S(2)}) collective-permute-start(bf16[16,4608]{1,0:T(8,128)(2,1)S(1)} %get-tuple-element.113), channel_id=1, source_target_pairs={{0,2},{1,3},{2,0},{3,1},{4,6},{5,7},{6,4},{7,5},{8,10},{9,11},{10,... | collective-permute-start | bytes 442376 | tf_op jit(solution)/shard_map/ppermute | solution.py:757
  81.7 10.0 %collective-permute-start.34 = (bf16[16,4608]{1,0:T(8,128)(2,1)S(1)}, bf16[16,4608]{1,0:T(8,128)(2,1)S(1)}, u32[]{:S(2)}, u32[]{:S(2)}) collective-permute-start(bf16[16,4608]{1,0:T(8,128)(2,1)S(1)} %shard_map.174), channel_id=1, source_target_pairs={{0,8},{1,9},{2,10},{3,11},{4,12},{5,13},{6,14},{7,15},{8,0},{9,1},... | collective-permute-start | bytes 442376 | tf_op jit(solution)/shard_map/ppermute | solution.py:757
  84.8 8.2 %collective-permute-start.36 = (bf16[16,4608]{1,0:T(8,128)(2,1)S(1)}, bf16[16,4608]{1,0:T(8,128)(2,1)S(1)}, u32[]{:S(2)}, u32[]{:S(2)}) collective-permute-start(bf16[16,4608]{1,0:T(8,128)(2,1)S(1)} %shard_map.175), channel_id=1, source_target_pairs={{0,4},{1,5},{2,6},{3,7},{4,8},{5,9},{6,10},{7,11},{8,12},{9,13},{1... | collective-permute-start | bytes 442376 | tf_op jit(solution)/shard_map/ppermute | solution.py:757
  99.0 10.7 %collective-permute-start.44 = (bf16[128,4608]{1,0:T(8,128)(2,1)S(1)}, bf16[128,4608]{1,0:T(8,128)(2,1)S(1)}, u32[]{:S(2)}, u32[]{:S(2)}) collective-permute-start(bf16[128,4608]{1,0:T(8,128)(2,1)S(1)} %get-tuple-element.136.x_ref.own_ref), channel_id=1, source_target_pairs={{0,1},{1,0},{2,3},{3,2},{4,5},{5,4},{6,7},{7,6},{8,9},{9,8},{10,11... | collective-permute-start | bytes 3538952 | tf_op jit(solution)/shard_map/ppermute | solution.py:757
  110.2 8.5 %collective-permute-start.51 = (bf16[480,128]{1,0:T(8,128)(2,1)S(1)}, bf16[480,128]{1,0:T(8,128)(2,1)S(1)}, u32[]{:S(2)}, u32[]{:S(2)}) collective-permute-start(bf16[480,128]{1,0:T(8,128)(2,1)S(1)} %get-tuple-element.146), channel_id=1, source_target_pairs={{0,2},{1,3},{2,0},{3,1},{4,6},{5,7},{6,4},{7,5},{8,10},{9,11},{10,... | collective-permute-start | bytes 368648 | tf_op jit(solution)/shard_map/ppermute | solution.py:757
  111.9 9.4 %collective-permute-start.49 = (bf16[480,128]{1,0:T(8,128)(2,1)S(1)}, bf16[480,128]{1,0:T(8,128)(2,1)S(1)}, u32[]{:S(2)}, u32[]{:S(2)}) collective-permute-start(bf16[480,128]{1,0:T(8,128)(2,1)S(1)} %get-tuple-element.145), channel_id=1, source_target_pairs={{0,2},{1,3},{2,0},{3,1},{4,6},{5,7},{6,4},{7,5},{8,10},{9,11},{10,... | collective-permute-start | bytes 368648 | tf_op jit(solution)/shard_map/ppermute | solution.py:757
  112.2 16.7 %collective-permute-start.48 = (bf16[13,4,16,384]{3,2,1,0:T(8,128)(2,1)S(1)}, bf16[13,4,16,384]{3,2,1,0:T(8,128)(2,1)S(1)}, u32[]{:S(2)}, u32[]{:S(2)}) collective-permute-start(bf16[13,4,16,384]{3,2,1,0:T(8,128)(2,1)S(1)} %shard_map.182), channel_id=1, source_target_pairs={{0,16},{1,17},{2,18},{3,19},{4,20},{5,21},{6,22},{7,23},{8,24},{9,... | collective-permute-start | bytes 1916936 | tf_op jit(solution)/shard_map/ppermute | solution.py:757
  113.9 14.9 %collective-permute-start.46 = (bf16[480,128]{1,0:T(8,128)(2,1)S(1)}, bf16[480,128]{1,0:T(8,128)(2,1)S(1)}, u32[]{:S(2)}, u32[]{:S(2)}) collective-permute-start(bf16[480,128]{1,0:T(8,128)(2,1)S(1)} %get-tuple-element.139), channel_id=1, source_target_pairs={{0,2},{1,3},{2,0},{3,1},{4,6},{5,7},{6,4},{7,5},{8,10},{9,11},{10,... | collective-permute-start | bytes 368648 | tf_op jit(solution)/shard_map/ppermute | solution.py:757
  116.1 13.6 %collective-permute-start.53 = (bf16[512,128]{1,0:T(8,128)(2,1)S(1)}, bf16[512,128]{1,0:T(8,128)(2,1)S(1)}, u32[]{:S(2)}, u32[]{:S(2)}) collective-permute-start(bf16[512,128]{1,0:T(8,128)(2,1)S(1)} %shard_map.185), channel_id=1, source_target_pairs={{0,12},{1,13},{2,14},{3,15},{4,0},{5,1},{6,2},{7,3},{8,4},{9,5},{1... | collective-permute-start | bytes 393224 | tf_op jit(solution)/shard_map/ppermute | solution.py:757
  118.7 11.0 %collective-permute-start.52 = (bf16[512,128]{1,0:T(8,128)(2,1)S(1)}, bf16[512,128]{1,0:T(8,128)(2,1)S(1)}, u32[]{:S(2)}, u32[]{:S(2)}) collective-permute-start(bf16[512,128]{1,0:T(8,128)(2,1)S(1)} %shard_map.190), channel_id=1, source_target_pairs={{0,8},{1,9},{2,10},{3,11},{4,12},{5,13},{6,14},{7,15},{8,0},{9,1},... | collective-permute-start | bytes 393224 | tf_op jit(solution)/shard_map/ppermute | solution.py:757
  121.3 8.4 %collective-permute-start.50 = (bf16[512,128]{1,0:T(8,128)(2,1)S(1)}, bf16[512,128]{1,0:T(8,128)(2,1)S(1)}, u32[]{:S(2)}, u32[]{:S(2)}) collective-permute-start(bf16[512,128]{1,0:T(8,128)(2,1)S(1)} %shard_map.189), channel_id=1, source_target_pairs={{0,4},{1,5},{2,6},{3,7},{4,8},{5,9},{6,10},{7,11},{8,12},{9,13},{1... | collective-permute-start | bytes 393224 | tf_op jit(solution)/shard_map/ppermute | solution.py:757
  (45 other events, 223.2 us)

commit v3 on v2

--- a/solution.py
+++ b/solution.py
@@ -252,7 +252,7 @@
                 continue
             rows_sum = acts[2 * p] + acts[2 * p + 1] + acts[2 * p + 2]
             for tile in range(channels // 128):
-                sum_ref[p, tile] = rows_sum[:, tile * 128 : (tile + 1) * 128]
+                sum_ref[p, tile, 0:slab, :] = rows_sum[:, tile * 128 : (tile + 1) * 128]
             for q in range(pool):
                 kept = jnp.where(max(p, q) + group < pool, 1.0 / 9.0, 0.0)
                 cell = None
@@ -799,11 +799,11 @@
             shape_of(wide, bf16),
             shape_of((4 * planes, images, units), bf16),
         ),
-        (group, conv_input, cotangent),
+        (after(group, weight_block), conv_input, cotangent),
         scalars=1,
     )
     picture_far = move(picture_send, dx=1)
-    weight_blocks = gather_chips(after(weight_block, picture_send))
+    weight_blocks = gather_chips(weight_block)
     weight_far = [move(block, dc=1) for block in weight_blocks]
     stacked, stacked_t, groups = call(
         functools.partial(widen, place, side),
@@ -834,7 +834,7 @@
             shape_of((chips * chip_rows, channels), bf16),
         ),
         (groups, stacked, conv_bias, *weight_blocks, *weight_far),
-        (pltpu.VMEM((pool, channels // 128, slab, 128), f32),),
+        (pltpu.VMEM((pool, channels // 128, slab + WIDTH, 128), f32),),
     )
 
     pooled_mine = after(pooled_mine, cot_far)
@@ -905,8 +905,8 @@
         low = call(add_rows, (shape_of(piece, bf16),), (kept[k], arrived[k]))[0]
         passed[k] = move(low, dz=-k)
     cross = lambda b, z, y, c: ((b + pairs) % (2 * pairs), z, y, c) if c != b // pairs else None
-    features_x = lax.ppermute(gathered, BOTH, links(cross))
-    x_came = move(after(x_pack, features_x), dx=1)
+    features_x = lax.ppermute(after(gathered, outs[1]), BOTH, links(cross))
+    x_came = move(after(x_pack, passed[order[0]]), dx=1)
     features_c = move(after(gathered, features_x), dc=1)
     d_total, d_mine, d_mine_low, d_other = call(
         functools.partial(block_total, place),

time: 139 us -> 136 us (0.978)
  waiting for transfers between devices: 54.3 us -> 51.2 us
    ppermute x56, waiting for transfers between devices: 53.7 us -> 50.7 us  [move(): return lax.ppermute(value, BOTH, links(where))]
    unnamed x24 -> x26, local copies, waits for them, and re-layouts: 3.28 us -> 3.62 us
  transfers between devices with their start and end apart: 58 -> 58, of which waited for: 30 -> 26; matrix products, arithmetic and copies ran while one was open for 1% -> 1% of each run, Pallas kernels for 18% -> 17%
where the time goes in v3:
time: 136 us
  waiting for transfers between devices  51.2 us (38%)
  starting transfers between devices  51.1 us (38%)
  Pallas kernels  29 us (21%)
  local copies, waits for them, and re-layouts  3.62 us (3%)
    ppermute x56, waiting for transfers between devices, move(): return lax.ppermute(value, BOTH, links(where))  50.7 us
    ppermute x56, starting transfers between devices, move(): return lax.ppermute(value, BOTH, links(where))  45.1 us
    pallas_call x32, Pallas kernels, call(): pl.pallas_call(body, out_shape=out_shape, **steps, in_specs=blocks or [SM...  24.2 us
    pallas_call x1, Pallas kernels, on_device(): pl.pallas_call(functools.partial(fc_grad, place), out_shape=shape_of((2,...  4.8 us
    all_to_all x1, starting transfers between devices, on_device(): lax.all_to_all(cot_send, 'mp', split_axis=0, concat_axis=0, tiled=True)  4.67 us
    unnamed x26, local copies, waits for them, and re-layouts  3.62 us
  transfers between devices with their start and end apart: 58, of which 26 were waited for; matrix products, arithmetic and copies ran while one was open for 1% of the time, Pallas kernels for 17%

profile of v3, /device:TPU:0, one launch (start us, length us, event | category | flops | bytes accessed | tf_op | source)
XLA Modules:
  0.0 136.1 jit_solution(5995673876919526397)
XLA Ops:
  4.6 2.9 %collective-permute-start.1 = (bf16[13,4,16,384]{3,2,1,0:T(8,128)(2,1)S(1)}, bf16[13,4,16,384]{3,2,1,0:T(8,128)(2,1)S(1)}, u32[]{:S(2)}, u32[]{:S(2)}) collective-permute-start(bf16[13,4,16,384]{3,2,1,0:T(8,128)(2,1)S(1)} %get-tuple-element.88), channel_id=1, source_target_pairs={{0,16},{1,17},{2,18},{3,19},{4,20},{5,21},{6,22},{7,23},{8,24},{9,... | collective-permute-start | bytes 1916936 | tf_op jit(solution)/shard_map/ppermute | solution.py:757
  10.6 2.2 %collective-permute-start.7 = (bf16[432,128]{1,0:T(8,128)(2,1)S(1)}, bf16[432,128]{1,0:T(8,128)(2,1)S(1)}, u32[]{:S(2)}, u32[]{:S(2)}) collective-permute-start(bf16[432,128]{1,0:T(8,128)(2,1)S(1)} %shard_map.162.refs_3_), channel_id=1, source_target_pairs={{0,12},{1,13},{2,14},{3,15},{4,0},{5,1},{6,2},{7,3},{8,4},{9,5},{1... | collective-permute-start | bytes 331784 | tf_op jit(solution)/shard_map/ppermute | solution.py:757
  13.7 4.7 %all-to-all-start = ((bf16[16,8,256]{2,1,0:T(8,128)(2,1)}), bf16[16,8,256]{2,1,0:T(8,128)(2,1)S(1)}, u32[]{:S(2)}, u32[]{:S(2)}) async-start(bf16[16,8,256]{2,1,0:T(8,128)(2,1)} %get-tuple-element.96), calls=%async_computation | async-start | bytes 131072 | tf_op jit(solution)/shard_map/all_to_all | solution.py:819
  20.5 2.1 %collective-permute-done.5.refs_7_ = bf16[432,128]{1,0:T(8,128)(2,1)S(1)} collective-permute-done((bf16[432,128]{1,0:T(8,128)(2,1)S(1)}, bf16[432,128]{1,0:T(8,128)(2,1)S(1)}, u32[]{:S(2)}, u32[]{:S(2)}) %collective-permute-start.5) | collective-permute-done | bytes 110624 | tf_op jit(solution)/shard_map/ppermute | solution.py:757
  25.9 2.7 %collective-permute-done.6.refs_8_ = bf16[432,128]{1,0:T(8,128)(2,1)S(1)} collective-permute-done((bf16[432,128]{1,0:T(8,128)(2,1)S(1)}, bf16[432,128]{1,0:T(8,128)(2,1)S(1)}, u32[]{:S(2)}, u32[]{:S(2)}) %collective-permute-start.6) | collective-permute-done | bytes 110624 | tf_op jit(solution)/shard_map/ppermute | solution.py:757
  28.5 2.0 %collective-permute-done.4.refs_6_ = bf16[432,128]{1,0:T(8,128)(2,1)S(1)} collective-permute-done((bf16[432,128]{1,0:T(8,128)(2,1)S(1)}, bf16[432,128]{1,0:T(8,128)(2,1)S(1)}, u32[]{:S(2)}, u32[]{:S(2)}) %collective-permute-start.4) | collective-permute-done | bytes 110624 | tf_op jit(solution)/shard_map/ppermute | solution.py:757
  30.5 1.9 %shard_map.164 = (bf16[1920,1152]{1,0:T(8,128)(2,1)S(1)}, bf16[1152,1920]{1,0:T(8,128)(2,1)S(1)}, f32[8,256]{1,0:T(8,128)S(1)}) custom-call(bf16[13,4,16,384]{3,2,1,0:T(8,128)(2,1)S(1)} %get-tuple-element.87.own_ref, bf16[13,4,16,384]{3,2,1,0:T(8,128)(2,1)S(1)} %collective-permute-done.1.far_ref), custom_call_target="tpu_custom_call" | custom-call | flops 2200000000 | bytes 1 | tf_op jit(solution)/shard_map/pallas_call | solution.py:79
  33.1 4.1 %shard_map.165 = (f32[1664,256]{1,0:T(8,128)S(1)}, bf16[8,4608]{1,0:T(8,128)(2,1)S(1)}, bf16[8,4608]{1,0:T(8,128)(2,1)S(1)}, bf16[3456,256]{1,0:T(8,128)(2,1)S(1)}) custom-call(f32[8,256]{1,0:T(8,128)S(1)} %get-tuple-element.90.refs_0_, bf16[1920,1152]{1,0:T(8,128)(2,1)S(1)} %get-tuple-element.92.refs_1_, f32[2,256]{1,0:T(2,128)S(1)} %copy-done.4, ...), custom_call_target="tpu_custom_call" | custom-call | flops 8249999872 | bytes 1 | tf_op jit(solution)/shard_map/pallas_call | solution.py:79
  40.1 2.0 %collective-permute-done.20.xc_ref = bf16[8,4608]{1,0:T(8,128)(2,1)S(1)} collective-permute-done((bf16[8,4608]{1,0:T(8,128)(2,1)S(1)}, bf16[8,4608]{1,0:T(8,128)(2,1)S(1)}, u32[]{:S(2)}, u32[]{:S(2)}) %collective-permute-start.20) | collective-permute-done | bytes 73760 | tf_op jit(solution)/shard_map/ppermute | solution.py:757
  46.1 2.6 %collective-permute-start.26 = (bf16[16,4608]{1,0:T(8,128)(2,1)S(1)}, bf16[16,4608]{1,0:T(8,128)(2,1)S(1)}, u32[]{:S(2)}, u32[]{:S(2)}) collective-permute-start(bf16[16,4608]{1,0:T(8,128)(2,1)S(1)} %shard_map.166.refs_0_), channel_id=1, source_target_pairs={{0,12},{1,13},{2,14},{3,15},{4,0},{5,1},{6,2},{7,3},{8,4},{9,5},{1... | collective-permute-start | bytes 442376 | tf_op jit(solution)/shard_map/ppermute | solution.py:757
  48.9 3.9 %collective-permute-done.22.refs_2_ = bf16[16,4608]{1,0:T(8,128)(2,1)S(1)} collective-permute-done((bf16[16,4608]{1,0:T(8,128)(2,1)S(1)}, bf16[16,4608]{1,0:T(8,128)(2,1)S(1)}, u32[]{:S(2)}, u32[]{:S(2)}) %collective-permute-start.22) | collective-permute-done | bytes 147488 | tf_op jit(solution)/shard_map/ppermute | solution.py:757
  55.1 5.7 %collective-permute-done.24.refs_4_ = bf16[16,4608]{1,0:T(8,128)(2,1)S(1)} collective-permute-done((bf16[16,4608]{1,0:T(8,128)(2,1)S(1)}, bf16[16,4608]{1,0:T(8,128)(2,1)S(1)}, u32[]{:S(2)}, u32[]{:S(2)}) %collective-permute-start.24) | collective-permute-done | bytes 147488 | tf_op jit(solution)/shard_map/ppermute | solution.py:757
  63.2 3.2 %collective-permute-done.25.refs_5_ = bf16[16,4608]{1,0:T(8,128)(2,1)S(1)} collective-permute-done((bf16[16,4608]{1,0:T(8,128)(2,1)S(1)}, bf16[16,4608]{1,0:T(8,128)(2,1)S(1)}, u32[]{:S(2)}, u32[]{:S(2)}) %collective-permute-start.25) | collective-permute-done | bytes 147488 | tf_op jit(solution)/shard_map/ppermute | solution.py:757
  78.2 3.0 %collective-permute-done.35.got_ref = bf16[16,4608]{1,0:T(8,128)(2,1)S(1)} collective-permute-done((bf16[16,4608]{1,0:T(8,128)(2,1)S(1)}, bf16[16,4608]{1,0:T(8,128)(2,1)S(1)}, u32[]{:S(2)}, u32[]{:S(2)}) %collective-permute-start.35) | collective-permute-done | bytes 147488 | tf_op jit(solution)/shard_map/ppermute | solution.py:757
  81.3 3.0 %collective-permute-done.37.got_ref = bf16[16,4608]{1,0:T(8,128)(2,1)S(1)} collective-permute-done((bf16[16,4608]{1,0:T(8,128)(2,1)S(1)}, bf16[16,4608]{1,0:T(8,128)(2,1)S(1)}, u32[]{:S(2)}, u32[]{:S(2)}) %collective-permute-start.37) | collective-permute-done | bytes 147488 | tf_op jit(solution)/shard_map/ppermute | solution.py:757
  85.2 4.1 %collective-permute-done.34.refs_1_ = bf16[16,4608]{1,0:T(8,128)(2,1)S(1)} collective-permute-done((bf16[16,4608]{1,0:T(8,128)(2,1)S(1)}, bf16[16,4608]{1,0:T(8,128)(2,1)S(1)}, u32[]{:S(2)}, u32[]{:S(2)}) %collective-permute-start.34) | collective-permute-done | bytes 147488 | tf_op jit(solution)/shard_map/ppermute | solution.py:757
  89.4 4.0 %collective-permute-start.42 = (bf16[208,256]{1,0:T(8,128)(2,1)S(1)}, bf16[208,256]{1,0:T(8,128)(2,1)S(1)}, u32[]{:S(2)}, u32[]{:S(2)}) collective-permute-start(bf16[208,256]{1,0:T(8,128)(2,1)S(1)} %get-tuple-element.128), channel_id=1, source_target_pairs={{0,16},{1,17},{2,18},{3,19},{4,20},{5,21},{6,22},{7,23},{8,24},{9,... | collective-permute-start | bytes 319496 | tf_op jit(solution)/shard_map/ppermute | solution.py:757
  100.8 3.6 %shard_map.181 = (f32[8,448,128]{2,1,0:T(8,128)S(1)}, bf16[8,448,128]{2,1,0:T(8,128)(2,1)S(1)}) custom-call(bf16[1152,1920]{1,0:T(8,128)(2,1)S(1)} %get-tuple-element.89.xt_ref, bf16[1664,256]{1,0:T(8,128)(2,1)S(1)} %get-tuple-element.145.d_ref, f32[1,256]{1,0:T(1,128)S(1)} %get-tuple-element.132.bias_ref, f32[8,256]{1,0:T(8,128)S(1)} %shard_map.180.st_ref), custom_call_target="tpu_custom_call" | custom-call | flops 4070000128 | bytes 1 | tf_op jit(solution)/shard_map/pallas_call | solution.py:79
  105.0 2.1 %shard_map.182 = bf16[13,4,16,384]{3,2,1,0:T(8,128)(2,1)S(1)} custom-call(bf16[1664,256]{1,0:T(8,128)(2,1)S(1)} %get-tuple-element.145.d_ref, bf16[2304,384]{1,0:T(8,128)(2,1)S(1)} %get-tuple-element.106.w_ref), custom_call_target="tpu_custom_call" | custom-call | flops 2420000000 | bytes 1 | tf_op jit(solution)/shard_map/pallas_call | solution.py:79
  113.6 2.5 %collective-permute-done.51.came_ref = bf16[480,128]{1,0:T(8,128)(2,1)S(1)} collective-permute-done((bf16[480,128]{1,0:T(8,128)(2,1)S(1)}, bf16[480,128]{1,0:T(8,128)(2,1)S(1)}, u32[]{:S(2)}, u32[]{:S(2)}) %collective-permute-start.51) | collective-permute-done | bytes 122912 | tf_op jit(solution)/shard_map/ppermute | solution.py:757
  116.7 2.1 %collective-permute-done.49.came_ref = bf16[480,128]{1,0:T(8,128)(2,1)S(1)} collective-permute-done((bf16[480,128]{1,0:T(8,128)(2,1)S(1)}, bf16[480,128]{1,0:T(8,128)(2,1)S(1)}, u32[]{:S(2)}, u32[]{:S(2)}) %collective-permute-start.49) | collective-permute-done | bytes 122912 | tf_op jit(solution)/shard_map/ppermute | solution.py:757
  119.6 4.8 %shard_map.186 = f32[2,4608,256]{2,1,0:T(8,128)} custom-call(bf16[128,4608]{1,0:T(8,128)(2,1)S(1)} %get-tuple-element.138.x_ref.own_ref, bf16[128,4608]{1,0:T(8,128)(2,1)S(1)} %collective-permute-done.44.oc_ref, bf16[128,4608]{1,0:T(8,128)(2,1)S(1)} %collective-permute-done.31.x_ref, bf16[128,4608]{1,0:T(8,128)(2,1)S(1)} %collective-permute-done.45.xc_ref, ...), custom_call_target="tpu_custom_call" | custom-call | flops 5280000000 | bytes 1 | tf_op jit(solution)/shard_map/pallas_call | solution.py:1002
  124.4 2.2 %shard_map.187.own_ref = bf16[13,4,16,384]{3,2,1,0:T(8,128)(2,1)S(1)} custom-call(bf16[1664,256]{1,0:T(8,128)(2,1)S(1)} %get-tuple-element.145.d_ref, bf16[2304,384]{1,0:T(8,128)(2,1)S(1)} %get-tuple-element.106.w_ref), custom_call_target="tpu_custom_call" | custom-call | flops 2420000000 | bytes 1 | tf_op jit(solution)/shard_map/pallas_call | solution.py:79
  133.3 2.0 %collective-permute-done.55.x_ref = bf16[240,128]{1,0:T(8,128)(2,1)S(1)} collective-permute-done((bf16[240,128]{1,0:T(8,128)(2,1)S(1)}, bf16[240,128]{1,0:T(8,128)(2,1)S(1)}, u32[]{:S(2)}, u32[]{:S(2)}) %collective-permute-start.55) | collective-permute-done | bytes 61472 | tf_op jit(solution)/shard_map/ppermute | solution.py:757
  (152 shorter events, 61.3 us)
Async XLA Ops:
  4.6 18.4 %collective-permute-start.1 = (bf16[13,4,16,384]{3,2,1,0:T(8,128)(2,1)S(1)}, bf16[13,4,16,384]{3,2,1,0:T(8,128)(2,1)S(1)}, u32[]{:S(2)}, u32[]{:S(2)}) collective-permute-start(bf16[13,4,16,384]{3,2,1,0:T(8,128)(2,1)S(1)} %get-tuple-element.88), channel_id=1, source_target_pairs={{0,16},{1,17},{2,18},{3,19},{4,20},{5,21},{6,22},{7,23},{8,24},{9,... | collective-permute-start | bytes 1916936 | tf_op jit(solution)/shard_map/ppermute | solution.py:757
  9.1 9.3 %collective-permute-start.3 = (bf16[432,128]{1,0:T(8,128)(2,1)S(1)}, bf16[432,128]{1,0:T(8,128)(2,1)S(1)}, u32[]{:S(2)}, u32[]{:S(2)}) collective-permute-start(bf16[432,128]{1,0:T(8,128)(2,1)S(1)} %shard_map.162.refs_3_), channel_id=1, source_target_pairs={{0,4},{1,5},{2,6},{3,7},{4,8},{5,9},{6,10},{7,11},{8,12},{9,13},{1... | collective-permute-start | bytes 331784 | tf_op jit(solution)/shard_map/ppermute | solution.py:757
  12.9 9.8 %collective-permute-start.5 = (bf16[432,128]{1,0:T(8,128)(2,1)S(1)}, bf16[432,128]{1,0:T(8,128)(2,1)S(1)}, u32[]{:S(2)}, u32[]{:S(2)}) collective-permute-start(bf16[432,128]{1,0:T(8,128)(2,1)S(1)} %shard_map.162.refs_3_), channel_id=1, source_target_pairs={{0,8},{1,9},{2,10},{3,11},{4,12},{5,13},{6,14},{7,15},{8,0},{9,1},... | collective-permute-start | bytes 331784 | tf_op jit(solution)/shard_map/ppermute | solution.py:757
  13.7 9.0 %collective-permute-start.9 = (bf16[432,128]{1,0:T(8,128)(2,1)S(1)}, bf16[432,128]{1,0:T(8,128)(2,1)S(1)}, u32[]{:S(2)}, u32[]{:S(2)}) collective-permute-start(bf16[432,128]{1,0:T(8,128)(2,1)S(1)} %shard_map.162.refs_3_), channel_id=1, source_target_pairs={{0,1},{1,0},{2,3},{3,2},{4,5},{5,4},{6,7},{7,6},{8,9},{9,8},{10,11... | collective-permute-start | bytes 331784 | tf_op jit(solution)/shard_map/ppermute | solution.py:757
  13.7 11.6 %all-to-all-start = ((bf16[16,8,256]{2,1,0:T(8,128)(2,1)}), bf16[16,8,256]{2,1,0:T(8,128)(2,1)S(1)}, u32[]{:S(2)}, u32[]{:S(2)}) async-start(bf16[16,8,256]{2,1,0:T(8,128)(2,1)} %get-tuple-element.96), calls=%async_computation | async-start | bytes 131072 | tf_op jit(solution)/shard_map/all_to_all | solution.py:819
  37.7 25.5 %collective-permute-start.28 = (bf16[4608,256]{1,0:T(8,128)(2,1)S(1)}, bf16[4608,256]{1,0:T(8,128)(2,1)S(1)}, u32[]{:S(2)}, u32[]{:S(2)}) collective-permute-start(bf16[4608,256]{1,0:T(8,128)(2,1)S(1)} %get-tuple-element.102), channel_id=1, source_target_pairs={{0,1},{1,0},{2,3},{3,2},{4,5},{5,4},{6,7},{7,6},{8,9},{9,8},{10,11... | collective-permute-start | bytes 7077896 | tf_op jit(solution)/shard_map/ppermute | solution.py:757
  44.2 8.6 %collective-permute-start.22 = (bf16[16,4608]{1,0:T(8,128)(2,1)S(1)}, bf16[16,4608]{1,0:T(8,128)(2,1)S(1)}, u32[]{:S(2)}, u32[]{:S(2)}) collective-permute-start(bf16[16,4608]{1,0:T(8,128)(2,1)S(1)} %shard_map.166.refs_0_), channel_id=1, source_target_pairs={{0,4},{1,5},{2,6},{3,7},{4,8},{5,9},{6,10},{7,11},{8,12},{9,13},{1... | collective-permute-start | bytes 442376 | tf_op jit(solution)/shard_map/ppermute | solution.py:757
  48.7 12.1 %collective-permute-start.24 = (bf16[16,4608]{1,0:T(8,128)(2,1)S(1)}, bf16[16,4608]{1,0:T(8,128)(2,1)S(1)}, u32[]{:S(2)}, u32[]{:S(2)}) collective-permute-start(bf16[16,4608]{1,0:T(8,128)(2,1)S(1)} %shard_map.166.refs_0_), channel_id=1, source_target_pairs={{0,8},{1,9},{2,10},{3,11},{4,12},{5,13},{6,14},{7,15},{8,0},{9,1},... | collective-permute-start | bytes 442376 | tf_op jit(solution)/shard_map/ppermute | solution.py:757
  52.8 13.6 %collective-permute-start.23 = (bf16[16,4608]{1,0:T(8,128)(2,1)S(1)}, bf16[16,4608]{1,0:T(8,128)(2,1)S(1)}, u32[]{:S(2)}, u32[]{:S(2)}) collective-permute-start(bf16[16,4608]{1,0:T(8,128)(2,1)S(1)} %collective-permute-done.22.refs_2_), channel_id=1, source_target_pairs={{0,2},{1,3},{2,0},{3,1},{4,6},{5,7},{6,4},{7,5},{8,10},{9,11},{10,... | collective-permute-start | bytes 442376 | tf_op jit(solution)/shard_map/ppermute | solution.py:757
  54.0 9.2 %collective-permute-start.27 = (bf16[16,4608]{1,0:T(8,128)(2,1)S(1)}, bf16[16,4608]{1,0:T(8,128)(2,1)S(1)}, u32[]{:S(2)}, u32[]{:S(2)}) collective-permute-start(bf16[16,4608]{1,0:T(8,128)(2,1)S(1)} %collective-permute-done.26.refs_6_), channel_id=1, source_target_pairs={{0,2},{1,3},{2,0},{3,1},{4,6},{5,7},{6,4},{7,5},{8,10},{9,11},{10,... | collective-permute-start | bytes 442376 | tf_op jit(solution)/shard_map/ppermute | solution.py:757
  71.5 21.8 %collective-permute-start.31 = (bf16[128,4608]{1,0:T(8,128)(2,1)S(1)}, bf16[128,4608]{1,0:T(8,128)(2,1)S(1)}, u32[]{:S(2)}, u32[]{:S(2)}) collective-permute-start(bf16[128,4608]{1,0:T(8,128)(2,1)S(1)} %get-tuple-element.138.x_ref.own_ref), channel_id=1, source_target_pairs={{1,17},{3,19},{5,21},{7,23},{9,25},{11,27},{13,29},{15,31},{16,0},... | collective-permute-start | bytes 3538952 | tf_op jit(solution)/shard_map/ppermute | solution.py:908
  73.2 8.0 %collective-permute-start.35 = (bf16[16,4608]{1,0:T(8,128)(2,1)S(1)}, bf16[16,4608]{1,0:T(8,128)(2,1)S(1)}, u32[]{:S(2)}, u32[]{:S(2)}) collective-permute-start(bf16[16,4608]{1,0:T(8,128)(2,1)S(1)} %get-tuple-element.119), channel_id=1, source_target_pairs={{0,2},{1,3},{2,0},{3,1},{4,6},{5,7},{6,4},{7,5},{8,10},{9,11},{10,... | collective-permute-start | bytes 442376 | tf_op jit(solution)/shard_map/ppermute | solution.py:757
  74.9 9.5 %collective-permute-start.37 = (bf16[16,4608]{1,0:T(8,128)(2,1)S(1)}, bf16[16,4608]{1,0:T(8,128)(2,1)S(1)}, u32[]{:S(2)}, u32[]{:S(2)}) collective-permute-start(bf16[16,4608]{1,0:T(8,128)(2,1)S(1)} %get-tuple-element.121), channel_id=1, source_target_pairs={{0,2},{1,3},{2,0},{3,1},{4,6},{5,7},{6,4},{7,5},{8,10},{9,11},{10,... | collective-permute-start | bytes 442376 | tf_op jit(solution)/shard_map/ppermute | solution.py:757
  75.3 18.1 %collective-permute-start.32 = (bf16[16,4608]{1,0:T(8,128)(2,1)S(1)}, bf16[16,4608]{1,0:T(8,128)(2,1)S(1)}, u32[]{:S(2)}, u32[]{:S(2)}) collective-permute-start(bf16[16,4608]{1,0:T(8,128)(2,1)S(1)} %get-tuple-element.113), channel_id=1, source_target_pairs={{0,2},{1,3},{2,0},{3,1},{4,6},{5,7},{6,4},{7,5},{8,10},{9,11},{10,... | collective-permute-start | bytes 442376 | tf_op jit(solution)/shard_map/ppermute | solution.py:757
  78.1 11.3 %collective-permute-start.34 = (bf16[16,4608]{1,0:T(8,128)(2,1)S(1)}, bf16[16,4608]{1,0:T(8,128)(2,1)S(1)}, u32[]{:S(2)}, u32[]{:S(2)}) collective-permute-start(bf16[16,4608]{1,0:T(8,128)(2,1)S(1)} %shard_map.174), channel_id=1, source_target_pairs={{0,8},{1,9},{2,10},{3,11},{4,12},{5,13},{6,14},{7,15},{8,0},{9,1},... | collective-permute-start | bytes 442376 | tf_op jit(solution)/shard_map/ppermute | solution.py:757
  81.3 12.1 %collective-permute-start.36 = (bf16[16,4608]{1,0:T(8,128)(2,1)S(1)}, bf16[16,4608]{1,0:T(8,128)(2,1)S(1)}, u32[]{:S(2)}, u32[]{:S(2)}) collective-permute-start(bf16[16,4608]{1,0:T(8,128)(2,1)S(1)} %shard_map.175), channel_id=1, source_target_pairs={{0,4},{1,5},{2,6},{3,7},{4,8},{5,9},{6,10},{7,11},{8,12},{9,13},{1... | collective-permute-start | bytes 442376 | tf_op jit(solution)/shard_map/ppermute | solution.py:757
  84.4 9.4 %collective-permute-start.38 = (bf16[16,4608]{1,0:T(8,128)(2,1)S(1)}, bf16[16,4608]{1,0:T(8,128)(2,1)S(1)}, u32[]{:S(2)}, u32[]{:S(2)}) collective-permute-start(bf16[16,4608]{1,0:T(8,128)(2,1)S(1)} %shard_map.176), channel_id=1, source_target_pairs={{0,12},{1,13},{2,14},{3,15},{4,0},{5,1},{6,2},{7,3},{8,4},{9,5},{1... | collective-permute-start | bytes 442376 | tf_op jit(solution)/shard_map/ppermute | solution.py:757
  95.9 11.3 %collective-permute-start.44 = (bf16[128,4608]{1,0:T(8,128)(2,1)S(1)}, bf16[128,4608]{1,0:T(8,128)(2,1)S(1)}, u32[]{:S(2)}, u32[]{:S(2)}) collective-permute-start(bf16[128,4608]{1,0:T(8,128)(2,1)S(1)} %get-tuple-element.138.x_ref.own_ref), channel_id=1, source_target_pairs={{0,1},{1,0},{2,3},{3,2},{4,5},{5,4},{6,7},{7,6},{8,9},{9,8},{10,11... | collective-permute-start | bytes 3538952 | tf_op jit(solution)/shard_map/ppermute | solution.py:757
  109.3 9.4 %collective-permute-start.49 = (bf16[480,128]{1,0:T(8,128)(2,1)S(1)}, bf16[480,128]{1,0:T(8,128)(2,1)S(1)}, u32[]{:S(2)}, u32[]{:S(2)}) collective-permute-start(bf16[480,128]{1,0:T(8,128)(2,1)S(1)} %get-tuple-element.147), channel_id=1, source_target_pairs={{0,2},{1,3},{2,0},{3,1},{4,6},{5,7},{6,4},{7,5},{8,10},{9,11},{10,... | collective-permute-start | bytes 368648 | tf_op jit(solution)/shard_map/ppermute | solution.py:757
  111.1 15.7 %collective-permute-start.48 = (bf16[13,4,16,384]{3,2,1,0:T(8,128)(2,1)S(1)}, bf16[13,4,16,384]{3,2,1,0:T(8,128)(2,1)S(1)}, u32[]{:S(2)}, u32[]{:S(2)}) collective-permute-start(bf16[13,4,16,384]{3,2,1,0:T(8,128)(2,1)S(1)} %shard_map.182), channel_id=1, source_target_pairs={{0,16},{1,17},{2,18},{3,19},{4,20},{5,21},{6,22},{7,23},{8,24},{9,... | collective-permute-start | bytes 1916936 | tf_op jit(solution)/shard_map/ppermute | solution.py:757
  111.9 14.6 %collective-permute-start.46 = (bf16[480,128]{1,0:T(8,128)(2,1)S(1)}, bf16[480,128]{1,0:T(8,128)(2,1)S(1)}, u32[]{:S(2)}, u32[]{:S(2)}) collective-permute-start(bf16[480,128]{1,0:T(8,128)(2,1)S(1)} %get-tuple-element.141), channel_id=1, source_target_pairs={{0,2},{1,3},{2,0},{3,1},{4,6},{5,7},{6,4},{7,5},{8,10},{9,11},{10,... | collective-permute-start | bytes 368648 | tf_op jit(solution)/shard_map/ppermute | solution.py:757
  113.5 14.1 %collective-permute-start.53 = (bf16[512,128]{1,0:T(8,128)(2,1)S(1)}, bf16[512,128]{1,0:T(8,128)(2,1)S(1)}, u32[]{:S(2)}, u32[]{:S(2)}) collective-permute-start(bf16[512,128]{1,0:T(8,128)(2,1)S(1)} %shard_map.185), channel_id=1, source_target_pairs={{0,12},{1,13},{2,14},{3,15},{4,0},{5,1},{6,2},{7,3},{8,4},{9,5},{1... | collective-permute-start | bytes 393224 | tf_op jit(solution)/shard_map/ppermute | solution.py:757
  116.1 11.5 %collective-permute-start.52 = (bf16[512,128]{1,0:T(8,128)(2,1)S(1)}, bf16[512,128]{1,0:T(8,128)(2,1)S(1)}, u32[]{:S(2)}, u32[]{:S(2)}) collective-permute-start(bf16[512,128]{1,0:T(8,128)(2,1)S(1)} %shard_map.190), channel_id=1, source_target_pairs={{0,8},{1,9},{2,10},{3,11},{4,12},{5,13},{6,14},{7,15},{8,0},{9,1},... | collective-permute-start | bytes 393224 | tf_op jit(solution)/shard_map/ppermute | solution.py:757
  118.8 8.8 %collective-permute-start.50 = (bf16[512,128]{1,0:T(8,128)(2,1)S(1)}, bf16[512,128]{1,0:T(8,128)(2,1)S(1)}, u32[]{:S(2)}, u32[]{:S(2)}) collective-permute-start(bf16[512,128]{1,0:T(8,128)(2,1)S(1)} %shard_map.189), channel_id=1, source_target_pairs={{0,4},{1,5},{2,6},{3,7},{4,8},{5,9},{6,10},{7,11},{8,12},{9,13},{1... | collective-permute-start | bytes 393224 | tf_op jit(solution)/shard_map/ppermute | solution.py:757
  (46 other events, 221.7 us)

commit v4 on v3

--- a/solution.py
+++ b/solution.py
@@ -932,7 +932,7 @@
     stitch_sums = call(
         functools.partial(stitch_terms, place),
         shape_of((8, channels), f32),
-        (after(d_total, d_other), *pooled),
+        (d_total, *pooled),
     )
     d_conv, d_bias = call(
         functools.partial(conv_slope, place, side, pool, images),

time: 136 us -> 136 us (level)
  no operation moved by 1% of the time
where the time goes in v4:
time: 136 us
  waiting for transfers between devices  51.2 us (38%)
  starting transfers between devices  51.1 us (38%)
  Pallas kernels  29 us (21%)
  local copies, waits for them, and re-layouts  3.62 us (3%)
    ppermute x56, waiting for transfers between devices, move(): return lax.ppermute(value, BOTH, links(where))  50.7 us
    ppermute x56, starting transfers between devices, move(): return lax.ppermute(value, BOTH, links(where))  45.1 us
    pallas_call x32, Pallas kernels, call(): pl.pallas_call(body, out_shape=out_shape, **steps, in_specs=blocks or [SM...  24.2 us
    pallas_call x1, Pallas kernels, on_device(): pl.pallas_call(functools.partial(fc_grad, place), out_shape=shape_of((2,...  4.8 us
    all_to_all x1, starting transfers between devices, on_device(): lax.all_to_all(cot_send, 'mp', split_axis=0, concat_axis=0, tiled=True)  4.67 us
    unnamed x26, local copies, waits for them, and re-layouts  3.62 us
  transfers between devices with their start and end apart: 58, of which 26 were waited for; matrix products, arithmetic and copies ran while one was open for 1% of the time, Pallas kernels for 17%

profile of v4, /device:TPU:0, one launch (start us, length us, event | category | flops | bytes accessed | tf_op | source)
XLA Modules:
  0.0 136.1 jit_solution(5995673876919526397)
XLA Ops:
  4.6 2.9 %collective-permute-start.1 = (bf16[13,4,16,384]{3,2,1,0:T(8,128)(2,1)S(1)}, bf16[13,4,16,384]{3,2,1,0:T(8,128)(2,1)S(1)}, u32[]{:S(2)}, u32[]{:S(2)}) collective-permute-start(bf16[13,4,16,384]{3,2,1,0:T(8,128)(2,1)S(1)} %get-tuple-element.87), channel_id=1, source_target_pairs={{0,16},{1,17},{2,18},{3,19},{4,20},{5,21},{6,22},{7,23},{8,24},{9,... | collective-permute-start | bytes 1916936 | tf_op jit(solution)/shard_map/ppermute | solution.py:757
  10.6 2.2 %collective-permute-start.7 = (bf16[432,128]{1,0:T(8,128)(2,1)S(1)}, bf16[432,128]{1,0:T(8,128)(2,1)S(1)}, u32[]{:S(2)}, u32[]{:S(2)}) collective-permute-start(bf16[432,128]{1,0:T(8,128)(2,1)S(1)} %shard_map.162.refs_3_), channel_id=1, source_target_pairs={{0,12},{1,13},{2,14},{3,15},{4,0},{5,1},{6,2},{7,3},{8,4},{9,5},{1... | collective-permute-start | bytes 331784 | tf_op jit(solution)/shard_map/ppermute | solution.py:757
  13.7 4.7 %all-to-all-start = ((bf16[16,8,256]{2,1,0:T(8,128)(2,1)}), bf16[16,8,256]{2,1,0:T(8,128)(2,1)S(1)}, u32[]{:S(2)}, u32[]{:S(2)}) async-start(bf16[16,8,256]{2,1,0:T(8,128)(2,1)} %get-tuple-element.95), calls=%async_computation | async-start | bytes 131072 | tf_op jit(solution)/shard_map/all_to_all | solution.py:819
  20.5 2.1 %collective-permute-done.5.refs_7_ = bf16[432,128]{1,0:T(8,128)(2,1)S(1)} collective-permute-done((bf16[432,128]{1,0:T(8,128)(2,1)S(1)}, bf16[432,128]{1,0:T(8,128)(2,1)S(1)}, u32[]{:S(2)}, u32[]{:S(2)}) %collective-permute-start.5) | collective-permute-done | bytes 110624 | tf_op jit(solution)/shard_map/ppermute | solution.py:757
  25.9 2.7 %collective-permute-done.6.refs_8_ = bf16[432,128]{1,0:T(8,128)(2,1)S(1)} collective-permute-done((bf16[432,128]{1,0:T(8,128)(2,1)S(1)}, bf16[432,128]{1,0:T(8,128)(2,1)S(1)}, u32[]{:S(2)}, u32[]{:S(2)}) %collective-permute-start.6) | collective-permute-done | bytes 110624 | tf_op jit(solution)/shard_map/ppermute | solution.py:757
  28.5 2.0 %collective-permute-done.4.refs_6_ = bf16[432,128]{1,0:T(8,128)(2,1)S(1)} collective-permute-done((bf16[432,128]{1,0:T(8,128)(2,1)S(1)}, bf16[432,128]{1,0:T(8,128)(2,1)S(1)}, u32[]{:S(2)}, u32[]{:S(2)}) %collective-permute-start.4) | collective-permute-done | bytes 110624 | tf_op jit(solution)/shard_map/ppermute | solution.py:757
  30.5 1.9 %shard_map.164 = (bf16[1920,1152]{1,0:T(8,128)(2,1)S(1)}, bf16[1152,1920]{1,0:T(8,128)(2,1)S(1)}, f32[8,256]{1,0:T(8,128)S(1)}) custom-call(bf16[13,4,16,384]{3,2,1,0:T(8,128)(2,1)S(1)} %get-tuple-element.86.own_ref, bf16[13,4,16,384]{3,2,1,0:T(8,128)(2,1)S(1)} %collective-permute-done.1.far_ref), custom_call_target="tpu_custom_call" | custom-call | flops 2200000000 | bytes 1 | tf_op jit(solution)/shard_map/pallas_call | solution.py:79
  33.1 4.1 %shard_map.165 = (f32[1664,256]{1,0:T(8,128)S(1)}, bf16[8,4608]{1,0:T(8,128)(2,1)S(1)}, bf16[8,4608]{1,0:T(8,128)(2,1)S(1)}, bf16[3456,256]{1,0:T(8,128)(2,1)S(1)}) custom-call(f32[8,256]{1,0:T(8,128)S(1)} %get-tuple-element.89.refs_0_, bf16[1920,1152]{1,0:T(8,128)(2,1)S(1)} %get-tuple-element.91.refs_1_, f32[2,256]{1,0:T(2,128)S(1)} %copy-done.4, ...), custom_call_target="tpu_custom_call" | custom-call | flops 8249999872 | bytes 1 | tf_op jit(solution)/shard_map/pallas_call | solution.py:79
  40.1 2.0 %collective-permute-done.20.xc_ref = bf16[8,4608]{1,0:T(8,128)(2,1)S(1)} collective-permute-done((bf16[8,4608]{1,0:T(8,128)(2,1)S(1)}, bf16[8,4608]{1,0:T(8,128)(2,1)S(1)}, u32[]{:S(2)}, u32[]{:S(2)}) %collective-permute-start.20) | collective-permute-done | bytes 73760 | tf_op jit(solution)/shard_map/ppermute | solution.py:757
  46.1 2.6 %collective-permute-start.26 = (bf16[16,4608]{1,0:T(8,128)(2,1)S(1)}, bf16[16,4608]{1,0:T(8,128)(2,1)S(1)}, u32[]{:S(2)}, u32[]{:S(2)}) collective-permute-start(bf16[16,4608]{1,0:T(8,128)(2,1)S(1)} %shard_map.166.refs_0_), channel_id=1, source_target_pairs={{0,12},{1,13},{2,14},{3,15},{4,0},{5,1},{6,2},{7,3},{8,4},{9,5},{1... | collective-permute-start | bytes 442376 | tf_op jit(solution)/shard_map/ppermute | solution.py:757
  48.9 3.9 %collective-permute-done.22.refs_2_ = bf16[16,4608]{1,0:T(8,128)(2,1)S(1)} collective-permute-done((bf16[16,4608]{1,0:T(8,128)(2,1)S(1)}, bf16[16,4608]{1,0:T(8,128)(2,1)S(1)}, u32[]{:S(2)}, u32[]{:S(2)}) %collective-permute-start.22) | collective-permute-done | bytes 147488 | tf_op jit(solution)/shard_map/ppermute | solution.py:757
  55.1 5.7 %collective-permute-done.24.refs_4_ = bf16[16,4608]{1,0:T(8,128)(2,1)S(1)} collective-permute-done((bf16[16,4608]{1,0:T(8,128)(2,1)S(1)}, bf16[16,4608]{1,0:T(8,128)(2,1)S(1)}, u32[]{:S(2)}, u32[]{:S(2)}) %collective-permute-start.24) | collective-permute-done | bytes 147488 | tf_op jit(solution)/shard_map/ppermute | solution.py:757
  63.2 3.2 %collective-permute-done.25.refs_5_ = bf16[16,4608]{1,0:T(8,128)(2,1)S(1)} collective-permute-done((bf16[16,4608]{1,0:T(8,128)(2,1)S(1)}, bf16[16,4608]{1,0:T(8,128)(2,1)S(1)}, u32[]{:S(2)}, u32[]{:S(2)}) %collective-permute-start.25) | collective-permute-done | bytes 147488 | tf_op jit(solution)/shard_map/ppermute | solution.py:757
  78.2 3.0 %collective-permute-done.35.got_ref = bf16[16,4608]{1,0:T(8,128)(2,1)S(1)} collective-permute-done((bf16[16,4608]{1,0:T(8,128)(2,1)S(1)}, bf16[16,4608]{1,0:T(8,128)(2,1)S(1)}, u32[]{:S(2)}, u32[]{:S(2)}) %collective-permute-start.35) | collective-permute-done | bytes 147488 | tf_op jit(solution)/shard_map/ppermute | solution.py:757
  81.3 3.0 %collective-permute-done.37.got_ref = bf16[16,4608]{1,0:T(8,128)(2,1)S(1)} collective-permute-done((bf16[16,4608]{1,0:T(8,128)(2,1)S(1)}, bf16[16,4608]{1,0:T(8,128)(2,1)S(1)}, u32[]{:S(2)}, u32[]{:S(2)}) %collective-permute-start.37) | collective-permute-done | bytes 147488 | tf_op jit(solution)/shard_map/ppermute | solution.py:757
  85.2 4.1 %collective-permute-done.34.refs_1_ = bf16[16,4608]{1,0:T(8,128)(2,1)S(1)} collective-permute-done((bf16[16,4608]{1,0:T(8,128)(2,1)S(1)}, bf16[16,4608]{1,0:T(8,128)(2,1)S(1)}, u32[]{:S(2)}, u32[]{:S(2)}) %collective-permute-start.34) | collective-permute-done | bytes 147488 | tf_op jit(solution)/shard_map/ppermute | solution.py:757
  89.4 4.0 %collective-permute-start.42 = (bf16[208,256]{1,0:T(8,128)(2,1)S(1)}, bf16[208,256]{1,0:T(8,128)(2,1)S(1)}, u32[]{:S(2)}, u32[]{:S(2)}) collective-permute-start(bf16[208,256]{1,0:T(8,128)(2,1)S(1)} %get-tuple-element.127), channel_id=1, source_target_pairs={{0,16},{1,17},{2,18},{3,19},{4,20},{5,21},{6,22},{7,23},{8,24},{9,... | collective-permute-start | bytes 319496 | tf_op jit(solution)/shard_map/ppermute | solution.py:757
  100.8 3.6 %shard_map.181 = (f32[8,448,128]{2,1,0:T(8,128)S(1)}, bf16[8,448,128]{2,1,0:T(8,128)(2,1)S(1)}) custom-call(bf16[1152,1920]{1,0:T(8,128)(2,1)S(1)} %get-tuple-element.88.xt_ref, bf16[1664,256]{1,0:T(8,128)(2,1)S(1)} %get-tuple-element.143.d_ref, f32[1,256]{1,0:T(1,128)S(1)} %get-tuple-element.131.bias_ref, f32[8,256]{1,0:T(8,128)S(1)} %shard_map.180.st_ref), custom_call_target="tpu_custom_call" | custom-call | flops 4070000128 | bytes 1 | tf_op jit(solution)/shard_map/pallas_call | solution.py:79
  105.0 2.1 %shard_map.182 = bf16[13,4,16,384]{3,2,1,0:T(8,128)(2,1)S(1)} custom-call(bf16[1664,256]{1,0:T(8,128)(2,1)S(1)} %get-tuple-element.143.d_ref, bf16[2304,384]{1,0:T(8,128)(2,1)S(1)} %get-tuple-element.105.w_ref), custom_call_target="tpu_custom_call" | custom-call | flops 2420000000 | bytes 1 | tf_op jit(solution)/shard_map/pallas_call | solution.py:79
  113.6 2.5 %collective-permute-done.51.came_ref = bf16[480,128]{1,0:T(8,128)(2,1)S(1)} collective-permute-done((bf16[480,128]{1,0:T(8,128)(2,1)S(1)}, bf16[480,128]{1,0:T(8,128)(2,1)S(1)}, u32[]{:S(2)}, u32[]{:S(2)}) %collective-permute-start.51) | collective-permute-done | bytes 122912 | tf_op jit(solution)/shard_map/ppermute | solution.py:757
  116.7 2.1 %collective-permute-done.49.came_ref = bf16[480,128]{1,0:T(8,128)(2,1)S(1)} collective-permute-done((bf16[480,128]{1,0:T(8,128)(2,1)S(1)}, bf16[480,128]{1,0:T(8,128)(2,1)S(1)}, u32[]{:S(2)}, u32[]{:S(2)}) %collective-permute-start.49) | collective-permute-done | bytes 122912 | tf_op jit(solution)/shard_map/ppermute | solution.py:757
  119.6 4.8 %shard_map.186 = f32[2,4608,256]{2,1,0:T(8,128)} custom-call(bf16[128,4608]{1,0:T(8,128)(2,1)S(1)} %get-tuple-element.136.x_ref.own_ref, bf16[128,4608]{1,0:T(8,128)(2,1)S(1)} %collective-permute-done.44.oc_ref, bf16[128,4608]{1,0:T(8,128)(2,1)S(1)} %collective-permute-done.31.x_ref, bf16[128,4608]{1,0:T(8,128)(2,1)S(1)} %collective-permute-done.45.xc_ref, ...), custom_call_target="tpu_custom_call" | custom-call | flops 5280000000 | bytes 1 | tf_op jit(solution)/shard_map/pallas_call | solution.py:1002
  124.4 2.2 %shard_map.187.own_ref = bf16[13,4,16,384]{3,2,1,0:T(8,128)(2,1)S(1)} custom-call(bf16[1664,256]{1,0:T(8,128)(2,1)S(1)} %get-tuple-element.143.d_ref, bf16[2304,384]{1,0:T(8,128)(2,1)S(1)} %get-tuple-element.105.w_ref), custom_call_target="tpu_custom_call" | custom-call | flops 2420000000 | bytes 1 | tf_op jit(solution)/shard_map/pallas_call | solution.py:79
  133.3 2.0 %collective-permute-done.55.x_ref = bf16[240,128]{1,0:T(8,128)(2,1)S(1)} collective-permute-done((bf16[240,128]{1,0:T(8,128)(2,1)S(1)}, bf16[240,128]{1,0:T(8,128)(2,1)S(1)}, u32[]{:S(2)}, u32[]{:S(2)}) %collective-permute-start.55) | collective-permute-done | bytes 61472 | tf_op jit(solution)/shard_map/ppermute | solution.py:757
  (152 shorter events, 61.3 us)
Async XLA Ops:
  4.6 18.4 %collective-permute-start.1 = (bf16[13,4,16,384]{3,2,1,0:T(8,128)(2,1)S(1)}, bf16[13,4,16,384]{3,2,1,0:T(8,128)(2,1)S(1)}, u32[]{:S(2)}, u32[]{:S(2)}) collective-permute-start(bf16[13,4,16,384]{3,2,1,0:T(8,128)(2,1)S(1)} %get-tuple-element.87), channel_id=1, source_target_pairs={{0,16},{1,17},{2,18},{3,19},{4,20},{5,21},{6,22},{7,23},{8,24},{9,... | collective-permute-start | bytes 1916936 | tf_op jit(solution)/shard_map/ppermute | solution.py:757
  9.1 9.3 %collective-permute-start.3 = (bf16[432,128]{1,0:T(8,128)(2,1)S(1)}, bf16[432,128]{1,0:T(8,128)(2,1)S(1)}, u32[]{:S(2)}, u32[]{:S(2)}) collective-permute-start(bf16[432,128]{1,0:T(8,128)(2,1)S(1)} %shard_map.162.refs_3_), channel_id=1, source_target_pairs={{0,4},{1,5},{2,6},{3,7},{4,8},{5,9},{6,10},{7,11},{8,12},{9,13},{1... | collective-permute-start | bytes 331784 | tf_op jit(solution)/shard_map/ppermute | solution.py:757
  12.9 9.8 %collective-permute-start.5 = (bf16[432,128]{1,0:T(8,128)(2,1)S(1)}, bf16[432,128]{1,0:T(8,128)(2,1)S(1)}, u32[]{:S(2)}, u32[]{:S(2)}) collective-permute-start(bf16[432,128]{1,0:T(8,128)(2,1)S(1)} %shard_map.162.refs_3_), channel_id=1, source_target_pairs={{0,8},{1,9},{2,10},{3,11},{4,12},{5,13},{6,14},{7,15},{8,0},{9,1},... | collective-permute-start | bytes 331784 | tf_op jit(solution)/shard_map/ppermute | solution.py:757
  13.7 9.0 %collective-permute-start.9 = (bf16[432,128]{1,0:T(8,128)(2,1)S(1)}, bf16[432,128]{1,0:T(8,128)(2,1)S(1)}, u32[]{:S(2)}, u32[]{:S(2)}) collective-permute-start(bf16[432,128]{1,0:T(8,128)(2,1)S(1)} %shard_map.162.refs_3_), channel_id=1, source_target_pairs={{0,1},{1,0},{2,3},{3,2},{4,5},{5,4},{6,7},{7,6},{8,9},{9,8},{10,11... | collective-permute-start | bytes 331784 | tf_op jit(solution)/shard_map/ppermute | solution.py:757
  13.7 11.6 %all-to-all-start = ((bf16[16,8,256]{2,1,0:T(8,128)(2,1)}), bf16[16,8,256]{2,1,0:T(8,128)(2,1)S(1)}, u32[]{:S(2)}, u32[]{:S(2)}) async-start(bf16[16,8,256]{2,1,0:T(8,128)(2,1)} %get-tuple-element.95), calls=%async_computation | async-start | bytes 131072 | tf_op jit(solution)/shard_map/all_to_all | solution.py:819
  37.7 25.5 %collective-permute-start.28 = (bf16[4608,256]{1,0:T(8,128)(2,1)S(1)}, bf16[4608,256]{1,0:T(8,128)(2,1)S(1)}, u32[]{:S(2)}, u32[]{:S(2)}) collective-permute-start(bf16[4608,256]{1,0:T(8,128)(2,1)S(1)} %get-tuple-element.101), channel_id=1, source_target_pairs={{0,1},{1,0},{2,3},{3,2},{4,5},{5,4},{6,7},{7,6},{8,9},{9,8},{10,11... | collective-permute-start | bytes 7077896 | tf_op jit(solution)/shard_map/ppermute | solution.py:757
  44.2 8.6 %collective-permute-start.22 = (bf16[16,4608]{1,0:T(8,128)(2,1)S(1)}, bf16[16,4608]{1,0:T(8,128)(2,1)S(1)}, u32[]{:S(2)}, u32[]{:S(2)}) collective-permute-start(bf16[16,4608]{1,0:T(8,128)(2,1)S(1)} %shard_map.166.refs_0_), channel_id=1, source_target_pairs={{0,4},{1,5},{2,6},{3,7},{4,8},{5,9},{6,10},{7,11},{8,12},{9,13},{1... | collective-permute-start | bytes 442376 | tf_op jit(solution)/shard_map/ppermute | solution.py:757
  48.7 12.1 %collective-permute-start.24 = (bf16[16,4608]{1,0:T(8,128)(2,1)S(1)}, bf16[16,4608]{1,0:T(8,128)(2,1)S(1)}, u32[]{:S(2)}, u32[]{:S(2)}) collective-permute-start(bf16[16,4608]{1,0:T(8,128)(2,1)S(1)} %shard_map.166.refs_0_), channel_id=1, source_target_pairs={{0,8},{1,9},{2,10},{3,11},{4,12},{5,13},{6,14},{7,15},{8,0},{9,1},... | collective-permute-start | bytes 442376 | tf_op jit(solution)/shard_map/ppermute | solution.py:757
  52.8 13.6 %collective-permute-start.23 = (bf16[16,4608]{1,0:T(8,128)(2,1)S(1)}, bf16[16,4608]{1,0:T(8,128)(2,1)S(1)}, u32[]{:S(2)}, u32[]{:S(2)}) collective-permute-start(bf16[16,4608]{1,0:T(8,128)(2,1)S(1)} %collective-permute-done.22.refs_2_), channel_id=1, source_target_pairs={{0,2},{1,3},{2,0},{3,1},{4,6},{5,7},{6,4},{7,5},{8,10},{9,11},{10,... | collective-permute-start | bytes 442376 | tf_op jit(solution)/shard_map/ppermute | solution.py:757
  54.0 9.2 %collective-permute-start.27 = (bf16[16,4608]{1,0:T(8,128)(2,1)S(1)}, bf16[16,4608]{1,0:T(8,128)(2,1)S(1)}, u32[]{:S(2)}, u32[]{:S(2)}) collective-permute-start(bf16[16,4608]{1,0:T(8,128)(2,1)S(1)} %collective-permute-done.26.refs_6_), channel_id=1, source_target_pairs={{0,2},{1,3},{2,0},{3,1},{4,6},{5,7},{6,4},{7,5},{8,10},{9,11},{10,... | collective-permute-start | bytes 442376 | tf_op jit(solution)/shard_map/ppermute | solution.py:757
  71.5 21.8 %collective-permute-start.31 = (bf16[128,4608]{1,0:T(8,128)(2,1)S(1)}, bf16[128,4608]{1,0:T(8,128)(2,1)S(1)}, u32[]{:S(2)}, u32[]{:S(2)}) collective-permute-start(bf16[128,4608]{1,0:T(8,128)(2,1)S(1)} %get-tuple-element.136.x_ref.own_ref), channel_id=1, source_target_pairs={{1,17},{3,19},{5,21},{7,23},{9,25},{11,27},{13,29},{15,31},{16,0},... | collective-permute-start | bytes 3538952 | tf_op jit(solution)/shard_map/ppermute | solution.py:908
  73.2 8.0 %collective-permute-start.35 = (bf16[16,4608]{1,0:T(8,128)(2,1)S(1)}, bf16[16,4608]{1,0:T(8,128)(2,1)S(1)}, u32[]{:S(2)}, u32[]{:S(2)}) collective-permute-start(bf16[16,4608]{1,0:T(8,128)(2,1)S(1)} %get-tuple-element.118), channel_id=1, source_target_pairs={{0,2},{1,3},{2,0},{3,1},{4,6},{5,7},{6,4},{7,5},{8,10},{9,11},{10,... | collective-permute-start | bytes 442376 | tf_op jit(solution)/shard_map/ppermute | solution.py:757
  74.9 9.5 %collective-permute-start.37 = (bf16[16,4608]{1,0:T(8,128)(2,1)S(1)}, bf16[16,4608]{1,0:T(8,128)(2,1)S(1)}, u32[]{:S(2)}, u32[]{:S(2)}) collective-permute-start(bf16[16,4608]{1,0:T(8,128)(2,1)S(1)} %get-tuple-element.120), channel_id=1, source_target_pairs={{0,2},{1,3},{2,0},{3,1},{4,6},{5,7},{6,4},{7,5},{8,10},{9,11},{10,... | collective-permute-start | bytes 442376 | tf_op jit(solution)/shard_map/ppermute | solution.py:757
  75.3 18.1 %collective-permute-start.32 = (bf16[16,4608]{1,0:T(8,128)(2,1)S(1)}, bf16[16,4608]{1,0:T(8,128)(2,1)S(1)}, u32[]{:S(2)}, u32[]{:S(2)}) collective-permute-start(bf16[16,4608]{1,0:T(8,128)(2,1)S(1)} %get-tuple-element.112), channel_id=1, source_target_pairs={{0,2},{1,3},{2,0},{3,1},{4,6},{5,7},{6,4},{7,5},{8,10},{9,11},{10,... | collective-permute-start | bytes 442376 | tf_op jit(solution)/shard_map/ppermute | solution.py:757
  78.1 11.3 %collective-permute-start.34 = (bf16[16,4608]{1,0:T(8,128)(2,1)S(1)}, bf16[16,4608]{1,0:T(8,128)(2,1)S(1)}, u32[]{:S(2)}, u32[]{:S(2)}) collective-permute-start(bf16[16,4608]{1,0:T(8,128)(2,1)S(1)} %shard_map.174), channel_id=1, source_target_pairs={{0,8},{1,9},{2,10},{3,11},{4,12},{5,13},{6,14},{7,15},{8,0},{9,1},... | collective-permute-start | bytes 442376 | tf_op jit(solution)/shard_map/ppermute | solution.py:757
  81.3 12.1 %collective-permute-start.36 = (bf16[16,4608]{1,0:T(8,128)(2,1)S(1)}, bf16[16,4608]{1,0:T(8,128)(2,1)S(1)}, u32[]{:S(2)}, u32[]{:S(2)}) collective-permute-start(bf16[16,4608]{1,0:T(8,128)(2,1)S(1)} %shard_map.175), channel_id=1, source_target_pairs={{0,4},{1,5},{2,6},{3,7},{4,8},{5,9},{6,10},{7,11},{8,12},{9,13},{1... | collective-permute-start | bytes 442376 | tf_op jit(solution)/shard_map/ppermute | solution.py:757
  84.4 9.4 %collective-permute-start.38 = (bf16[16,4608]{1,0:T(8,128)(2,1)S(1)}, bf16[16,4608]{1,0:T(8,128)(2,1)S(1)}, u32[]{:S(2)}, u32[]{:S(2)}) collective-permute-start(bf16[16,4608]{1,0:T(8,128)(2,1)S(1)} %shard_map.176), channel_id=1, source_target_pairs={{0,12},{1,13},{2,14},{3,15},{4,0},{5,1},{6,2},{7,3},{8,4},{9,5},{1... | collective-permute-start | bytes 442376 | tf_op jit(solution)/shard_map/ppermute | solution.py:757
  95.9 11.3 %collective-permute-start.44 = (bf16[128,4608]{1,0:T(8,128)(2,1)S(1)}, bf16[128,4608]{1,0:T(8,128)(2,1)S(1)}, u32[]{:S(2)}, u32[]{:S(2)}) collective-permute-start(bf16[128,4608]{1,0:T(8,128)(2,1)S(1)} %get-tuple-element.136.x_ref.own_ref), channel_id=1, source_target_pairs={{0,1},{1,0},{2,3},{3,2},{4,5},{5,4},{6,7},{7,6},{8,9},{9,8},{10,11... | collective-permute-start | bytes 3538952 | tf_op jit(solution)/shard_map/ppermute | solution.py:757
  109.3 9.4 %collective-permute-start.49 = (bf16[480,128]{1,0:T(8,128)(2,1)S(1)}, bf16[480,128]{1,0:T(8,128)(2,1)S(1)}, u32[]{:S(2)}, u32[]{:S(2)}) collective-permute-start(bf16[480,128]{1,0:T(8,128)(2,1)S(1)} %get-tuple-element.145), channel_id=1, source_target_pairs={{0,2},{1,3},{2,0},{3,1},{4,6},{5,7},{6,4},{7,5},{8,10},{9,11},{10,... | collective-permute-start | bytes 368648 | tf_op jit(solution)/shard_map/ppermute | solution.py:757
  111.1 15.7 %collective-permute-start.48 = (bf16[13,4,16,384]{3,2,1,0:T(8,128)(2,1)S(1)}, bf16[13,4,16,384]{3,2,1,0:T(8,128)(2,1)S(1)}, u32[]{:S(2)}, u32[]{:S(2)}) collective-permute-start(bf16[13,4,16,384]{3,2,1,0:T(8,128)(2,1)S(1)} %shard_map.182), channel_id=1, source_target_pairs={{0,16},{1,17},{2,18},{3,19},{4,20},{5,21},{6,22},{7,23},{8,24},{9,... | collective-permute-start | bytes 1916936 | tf_op jit(solution)/shard_map/ppermute | solution.py:757
  111.9 14.6 %collective-permute-start.46 = (bf16[480,128]{1,0:T(8,128)(2,1)S(1)}, bf16[480,128]{1,0:T(8,128)(2,1)S(1)}, u32[]{:S(2)}, u32[]{:S(2)}) collective-permute-start(bf16[480,128]{1,0:T(8,128)(2,1)S(1)} %get-tuple-element.139), channel_id=1, source_target_pairs={{0,2},{1,3},{2,0},{3,1},{4,6},{5,7},{6,4},{7,5},{8,10},{9,11},{10,... | collective-permute-start | bytes 368648 | tf_op jit(solution)/shard_map/ppermute | solution.py:757
  113.5 14.1 %collective-permute-start.53 = (bf16[512,128]{1,0:T(8,128)(2,1)S(1)}, bf16[512,128]{1,0:T(8,128)(2,1)S(1)}, u32[]{:S(2)}, u32[]{:S(2)}) collective-permute-start(bf16[512,128]{1,0:T(8,128)(2,1)S(1)} %shard_map.185), channel_id=1, source_target_pairs={{0,12},{1,13},{2,14},{3,15},{4,0},{5,1},{6,2},{7,3},{8,4},{9,5},{1... | collective-permute-start | bytes 393224 | tf_op jit(solution)/shard_map/ppermute | solution.py:757
  116.1 11.5 %collective-permute-start.52 = (bf16[512,128]{1,0:T(8,128)(2,1)S(1)}, bf16[512,128]{1,0:T(8,128)(2,1)S(1)}, u32[]{:S(2)}, u32[]{:S(2)}) collective-permute-start(bf16[512,128]{1,0:T(8,128)(2,1)S(1)} %shard_map.190), channel_id=1, source_target_pairs={{0,8},{1,9},{2,10},{3,11},{4,12},{5,13},{6,14},{7,15},{8,0},{9,1},... | collective-permute-start | bytes 393224 | tf_op jit(solution)/shard_map/ppermute | solution.py:757
  118.8 8.8 %collective-permute-start.50 = (bf16[512,128]{1,0:T(8,128)(2,1)S(1)}, bf16[512,128]{1,0:T(8,128)(2,1)S(1)}, u32[]{:S(2)}, u32[]{:S(2)}) collective-permute-start(bf16[512,128]{1,0:T(8,128)(2,1)S(1)} %shard_map.189), channel_id=1, source_target_pairs={{0,4},{1,5},{2,6},{3,7},{4,8},{5,9},{6,10},{7,11},{8,12},{9,13},{1... | collective-permute-start | bytes 393224 | tf_op jit(solution)/shard_map/ppermute | solution.py:757
  (46 other events, 221.7 us)
